TPU v7x, 32 devices: a whole 2x2x4 slice. The times are simulated.
32 devices in a mesh: groups: 2 (over x), pb: 16 (over z, y, core).
Axes of the slice: x: 2, y: 2, z: 4, core: 2. Of those that a mesh axis runs over, the one named last changes fastest.
Arguments:
- hidden: bfloat16 [8192, 4096], P(('groups', 'pb')), parts along dimension 0, may hold values from -6 to 6
- final_gain: bfloat16 [4096], replicated, may hold values from 0.099609375 to 1.8984375
- last_row: int32 [32, 256], P(('groups', 'pb')), parts along dimension 0, may hold values from 0 to 255, each once within a row
- pair_owner: int32 [4096, 2], P(('groups', 'pb')), parts along dimension 0, may hold values from 0 to 4095, as said below
- hard_negatives: int32 [32, 4], P(('groups', 'pb')), parts along dimension 0, may hold values from -1 to 15, as said below
Outputs:
- pooled_grad: float32 [8192, 4096], P(('groups', 'pb')), parts along dimension 0
- block_loss: float32 [32], P(('groups', 'pb')), parts along dimension 0
There are 2 independent parts, one for each index of `groups`. A program takes and returns all parts, laid end to end along the dimension named above; an argument that names none is the same for every part. Nothing has to cross between parts.
Inputs may be any that keep to these rules, and one draw needn't show every extreme that they name: `last_row`: each device's row names each of its 256 rows once. `pair_owner`: every global sequence index is named exactly once. The 128 pairs of one query block name at most 32 sequences of any one device, and exactly 32 of some device. `hard_negatives`: entry r of query block j is -1 or block (j + r + 1) mod 16. Every row names at least one block, and some row names all 4.
All inputs are finite; a program needn't handle non-finite values.
Results may differ from a plain program's by a relative error of at most 0.006.
Values may be sent and summed in bfloat16 or wider, within the bound.
No kernel may reach another device: no remote copies, remote signals or barrier semaphores. Data moves between devices by JAX's collectives and lax.ppermute only.
A program may use at most 128 MiB of HBM per device.

v0:
```python
import jax
import jax.numpy as jnp
from jax import lax
from jax.sharding import PartitionSpec as P

inverse_temp = 50.0
token_eps = 1e-05


def from_behind(value, axis, steps):
    count = lax.axis_size(axis)
    pairs = [(source, (source + steps) % count) for source in range(count)]
    return lax.ppermute(value, axis, pairs)


def similarity(queries, documents):
    return inverse_temp * lax.dot_general(
        queries, documents, (((1,), (1,)), ((), ())), preferred_element_type=jnp.float32
    )


def transposed(weights, queries):
    return lax.dot_general(
        weights, queries, (((0,), (0,)), ((), ())), preferred_element_type=jnp.float32
    )


def combine_docs(weights, documents):
    return jnp.dot(weights, documents, preferred_element_type=jnp.float32)


def skipped(listed, function, operands, out_shape):
    return lax.cond(
        listed,
        lambda inputs: function(*inputs),
        lambda inputs: jnp.zeros(out_shape, jnp.float32),
        operands,
    )


def local(hidden, final_gain, last_row, pair_owner, hard_negatives):
    values = hidden.astype(jnp.float32)
    scale_row = lax.rsqrt(jnp.mean(values * values, axis=-1, keepdims=True) + token_eps)
    normed = (values * scale_row * final_gain.astype(jnp.float32)).astype(jnp.bfloat16)
    seq_count = last_row.shape[1]
    model_width = hidden.shape[1]
    pooled = normed[last_row[0]].astype(jnp.float32)
    inverse_norm = lax.rsqrt(jnp.sum(pooled * pooled, axis=-1, keepdims=True) + 1e-06)
    unit_vec = pooled * inverse_norm
    embedding = unit_vec.astype(jnp.bfloat16)
    devices = lax.axis_size("pb")
    capacity = 2 * seq_count // devices
    pair_count = pair_owner.shape[0]
    wanted = jnp.concatenate([pair_owner[:, 0], pair_owner[:, 1]])
    holder = wanted // seq_count
    within = wanted % seq_count
    entry_ids = jnp.arange(2 * pair_count, dtype=jnp.int32)
    earlier = (holder[None, :] == holder[:, None]) & (entry_ids[None, :] < entry_ids[:, None])
    position = jnp.sum(earlier.astype(jnp.int32), axis=1)
    request = jnp.full((devices, capacity), -1, jnp.int32).at[holder, position].set(within)
    served = lax.all_to_all(request, "pb", split_axis=0, concat_axis=0, tiled=True)
    outgoing = jnp.where(
        served[:, :, None] >= 0, embedding[jnp.maximum(served, 0)], jnp.zeros((), jnp.bfloat16)
    )
    received = lax.all_to_all(outgoing, "pb", split_axis=0, concat_axis=0, tiled=True)
    gathered = received[holder, position]
    queries = gathered[:pair_count]
    own_docs = gathered[pair_count:]
    listed_ids = hard_negatives[0]
    window = hard_negatives.shape[1]
    listed = [listed_ids[offset] >= 0 for offset in range(window)]
    neighbours = []
    moving = own_docs
    for offset in range(window):
        moving = from_behind(moving, "pb", -1)
        neighbours.append(moving)
    tile_shape = (pair_count, pair_count)
    score_blocks = [similarity(queries, own_docs)]
    for offset in range(window):
        score_blocks.append(
            skipped(listed[offset], similarity, (queries, neighbours[offset]), tile_shape)
        )
    all_scores = jnp.concatenate(score_blocks, axis=1)
    usable = jnp.concatenate(
        [jnp.ones((pair_count,), jnp.bool_)]
        + [jnp.broadcast_to(listed[offset], (pair_count,)) for offset in range(window)]
    )
    masked = jnp.where(usable[None, :], all_scores, -jnp.inf)
    row_max = jnp.max(masked, axis=1, keepdims=True)
    log_total = row_max + jnp.log(jnp.sum(jnp.exp(masked - row_max), axis=1, keepdims=True))
    diagonal = jnp.arange(pair_count, dtype=jnp.int32)
    positive = all_scores[diagonal, diagonal]
    block_loss = jnp.mean(log_total[:, 0] - positive).reshape(1)
    columns = jnp.arange((window + 1) * pair_count, dtype=jnp.int32)
    target = (columns[None, :] == diagonal[:, None]).astype(jnp.float32)
    coefficients = (inverse_temp * (jnp.exp(masked - log_total) - target)).astype(jnp.bfloat16)
    pieces = [
        coefficients[:, offset * pair_count : (offset + 1) * pair_count]
        for offset in range(window + 1)
    ]
    grad_shape = (pair_count, model_width)
    query_sum = combine_docs(pieces[0], own_docs)
    for offset in range(window):
        query_sum = query_sum + skipped(
            listed[offset], combine_docs, (pieces[offset + 1], neighbours[offset]), grad_shape
        )
    query_grad = query_sum.astype(jnp.bfloat16)
    own_part = transposed(pieces[0], queries).astype(jnp.bfloat16)
    partial_value = [
        skipped(listed[offset], transposed, (pieces[offset + 1], queries), grad_shape).astype(
            jnp.bfloat16
        )
        for offset in range(window)
    ]
    running = partial_value[window - 1].astype(jnp.float32)
    for offset in range(window):
        running = from_behind(running, "pb", 1)
        if offset + 1 < window:
            running = running + partial_value[window - 2 - offset].astype(jnp.float32)
    doc_grad = (own_part.astype(jnp.float32) + running).astype(jnp.bfloat16)
    answers = jnp.concatenate([query_grad, doc_grad], axis=0)
    returning = (
        jnp.zeros((devices, capacity, model_width), jnp.bfloat16).at[holder, position].set(answers)
    )
    returned = lax.all_to_all(returning, "pb", split_axis=0, concat_axis=0, tiled=True)
    slot_ids = jnp.where(served >= 0, served, seq_count).reshape(-1)
    emb_grad = (
        jnp.zeros((seq_count, model_width), jnp.bfloat16)
        .at[slot_ids]
        .set(returned.reshape(-1, model_width), mode="drop")
    )
    gradient = emb_grad.astype(jnp.float32)
    pooled_grad = gradient - unit_vec * jnp.sum(unit_vec * gradient, axis=-1, keepdims=True)
    return (pooled_grad, block_loss)


def solution(mesh):
    return jax.shard_map(
        local,
        mesh=mesh,
        in_specs=(
            P(("groups", "pb"), None),
            P(),
            P(("groups", "pb"), None),
            P(("groups", "pb"), None),
            P(("groups", "pb"), None),
        ),
        out_specs=(P(("groups", "pb"), None), P(("groups", "pb"))),
        check_vma=False,
    )
```

profile of v0, /device:TPU:15, one launch (start us, length us, event | category | flops | bytes accessed | tf_op | source)
XLA Modules:
  0.0 558.4 jit_solution(4259982440103671858)
XLA Ops:
  2.3 35.5 %scatter_fusion = s32[16,32]{1,0:T(8,128)} fusion(s32[16,32]{1,0:T(8,128)} %broadcast_in_dim.42, s32[256]{0:T(256)S(1)} %bitcast.53, s32[256]{0:T(256)S(1)} %get-tuple-element.204), kind=kCustom, calls=%fused_computation.4 | custom fusion | bytes 5120 | tf_op jit(solution)/shard_map/scatter | solution.py:60
  37.8 6.7 %all-to-all-start = ((s32[16,1,32]{2,1,0:T(1,128)}), s32[16,1,32]{2,1,0:T(1,128)S(1)}, u32[]{:S(2)}, u32[]{:S(2)}) async-start(s32[16,1,32]{2,1,0:T(1,128)} %bitcast.5), calls=%async_computation | async-start | bytes 16384 | tf_op jit(solution)/shard_map/all_to_all | solution.py:61
  48.3 3.2 gather_fusion
  54.4 4.4 gather_fusion.1
  58.8 2.5 broadcast_select_fusion
  61.3 98.2 %all_to_all.22 = bf16[16,32,4096]{2,1,0:T(8,128)(2,1)} all-to-all(bf16[16,32,4096]{2,1,0:T(8,128)(2,1)S(1)} %broadcast_select_fusion), channel_id=1, replica_groups=mesh['groups'=2,'pb'=16] {'pb'}, dimensions={0} | all-to-all | bytes 8388608 | tf_op jit(solution)/shard_map/all_to_all | solution.py:65
  159.5 6.0 %gather_fusion.2 = bf16[256,4096]{1,0:T(8,128)(2,1)S(1)} fusion(bf16[16,32,4096]{2,1,0:T(8,128)(2,1)} %all_to_all.22, s32[256]{0:T(256)S(1)} %bitcast.55), kind=kCustom, calls=%fused_computation.2 | custom fusion | bytes 4196352 | tf_op jit(solution)/shard_map/gather | solution.py:66
  165.9 14.9 %collective-permute-done = bf16[128,4096]{1,0:T(8,128)(2,1)S(1)} collective-permute-done((bf16[128,4096]{1,0:T(8,128)(2,1)S(1)}, bf16[128,4096]{1,0:T(8,128)(2,1)S(1)}, u32[]{:S(2)}, u32[]{:S(2)}) %collective-permute-start) | collective-permute-done | bytes 1048608 | tf_op jit(solution)/shard_map/ppermute | solution.py:13
  181.8 15.1 %collective-permute-done.1 = bf16[128,4096]{1,0:T(8,128)(2,1)S(1)} collective-permute-done((bf16[128,4096]{1,0:T(8,128)(2,1)S(1)}, bf16[128,4096]{1,0:T(8,128)(2,1)S(1)}, u32[]{:S(2)}, u32[]{:S(2)}) %collective-permute-start.1) | collective-permute-done | bytes 1048608 | tf_op jit(solution)/shard_map/ppermute | solution.py:13
  197.9 15.2 %collective-permute-done.2 = bf16[128,4096]{1,0:T(8,128)(2,1)} collective-permute-done((bf16[128,4096]{1,0:T(8,128)(2,1)S(1)}, bf16[128,4096]{1,0:T(8,128)(2,1)}, u32[]{:S(2)}, u32[]{:S(2)}) %collective-permute-start.2) | collective-permute-done | bytes 1048608 | tf_op jit(solution)/shard_map/ppermute | solution.py:13
  240.7 2.8 convert_element_type.153
  247.1 21.8 %collective-permute-done.4 = f32[128,4096]{1,0:T(8,128)} collective-permute-done((f32[128,4096]{1,0:T(8,128)}, f32[128,4096]{1,0:T(8,128)}, u32[]{:S(2)}, u32[]{:S(2)}) %collective-permute-start.4) | collective-permute-done | bytes 2097184 | tf_op jit(solution)/shard_map/ppermute | solution.py:13
  268.9 3.4 convert_add_fusion.2
  272.2 3.4 collective-permute-start.5
  276.8 22.1 %collective-permute-done.5 = f32[128,4096]{1,0:T(8,128)} collective-permute-done((f32[128,4096]{1,0:T(8,128)}, f32[128,4096]{1,0:T(8,128)}, u32[]{:S(2)}, u32[]{:S(2)}) %collective-permute-start.5) | collective-permute-done | bytes 2097184 | tf_op jit(solution)/shard_map/ppermute | solution.py:13
  298.9 3.4 convert_add_fusion.1
  302.3 3.4 collective-permute-start.6
  307.2 21.8 %collective-permute-done.6 = f32[128,4096]{1,0:T(8,128)} collective-permute-done((f32[128,4096]{1,0:T(8,128)}, f32[128,4096]{1,0:T(8,128)}, u32[]{:S(2)}, u32[]{:S(2)}) %collective-permute-start.6) | collective-permute-done | bytes 2097184 | tf_op jit(solution)/shard_map/ppermute | solution.py:13
  329.0 3.4 convert_add_fusion
  332.4 3.4 collective-permute-start.7
  335.8 3.1 conditional.18
  335.8 3.1 fusion.30
  342.2 3.0 conditional.19
  342.2 3.0 fusion.31
  350.7 8.4 %collective-permute-done.7 = f32[128,4096]{1,0:T(8,128)} collective-permute-done((f32[128,4096]{1,0:T(8,128)}, f32[128,4096]{1,0:T(8,128)}, u32[]{:S(2)}, u32[]{:S(2)}) %collective-permute-start.7) | collective-permute-done | bytes 2097184 | tf_op jit(solution)/shard_map/ppermute | solution.py:13
  361.1 2.5 broadcast_in_dim.44
  363.6 65.1 %scatter_fusion.1 = bf16[16,32,4096]{2,1,0:T(8,128)(2,1)} fusion(bf16[16,32,4096]{2,1,0:T(8,128)(2,1)} %broadcast_in_dim.44, s32[256]{0:T(256)S(1)} %bitcast.54, bf16[256,4096]{1,0:T(8,128)(2,1)S(1)} %pad_maximum_fusion), kind=kCustom, calls=%fused_computation.5 | custom fusion | bytes 6293504 | tf_op jit(solution)/shard_map/scatter | solution.py:123
  428.6 21.3 %all-to-all-start.2 = ((bf16[16,32,4096]{2,1,0:T(8,128)(2,1)}), bf16[16,32,4096]{2,1,0:T(8,128)(2,1)}, u32[]{:S(2)}, u32[]{:S(2)}) async-start(bf16[16,32,4096]{2,1,0:T(8,128)(2,1)} %scatter_fusion.1), calls=%async_computation.2 | async-start | bytes 8388608 | tf_op jit(solution)/shard_map/all_to_all | solution.py:125
  452.0 90.4 %all-to-all-done.2 = bf16[16,32,4096]{2,1,0:T(8,128)(2,1)} async-done(((bf16[16,32,4096]{2,1,0:T(8,128)(2,1)}), bf16[16,32,4096]{2,1,0:T(8,128)(2,1)}, u32[]{:S(2)}, u32[]{:S(2)}) %all-to-all-start.2) | async-done | bytes 4194336 | tf_op jit(solution)/shard_map/all_to_all | solution.py:125
  542.5 9.1 %scatter_custom_fusion.2 = bf16[256,4096]{1,0:T(8,128)(2,1)} fusion(s32[512]{0:T(512)S(1)} %bitcast.61, bf16[512,4096]{1,0:T(8,128)(2,1)} %bitcast.18, bf16[]{:T(256)} %constant.53.clone.1), kind=kCustom, calls=%fused_computation.36 | custom fusion | bytes 2097664 | tf_op jit(solution)/shard_map/scatter | solution.py:130
  551.6 2.6 fusion.7
  554.2 3.1 convert_subtract_fusion
  (117 shorter events, 69.7 us)
Async XLA Ops:
  0.6 43.9 %copy-start.15 = (bf16[4096]{0:T(1024)(128)(2,1)S(1)}, bf16[4096]{0:T(1024)(128)(2,1)}, u32[]{:S(2)}) copy-start(bf16[4096]{0:T(1024)(128)(2,1)} %param.30) | copy-start | bytes 24580
  0.6 43.9 %copy-start.3 = (bf16[256,4096]{1,0:T(8,128)(2,1)S(1)}, bf16[256,4096]{1,0:T(8,128)(2,1)}, u32[]{:S(2)}) copy-start(bf16[256,4096]{1,0:T(8,128)(2,1)} %param.29) | copy-start | bytes 6291460
  37.8 10.4 %all-to-all-start = ((s32[16,1,32]{2,1,0:T(1,128)}), s32[16,1,32]{2,1,0:T(1,128)S(1)}, u32[]{:S(2)}, u32[]{:S(2)}) async-start(s32[16,1,32]{2,1,0:T(1,128)} %bitcast.5), calls=%async_computation | async-start | bytes 16384 | tf_op jit(solution)/shard_map/all_to_all | solution.py:61
  44.5 1.6 copy-start.4
  46.1 0.7 copy-start.17
  51.6 2.2 copy-start
  53.8 0.6 copy-start.13
  165.5 47.7 %copy-start.16 = (s32[1,4]{1,0:T(1,128)S(1)}, s32[1,4]{1,0:T(1,128)}, u32[]{:S(2)}) copy-start(s32[1,4]{1,0:T(1,128)} %param.33) | copy-start | bytes 52
  165.7 15.2 %collective-permute-start = (bf16[128,4096]{1,0:T(8,128)(2,1)S(1)}, bf16[128,4096]{1,0:T(8,128)(2,1)S(1)}, u32[]{:S(2)}, u32[]{:S(2)}) collective-permute-start(bf16[128,4096]{1,0:T(8,128)(2,1)S(1)} %get-tuple-element.198), channel_id=1, source_target_pairs={{0,15},{1,0},{2,1},{3,2},{4,3},{5,4},{6,5},{7,6},{8,7},{9,8},{10,9... | collective-permute-start | bytes 3145736 | tf_op jit(solution)/shard_map/ppermute | solution.py:13
  180.8 1.0 copy-start.8
  181.8 15.1 %collective-permute-start.1 = (bf16[128,4096]{1,0:T(8,128)(2,1)S(1)}, bf16[128,4096]{1,0:T(8,128)(2,1)S(1)}, u32[]{:S(2)}, u32[]{:S(2)}) collective-permute-start(bf16[128,4096]{1,0:T(8,128)(2,1)S(1)} %collective-permute-done), channel_id=1, source_target_pairs={{0,15},{1,0},{2,1},{3,2},{4,3},{5,4},{6,5},{7,6},{8,7},{9,8},{10,9... | collective-permute-start | bytes 3145736 | tf_op jit(solution)/shard_map/ppermute | solution.py:13
  196.9 1.0 copy-start.11
  197.9 15.2 %collective-permute-start.2 = (bf16[128,4096]{1,0:T(8,128)(2,1)S(1)}, bf16[128,4096]{1,0:T(8,128)(2,1)}, u32[]{:S(2)}, u32[]{:S(2)}) collective-permute-start(bf16[128,4096]{1,0:T(8,128)(2,1)S(1)} %collective-permute-done.1), channel_id=1, source_target_pairs={{0,15},{1,0},{2,1},{3,2},{4,3},{5,4},{6,5},{7,6},{8,7},{9,8},{10,9... | collective-permute-start | bytes 3145736 | tf_op jit(solution)/shard_map/ppermute | solution.py:13
  213.1 17.7 %collective-permute-start.3 = (bf16[128,4096]{1,0:T(8,128)(2,1)}, bf16[128,4096]{1,0:T(8,128)(2,1)}, u32[]{:S(2)}, u32[]{:S(2)}) collective-permute-start(bf16[128,4096]{1,0:T(8,128)(2,1)} %collective-permute-done.2), channel_id=1, source_target_pairs={{0,15},{1,0},{2,1},{3,2},{4,3},{5,4},{6,5},{7,6},{8,7},{9,8},{10,9... | collective-permute-start | bytes 3145736 | tf_op jit(solution)/shard_map/ppermute | solution.py:13
  222.9 1.2 copy-start.9
  238.6 0.7 copy-start.12
  243.5 25.4 %collective-permute-start.4 = (f32[128,4096]{1,0:T(8,128)}, f32[128,4096]{1,0:T(8,128)}, u32[]{:S(2)}, u32[]{:S(2)}) collective-permute-start(f32[128,4096]{1,0:T(8,128)} %convert_element_type.153), channel_id=1, source_target_pairs={{0,1},{1,2},{2,3},{3,4},{4,5},{5,6},{6,7},{7,8},{8,9},{9,10},{10,1... | collective-permute-start | bytes 6291464 | tf_op jit(solution)/shard_map/ppermute | solution.py:13
  272.2 26.7 %collective-permute-start.5 = (f32[128,4096]{1,0:T(8,128)}, f32[128,4096]{1,0:T(8,128)}, u32[]{:S(2)}, u32[]{:S(2)}) collective-permute-start(f32[128,4096]{1,0:T(8,128)} %convert_add_fusion.2), channel_id=1, source_target_pairs={{0,1},{1,2},{2,3},{3,4},{4,5},{5,6},{6,7},{7,8},{8,9},{9,10},{10,1... | collective-permute-start | bytes 6291464 | tf_op jit(solution)/shard_map/ppermute | solution.py:13
  302.3 26.7 %collective-permute-start.6 = (f32[128,4096]{1,0:T(8,128)}, f32[128,4096]{1,0:T(8,128)}, u32[]{:S(2)}, u32[]{:S(2)}) collective-permute-start(f32[128,4096]{1,0:T(8,128)} %convert_add_fusion.1), channel_id=1, source_target_pairs={{0,1},{1,2},{2,3},{3,4},{4,5},{5,6},{6,7},{7,8},{8,9},{9,10},{10,1... | collective-permute-start | bytes 6291464 | tf_op jit(solution)/shard_map/ppermute | solution.py:13
  332.4 26.7 %collective-permute-start.7 = (f32[128,4096]{1,0:T(8,128)}, f32[128,4096]{1,0:T(8,128)}, u32[]{:S(2)}, u32[]{:S(2)}) collective-permute-start(f32[128,4096]{1,0:T(8,128)} %convert_add_fusion), channel_id=1, source_target_pairs={{0,1},{1,2},{2,3},{3,4},{4,5},{5,6},{6,7},{7,8},{8,9},{9,10},{10,1... | collective-permute-start | bytes 6291464 | tf_op jit(solution)/shard_map/ppermute | solution.py:13
  338.8 1.6 copy-start.10
  345.3 2.7 copy-start.6
  345.3 2.7 copy-start.7
  346.6 1.8 copy-start.5
  428.6 113.8 %all-to-all-start.2 = ((bf16[16,32,4096]{2,1,0:T(8,128)(2,1)}), bf16[16,32,4096]{2,1,0:T(8,128)(2,1)}, u32[]{:S(2)}, u32[]{:S(2)}) async-start(bf16[16,32,4096]{2,1,0:T(8,128)(2,1)} %scatter_fusion.1), calls=%async_computation.2 | async-start | bytes 8388608 | tf_op jit(solution)/shard_map/all_to_all | solution.py:125
  450.0 101.6 %copy-start.1 = (bf16[256,4096]{1,0:T(8,128)(2,1)S(1)}, bf16[256,4096]{1,0:T(8,128)(2,1)}, u32[]{:S(2)}) copy-start(bf16[256,4096]{1,0:T(8,128)(2,1)} %gather_fusion) | copy-start | bytes 6291460
  450.0 101.6 %copy-start.14 = (f32[256]{0:T(256)S(1)}, f32[256]{0:T(256)}, u32[]{:S(2)}) copy-start(f32[256]{0:T(256)} %copy-done.13) | copy-start | bytes 3076
  551.6 2.6 copy-start.2
where the time goes:
time: 562 us; the launch traced here: 558 us
  waiting for transfers between devices  211 us (38%)
  local copies, waits for them, and re-layouts  151 us (27%)
  blocking collectives  98.2 us (17%)
  starting transfers between devices  40.5 us (7%)
  other arithmetic  33.5 us (6%)
  matrix products  19.2 us (3%)
    ppermute x8, waiting for transfers between devices, from_behind(): return lax.ppermute(value, axis, pairs)  119 us
    all_to_all x1, blocking collectives, local(): lax.all_to_all(outgoing, 'pb', split_axis=0, concat_axis=0, tiled=True)  98.2 us
    all_to_all x1, waiting for transfers between devices, local(): lax.all_to_all(returning, 'pb', split_axis=0, concat_axis=0, tiled=True)  90.4 us
    scatter x1, local copies, waits for them, and re-layouts, local(): jnp.zeros((devices, capacity, model_width), jnp.bfloat16)  65.1 us
    scatter x1, local copies, waits for them, and re-layouts, local(): jnp.full((devices, capacity), -1, jnp.int32).at[holder, position]  35.5 us
    all_to_all x1, starting transfers between devices, local(): lax.all_to_all(returning, 'pb', split_axis=0, concat_axis=0, tiled=True)  21.3 us
    unnamed x43, local copies, waits for them, and re-layouts  12.8 us
    ppermute x8, starting transfers between devices, from_behind(): return lax.ppermute(value, axis, pairs)  12.5 us
  transfers between devices with their start and end apart: 10, of which 9 were waited for; matrix products, arithmetic and copies ran while one was open for 6% of the time, Pallas kernels for 0%

commit v1 on v0

--- a/solution.py
+++ b/solution.py
@@ -1,10 +1,327 @@
+import functools
+
 import jax
 import jax.numpy as jnp
 from jax import lax
+from jax.experimental import pallas as pl
+from jax.experimental.pallas import tpu as pltpu
 from jax.sharding import PartitionSpec as P
 
 inverse_temp = 50.0
 token_eps = 1e-05
+unit_eps = 1e-06
+lanes = 128
+vmem_limit = 56 * 1024 * 1024
+
+
+def norm_kernel(last_ref, hidden_ref, gain_ref, normed_ref, inv_ref, emb_ref):
+    rows, width = normed_ref.shape
+    source = hidden_ref.shape[0]
+    parts, _, piece = emb_ref.shape
+    columns = lax.broadcasted_iota(jnp.int32, (rows, source), 1)
+    pick = jnp.where(columns == last_ref[...], 1.0, 0.0).astype(jnp.bfloat16)
+    values = jnp.dot(pick, hidden_ref[...], preferred_element_type=jnp.float32)
+    scale = lax.rsqrt(jnp.mean(values * values, axis=-1, keepdims=True) + token_eps)
+    normed = (values * scale * gain_ref[...].astype(jnp.float32)).astype(jnp.bfloat16)
+    normed_ref[...] = normed
+    pooled = normed.astype(jnp.float32)
+    inverse = lax.rsqrt(jnp.sum(pooled * pooled, axis=-1, keepdims=True) + unit_eps)
+    inv_ref[...] = jnp.broadcast_to(inverse, inv_ref.shape)
+    embedding = (pooled * inverse).astype(jnp.bfloat16)
+    for part in range(parts):
+        emb_ref[part] = embedding[:, part * piece : (part + 1) * piece]
+
+
+def norm_call(last_column, hidden, gain_row, parts):
+    seqs, width = hidden.shape
+    piece = width // parts
+    rows = 32
+    return pl.pallas_call(
+        norm_kernel,
+        grid=(seqs // rows,),
+        in_specs=[
+            pl.BlockSpec((rows, 1), lambda i: (i, 0)),
+            pl.BlockSpec((seqs, width), lambda i: (0, 0)),
+            pl.BlockSpec((1, width), lambda i: (0, 0)),
+        ],
+        out_specs=[
+            pl.BlockSpec((rows, width), lambda i: (i, 0)),
+            pl.BlockSpec((rows, lanes), lambda i: (i, 0)),
+            pl.BlockSpec((parts, rows, piece), lambda i: (0, i, 0)),
+        ],
+        out_shape=[
+            jax.ShapeDtypeStruct((seqs, width), jnp.bfloat16),
+            jax.ShapeDtypeStruct((seqs, lanes), jnp.float32),
+            jax.ShapeDtypeStruct((parts, seqs, piece), jnp.bfloat16),
+        ],
+        compiler_params=pltpu.CompilerParams(vmem_limit_bytes=vmem_limit),
+        name="norm_rows",
+    )(last_column, hidden, gain_row)
+
+
+def score_kernel(blocks, pairs, window, own_ref, emb_ref, q_ref, d_ref, s_ref, wide, picked):
+    seqs = emb_ref.shape[0]
+    chunk = 256
+
+    def widen(step, carry):
+        at = pl.multiple_of(step * chunk, chunk)
+        wide[pl.ds(at, chunk), :] = emb_ref[pl.ds(at, chunk), :].astype(jnp.float32)
+        return carry
+
+    lax.fori_loop(0, seqs // chunk, widen, 0)
+
+    def pick_block(block, carry):
+        def pick_rows(step, inner):
+            base = pl.multiple_of(step * 8, 8)
+            for k in range(8):
+                picked[pl.ds(base + k, 1), :] = wide[pl.ds(own_ref[block, base + k], 1), :]
+            return inner
+
+        lax.fori_loop(0, 2 * pairs // 8, pick_rows, 0)
+        at = pl.multiple_of(block * pairs, pairs)
+        q_ref[pl.ds(at, pairs), :] = picked[:pairs, :].astype(jnp.bfloat16)
+        d_ref[pl.ds(at, pairs), :] = picked[pairs:, :].astype(jnp.bfloat16)
+        return carry
+
+    lax.fori_loop(0, blocks, pick_block, 0)
+    d_ref[blocks * pairs :, :] = d_ref[: window * pairs, :]
+    groups = s_ref.shape[0]
+    fine = pairs // groups
+
+    def score_block(block, carry):
+        at = pl.multiple_of(block * pairs, pairs)
+        queries = q_ref[pl.ds(at, pairs), :]
+        for column in range(window + 1):
+            there = pl.multiple_of(at + column * pairs, pairs)
+            documents = d_ref[pl.ds(there, pairs), :]
+            tile = inverse_temp * lax.dot_general(
+                queries, documents, (((1,), (1,)), ((), ())), preferred_element_type=jnp.float32
+            )
+            row = pl.multiple_of((column * blocks + block) * fine, fine)
+            s_ref[:, pl.ds(row, fine), :] = tile.reshape(groups, fine, pairs)
+        return carry
+
+    lax.fori_loop(0, blocks, score_block, 0)
+
+
+def score_call(own, embedded, blocks, pairs, window):
+    seqs, piece = embedded.shape
+    fine = pairs // blocks
+    tiles = blocks * (window + 1)
+    whole = pl.BlockSpec(memory_space=pltpu.VMEM)
+    return pl.pallas_call(
+        functools.partial(score_kernel, blocks, pairs, window),
+        in_specs=[pl.BlockSpec(memory_space=pltpu.SMEM), whole],
+        out_specs=[whole, whole, whole],
+        out_shape=[
+            jax.ShapeDtypeStruct((blocks * pairs, piece), jnp.bfloat16),
+            jax.ShapeDtypeStruct(((blocks + window) * pairs, piece), jnp.bfloat16),
+            jax.ShapeDtypeStruct((blocks, tiles * fine, pairs), jnp.float32),
+        ],
+        scratch_shapes=[
+            pltpu.VMEM((seqs, piece), jnp.float32),
+            pltpu.VMEM((2 * pairs, piece), jnp.float32),
+        ],
+        compiler_params=pltpu.CompilerParams(vmem_limit_bytes=vmem_limit),
+        name="partial_scores",
+    )(own, embedded)
+
+
+def softmax_kernel(blocks, window, listed_ref, s_ref, c_ref, loss_ref):
+    fine = s_ref.shape[2]
+    pairs = s_ref.shape[3]
+    first = lax.axis_index("pb") * fine
+    rows = lax.broadcasted_iota(jnp.int32, (fine, pairs), 0) + first
+    target = lax.broadcasted_iota(jnp.int32, (fine, pairs), 1) == rows
+
+    def one_block(block):
+        listed = [True] + [listed_ref[block, offset] >= 0 for offset in range(window)]
+        tiles = [s_ref[0, block]]
+        for offset in range(window):
+            tiles.append(jnp.where(listed[offset + 1], s_ref[offset + 1, block], -jnp.inf))
+        top = functools.reduce(jnp.maximum, tiles)
+        row_max = jnp.max(top, axis=1, keepdims=True)
+        total = functools.reduce(jnp.add, [jnp.exp(tile - row_max) for tile in tiles])
+        log_total = row_max + jnp.log(jnp.sum(total, axis=1, keepdims=True))
+        positive = jnp.sum(jnp.where(target, tiles[0], 0.0), axis=1, keepdims=True)
+        loss_ref[pl.ds(block, 1), :] = jnp.broadcast_to(
+            jnp.sum(log_total - positive, axis=0, keepdims=True), (1, pairs)
+        )
+        shares = [jnp.exp(tile - log_total) for tile in tiles]
+        shares[0] = shares[0] - jnp.where(target, 1.0, 0.0)
+        return [inverse_temp * share for share in shares]
+
+    def two_blocks(step, carry):
+        even = one_block(2 * step)
+        odd = one_block(2 * step + 1)
+        for column in range(window + 1):
+            both = jnp.concatenate([even[column], odd[column]], axis=0)
+            c_ref[column, step] = both.astype(jnp.bfloat16)
+        return carry
+
+    lax.fori_loop(0, blocks // 2, two_blocks, 0)
+
+
+def softmax_call(listed, scores, blocks, window):
+    fine, pairs = scores.shape[2:]
+    whole = pl.BlockSpec(memory_space=pltpu.VMEM)
+    return pl.pallas_call(
+        functools.partial(softmax_kernel, blocks, window),
+        in_specs=[pl.BlockSpec(memory_space=pltpu.SMEM), whole],
+        out_specs=[whole, whole],
+        out_shape=[
+            jax.ShapeDtypeStruct((window + 1, blocks // 2, 2 * fine, pairs), jnp.bfloat16),
+            jax.ShapeDtypeStruct((blocks, pairs), jnp.float32),
+        ],
+        compiler_params=pltpu.CompilerParams(vmem_limit_bytes=vmem_limit),
+        name="softmax_rows",
+    )(listed, scores)
+
+
+def grad_kernel(blocks, pairs, window, own_ref, c_ref, q_ref, d_ref, out_ref, wide, dsum, picked):
+    fine = pairs // blocks
+    seqs = wide.shape[0]
+    dsum[...] = jnp.zeros_like(dsum)
+
+    def scatter_rows(block, offset):
+        def step_rows(step, inner):
+            base = pl.multiple_of(step * 8, 8)
+            for k in range(8):
+                wide[pl.ds(own_ref[block, offset + base + k], 1), :] = picked[
+                    pl.ds(base + k, 1), :
+                ]
+            return inner
+
+        lax.fori_loop(0, pairs // 8, step_rows, 0)
+
+    def one_block(block, coefficients):
+        at = pl.multiple_of(block * pairs, pairs)
+        picked[...] = jnp.dot(
+            coefficients,
+            d_ref[pl.ds(at, (window + 1) * pairs), :],
+            preferred_element_type=jnp.float32,
+        )
+        scatter_rows(block, 0)
+        dsum[pl.ds(at, (window + 1) * pairs), :] += lax.dot_general(
+            coefficients,
+            q_ref[pl.ds(at, pairs), :],
+            (((0,), (0,)), ((), ())),
+            preferred_element_type=jnp.float32,
+        )
+
+    def two_blocks(step, carry):
+        pieces = [c_ref[:, column, step].astype(jnp.float32) for column in range(window + 1)]
+        for half in range(2):
+            coefficients = jnp.concatenate(
+                [
+                    piece[:, half * fine : (half + 1) * fine].reshape(pairs, pairs)
+                    for piece in pieces
+                ],
+                axis=1,
+            ).astype(jnp.bfloat16)
+            one_block(2 * step + half, coefficients)
+        return carry
+
+    lax.fori_loop(0, blocks // 2, two_blocks, 0)
+    dsum[: window * pairs, :] += dsum[blocks * pairs :, :]
+
+    def doc_block(block, carry):
+        at = pl.multiple_of(block * pairs, pairs)
+        picked[...] = dsum[pl.ds(at, pairs), :]
+        scatter_rows(block, pairs)
+        return carry
+
+    lax.fori_loop(0, blocks, doc_block, 0)
+    slots = out_ref.shape[1]
+
+    def narrow(part, carry):
+        at = pl.multiple_of(part * slots, slots)
+        out_ref[part] = wide[pl.ds(at, slots), :].astype(jnp.bfloat16)
+        return carry
+
+    lax.fori_loop(0, seqs // slots, narrow, 0)
+
+
+def grad_call(own, coefficients, queries, documents, blocks, pairs, window):
+    count, piece = queries.shape
+    seqs = 2 * count
+    whole = pl.BlockSpec(memory_space=pltpu.VMEM)
+    return pl.pallas_call(
+        functools.partial(grad_kernel, blocks, pairs, window),
+        in_specs=[pl.BlockSpec(memory_space=pltpu.SMEM), whole, whole, whole],
+        out_specs=whole,
+        out_shape=jax.ShapeDtypeStruct((blocks, seqs // blocks, piece), jnp.bfloat16),
+        scratch_shapes=[
+            pltpu.VMEM((seqs, piece), jnp.float32),
+            pltpu.VMEM(((blocks + window) * pairs, piece), jnp.float32),
+            pltpu.VMEM((pairs, piece), jnp.float32),
+        ],
+        compiler_params=pltpu.CompilerParams(vmem_limit_bytes=vmem_limit),
+        name="slice_grads",
+    )(own, coefficients, queries, documents)
+
+
+def project_kernel(grad_ref, normed_ref, inv_ref, out_ref):
+    parts, _, piece = grad_ref.shape
+    inverse = inv_ref[:, :1]
+    total = 0.0
+    for part in range(parts):
+        cut = slice(part * piece, (part + 1) * piece)
+        unit = normed_ref[:, cut].astype(jnp.float32) * inverse
+        total = total + unit * grad_ref[part].astype(jnp.float32)
+    along = jnp.sum(total, axis=-1, keepdims=True)
+    for part in range(parts):
+        cut = slice(part * piece, (part + 1) * piece)
+        unit = normed_ref[:, cut].astype(jnp.float32) * inverse
+        out_ref[:, cut] = grad_ref[part].astype(jnp.float32) - unit * along
+
+
+def project_call(returned, normed, inverse):
+    parts, seqs, piece = returned.shape
+    width = normed.shape[1]
+    rows = 32
+    return pl.pallas_call(
+        project_kernel,
+        grid=(seqs // rows,),
+        in_specs=[
+            pl.BlockSpec((parts, rows, piece), lambda i: (0, i, 0)),
+            pl.BlockSpec((rows, width), lambda i: (i, 0)),
+            pl.BlockSpec((rows, lanes), lambda i: (i, 0)),
+        ],
+        out_specs=pl.BlockSpec((rows, width), lambda i: (i, 0)),
+        out_shape=jax.ShapeDtypeStruct((seqs, width), jnp.float32),
+        compiler_params=pltpu.CompilerParams(vmem_limit_bytes=vmem_limit),
+        name="project_out",
+    )(returned, normed, inverse)
+
+
+def feature_plan(hidden, final_gain, last_row, pair_owner, hard_negatives):
+    devices = lax.axis_size("pb")
+    seqs, width = hidden.shape
+    pairs = pair_owner.shape[0]
+    window = hard_negatives.shape[1]
+    piece = width // devices
+    fine = pairs // devices
+    facts = jnp.concatenate([pair_owner.T.reshape(-1), hard_negatives[0]]).reshape(1, -1)
+    every = lax.all_gather(facts, "pb", axis=0, tiled=True)
+    own = every[:, : 2 * pairs]
+    listed = every[:, 2 * pairs :]
+    normed, inverse, embedding = norm_call(
+        last_row.reshape(seqs, 1), hidden, final_gain.reshape(1, width), devices
+    )
+    embedded = lax.all_to_all(embedding, "pb", split_axis=0, concat_axis=0, tiled=True)
+    queries, documents, partial_scores = score_call(
+        own, embedded.reshape(devices * seqs, piece), devices, pairs, window
+    )
+    scores = lax.psum_scatter(partial_scores, "pb", scatter_dimension=0, tiled=False)
+    coefficients, losses = softmax_call(
+        listed, scores.reshape(window + 1, devices, fine, pairs), devices, window
+    )
+    block_loss = lax.psum_scatter(losses[:, 0], "pb", scatter_dimension=0, tiled=True) / pairs
+    shared = lax.all_gather(coefficients, "pb", axis=0, tiled=False)
+    grads = grad_call(own, shared, queries, documents, devices, pairs, window)
+    returned = lax.all_to_all(grads, "pb", split_axis=0, concat_axis=0, tiled=True)
+    return project_call(returned, normed, inverse), block_loss
 
 
 def from_behind(value, axis, steps):
@@ -38,7 +355,7 @@
     )
 
 
-def local(hidden, final_gain, last_row, pair_owner, hard_negatives):
+def row_plan(hidden, final_gain, last_row, pair_owner, hard_negatives):
     values = hidden.astype(jnp.float32)
     scale_row = lax.rsqrt(jnp.mean(values * values, axis=-1, keepdims=True) + token_eps)
     normed = (values * scale_row * final_gain.astype(jnp.float32)).astype(jnp.bfloat16)
@@ -135,6 +452,10 @@
 
 
 def solution(mesh):
+    def local(hidden, final_gain, last_row, pair_owner, hard_negatives):
+        plan = feature_plan if hidden.shape[1] >= lanes * mesh.shape["pb"] else row_plan
+        return plan(hidden, final_gain, last_row, pair_owner, hard_negatives)
+
     return jax.shard_map(
         local,
         mesh=mesh,

time: 562 us -> 393 us (0.70)
  the two profiles are of different devices: /device:TPU:15 before, /device:TPU:1 now
where the time goes in v1:
time: 393 us; the launch traced here: 390 us
  blocking collectives  146 us (37%)
  waiting for transfers between devices  122 us (31%)
  Pallas kernels  84.9 us (22%)
  between operations  16.4 us (4%)
  starting transfers between devices  11.5 us (3%)
  local copies, waits for them, and re-layouts  8.67 us (2%)
    unnamed x2, blocking collectives  146 us
    reduce_scatter x1, waiting for transfers between devices, feature_plan(): lax.psum_scatter(partial_scores, 'pb', scatter_dimension=0, tiled=False)  78.4 us
    all_gather x1, waiting for transfers between devices, feature_plan(): shared = lax.all_gather(coefficients, 'pb', axis=0, tiled=False)  43.8 us
    pallas_call x1, Pallas kernels, grad_call(): pl.pallas_call(functools.partial(grad_kernel, blocks, pairs, window), in_...  34.6 us
    pallas_call x1, Pallas kernels, score_call(): pl.pallas_call(functools.partial(score_kernel, blocks, pairs, window), in...  30.6 us
    pallas_call x1, Pallas kernels, norm_call(): pl.pallas_call(norm_kernel, grid=(seqs // rows,), in_specs=[pl.BlockSpec(...  9.16 us
  transfers between devices with their start and end apart: 4, of which 2 were waited for; matrix products, arithmetic and copies ran while one was open for 1% of the time, Pallas kernels for 0%

profile of v1, /device:TPU:1, one launch (start us, length us, event | category | flops | bytes accessed | tf_op | source)
XLA Modules:
  0.0 389.5 jit_solution(8580314463309228695)
XLA Ops:
  7.2 1.3 reshape.22.gain_ref
  8.5 1.5 copy.8.last_ref
  9.9 9.2 %norm_rows.1 = (bf16[256,4096]{1,0:T(8,128)(2,1)}, f32[256,128]{1,0:T(8,128)}, bf16[16,256,256]{2,1,0:T(8,128)(2,1)}) custom-call(s32[256,1]{1,0:T(8,128)} %copy.8.last_ref, bf16[256,4096]{1,0:T(8,128)(2,1)} %hidden_ref.1, bf16[1,4096]{1,0:T(2,128)(2,1)} %reshape.22.gain_ref), custom_call_target="tpu_custom_call" | custom-call | tf_op jit(solution)/shard_map/norm_rows/pallas_call | solution.py:39
  19.1 7.5 %all-to-all-start = ((bf16[16,256,256]{2,1,0:T(8,128)(2,1)}), bf16[16,256,256]{2,1,0:T(8,128)(2,1)S(1)}, u32[]{:S(2)}, u32[]{:S(2)}) async-start(bf16[16,256,256]{2,1,0:T(8,128)(2,1)} %get-tuple-element.10), calls=%async_computation | async-start | bytes 4194304 | tf_op jit(solution)/shard_map/all_to_all | solution.py:312
  26.6 0.0 reduce-scatter.2.cloned.1.call-start
  26.6 0.0 copy-done.3
  26.7 0.6 fusion
  27.8 0.0 copy-done.4
  27.8 0.0 copy-done.5
  27.8 0.1 add_dynamic-update-slice_fusion
  28.0 84.1 %all-reduce = s32[4160]{0:T(1024)S(1)} all-reduce(s32[4160]{0:T(1024)S(1)} %add_dynamic-update-slice_fusion), channel_id=2, replica_groups=mesh['groups'=2,'pb'=16] {'pb'}, use_global_device_ids=true, to_apply=%add | all-reduce | flops 4160 | bytes 33280
  112.1 0.1 reshape.24
  112.2 0.6 slice.12.own_ref
  112.8 0.0 all-to-all-done
  112.8 1.3 copy-done
  114.1 30.6 %partial_scores.1 = (bf16[2048,256]{1,0:T(8,128)(2,1)}, bf16[2560,256]{1,0:T(8,128)(2,1)}, f32[16,640,128]{2,1,0:T(8,128)}) custom-call(s32[16,256]{1,0:T(8,128)} %slice.12.own_ref, bf16[4096,256]{1,0:T(8,128)(2,1)} %bitcast.10), custom_call_target="tpu_custom_call" | custom-call | tf_op jit(solution)/shard_map/partial_scores/pallas_call | solution.py:112
  144.7 0.0 reduce-scatter.2.cloned.1.call-update
  144.7 0.0 all-gather.4.cloned.1.call-start
  144.8 0.6 slice.13.listed_ref
  145.4 78.4 %reduce-scatter.2.cloned.1.call-done = f32[1,640,128]{2,1,0:T(8,128)} async-done(((f32[16,640,128]{2,1,0:T(8,128)}), f32[1,640,128]{2,1,0:T(8,128)}) %reduce-scatter.2.cloned.1.call-update) | async-done | bytes 327696 | tf_op jit(solution)/shard_map/reduce_scatter | solution.py:316
  223.8 3.2 softmax_rows.1
  227.0 0.0 all-gather.4.cloned.1.call-update
  227.1 43.8 %all-gather.4.cloned.1.call-done = bf16[80,8,16,128]{3,2,1,0:T(8,128)(2,1)} async-done(((bf16[5,8,16,128]{3,2,1,0:T(8,128)(2,1)}), bf16[80,8,16,128]{3,2,1,0:T(8,128)(2,1)}) %all-gather.4.cloned.1.call-update) | async-done | bytes 2621456 | tf_op jit(solution)/shard_map/all_gather | solution.py:321
  270.8 34.6 %slice_grads.1 = bf16[16,256,256]{2,1,0:T(8,128)(2,1)} custom-call(s32[16,256]{1,0:T(8,128)} %slice.12.own_ref, bf16[16,5,8,16,128]{4,3,2,1,0:T(8,128)(2,1)} %bitcast.11, bf16[2048,256]{1,0:T(8,128)(2,1)} %get-tuple-element.13.q_ref, bf16[2560,256]{1,0:T(8,128)(2,1)} %get-tuple-element.14.d_ref), custom_call_target="tpu_custom_call" | custom-call | tf_op jit(solution)/shard_map/slice_grads/pallas_call | solution.py:249
  305.5 3.9 all-to-all-start.1
  309.4 0.0 copy-done.2
  309.4 0.1 slice_reduce_fusion
  309.5 61.6 %all-reduce.1 = f32[16]{0:T(128)S(1)} all-reduce(f32[16]{0:T(128)S(1)} %slice_reduce_fusion), channel_id=5, replica_groups=mesh['groups'=2,'pb'=16] {'pb'}, use_global_device_ids=true, to_apply=%region_1.0.clone | all-reduce | flops 16 | bytes 128
  371.0 1.2 dynamic-slice.2
  372.8 0.0 all-to-all-done.1.grad_ref
  372.8 1.3 copy-done.1
  374.2 7.4 %project_out.1 = f32[256,4096]{1,0:T(8,128)} custom-call(bf16[16,256,256]{2,1,0:T(8,128)(2,1)} %copy-done.1, bf16[256,4096]{1,0:T(8,128)(2,1)} %get-tuple-element.15.normed_ref, f32[256,128]{1,0:T(8,128)} %get-tuple-element.16.inv_ref), custom_call_target="tpu_custom_call" | custom-call | tf_op jit(solution)/shard_map/project_out/pallas_call | solution.py:283
  (7 shorter events, 0.0 us)
Async XLA Ops:
  19.1 7.6 %copy-start.3 = (u32[32]{0:T(128)S(1)}, u32[32]{0:T(128)}, u32[]{:S(2)}) copy-start(u32[32]{0:T(128)} %constant.7) | copy-start | bytes 388
  19.1 8.7 %copy-start.4 = (s32[128,2]{0,1:T(2,128)S(1)}, s32[128,2]{0,1:T(2,128)}, u32[]{:S(2)}) copy-start(s32[128,2]{0,1:T(2,128)} %param.8) | copy-start | bytes 3076
  19.1 8.7 %copy-start.5 = (s32[1,4]{1,0:T(1,128)S(1)}, s32[1,4]{1,0:T(1,128)}, u32[]{:S(2)}) copy-start(s32[1,4]{1,0:T(1,128)} %param.9) | copy-start | bytes 52
  19.1 93.7 %all-to-all-start = ((bf16[16,256,256]{2,1,0:T(8,128)(2,1)}), bf16[16,256,256]{2,1,0:T(8,128)(2,1)S(1)}, u32[]{:S(2)}, u32[]{:S(2)}) async-start(bf16[16,256,256]{2,1,0:T(8,128)(2,1)} %get-tuple-element.10), calls=%async_computation | async-start | bytes 4194304 | tf_op jit(solution)/shard_map/all_to_all | solution.py:312
  26.6 197.2 %reduce-scatter.2.cloned.1.call-start = ((), (), s32[]{:S(2)}) async-start(), calls=%async_computation.3 | async-start | bytes 5570560 | tf_op jit(solution)/shard_map/reduce_scatter | solution.py:316
  112.8 1.3 copy-start
  144.7 126.1 %all-gather.4.cloned.1.call-start = ((), (), s32[]{:S(2)}) async-start(), calls=%async_computation.4 | async-start | bytes 2785280 | tf_op jit(solution)/shard_map/all_gather | solution.py:321
  305.5 3.9 %copy-start.2 = (f32[16,128]{1,0:T(8,128)S(1)}, f32[16,128]{1,0:T(8,128)}, u32[]{:S(2)}) copy-start(f32[16,128]{1,0:T(8,128)} %get-tuple-element.17) | copy-start | bytes 24580
  305.5 67.4 %all-to-all-start.1 = ((bf16[16,256,256]{2,1,0:T(8,128)(2,1)}), bf16[16,256,256]{2,1,0:T(8,128)(2,1)S(1)}, u32[]{:S(2)}, u32[]{:S(2)}) async-start(bf16[16,256,256]{2,1,0:T(8,128)(2,1)} %slice_grads.1), calls=%async_computation.2 | async-start | bytes 4194304 | tf_op jit(solution)/shard_map/all_to_all | solution.py:323
  372.8 1.3 copy-start.1
Sparse Core Ops, SparseCore 0:
  144.8 78.9 reduce-scatter.1
  227.2 43.6 all-gather.3

commit v2 on v1

--- a/solution.py
+++ b/solution.py
@@ -14,70 +14,102 @@
 vmem_limit = 56 * 1024 * 1024
 
 
-def norm_kernel(last_ref, hidden_ref, gain_ref, normed_ref, inv_ref, emb_ref):
-    rows, width = normed_ref.shape
-    source = hidden_ref.shape[0]
+def norm_kernel(last_ref, hidden_ref, gain_ref, owner_ref, negative_ref, normed_ref, inv_ref, emb_ref):
+    seqs, width = normed_ref.shape
     parts, _, piece = emb_ref.shape
-    columns = lax.broadcasted_iota(jnp.int32, (rows, source), 1)
-    pick = jnp.where(columns == last_ref[...], 1.0, 0.0).astype(jnp.bfloat16)
-    values = jnp.dot(pick, hidden_ref[...], preferred_element_type=jnp.float32)
-    scale = lax.rsqrt(jnp.mean(values * values, axis=-1, keepdims=True) + token_eps)
-    normed = (values * scale * gain_ref[...].astype(jnp.float32)).astype(jnp.bfloat16)
-    normed_ref[...] = normed
-    pooled = normed.astype(jnp.float32)
-    inverse = lax.rsqrt(jnp.sum(pooled * pooled, axis=-1, keepdims=True) + unit_eps)
+    pairs = owner_ref.shape[0]
+    cuts = [slice(part * piece, (part + 1) * piece) for part in range(parts)]
+    sources = lax.broadcasted_iota(jnp.int32, (seqs, seqs), 0)
+    pick = jnp.where(sources == last_ref[...], 1.0, 0.0).astype(jnp.bfloat16)
+
+    def folded(squares):
+        return functools.reduce(
+            jnp.add, [squares[:, at : at + lanes] for at in range(0, piece, lanes)]
+        )
+
+    total = jnp.zeros((seqs, lanes), jnp.float32)
+    for cut in cuts:
+        values = lax.dot_general(
+            pick, hidden_ref[:, cut], (((0,), (0,)), ((), ())), preferred_element_type=jnp.float32
+        )
+        normed_ref[:, cut] = values.astype(jnp.bfloat16)
+        total = total + folded(values * values)
+    scale = lax.rsqrt(jnp.sum(total, axis=-1, keepdims=True) / width + token_eps)
+    total = jnp.zeros((seqs, lanes), jnp.float32)
+    for cut in cuts:
+        values = normed_ref[:, cut].astype(jnp.float32)
+        normed = (values * scale * gain_ref[:, cut].astype(jnp.float32)).astype(jnp.bfloat16)
+        normed_ref[:, cut] = normed
+        pooled = normed.astype(jnp.float32)
+        total = total + folded(pooled * pooled)
+    inverse = lax.rsqrt(jnp.sum(total, axis=-1, keepdims=True) + unit_eps)
     inv_ref[...] = jnp.broadcast_to(inverse, inv_ref.shape)
-    embedding = (pooled * inverse).astype(jnp.bfloat16)
-    for part in range(parts):
-        emb_ref[part] = embedding[:, part * piece : (part + 1) * piece]
-
-
-def norm_call(last_column, hidden, gain_row, parts):
+
+    lane = lax.broadcasted_iota(jnp.int32, (pairs, lanes), 1)
+    columns = jnp.where(lane == 0, owner_ref[:, :1], jnp.where(lane == 1, owner_ref[:, 1:], 0))
+    owners = columns.astype(jnp.float32).T
+    high = jnp.floor(owners * (1.0 / 256.0))
+    low = owners - 256.0 * high
+    row = lax.broadcasted_iota(jnp.int32, (16, lanes), 0)
+    spot = lax.broadcasted_iota(jnp.int32, (16, lanes), 1)
+    left = jnp.where(row == 0, low[:1], jnp.where(row == 1, high[:1], 0.0))
+    right = jnp.where(row == 0, low[1:2], jnp.where(row == 1, high[1:2], 0.0))
+    for offset in range(negative_ref.shape[1]):
+        named = (negative_ref[0, offset] >= 0).astype(jnp.float32)
+        left = jnp.where((row == 2) & (spot == offset), named, left)
+    facts = jnp.concatenate([left, right], axis=1).astype(jnp.bfloat16)
+
+    for part, cut in enumerate(cuts):
+        emb_ref[part, :seqs] = (normed_ref[:, cut].astype(jnp.float32) * inverse).astype(jnp.bfloat16)
+        emb_ref[part, seqs:] = facts
+
+
+def norm_call(last_row, hidden, gain_row, pair_owner, hard_negatives, parts):
     seqs, width = hidden.shape
     piece = width // parts
-    rows = 32
+    whole = pl.BlockSpec(memory_space=pltpu.VMEM)
     return pl.pallas_call(
         norm_kernel,
-        grid=(seqs // rows,),
-        in_specs=[
-            pl.BlockSpec((rows, 1), lambda i: (i, 0)),
-            pl.BlockSpec((seqs, width), lambda i: (0, 0)),
-            pl.BlockSpec((1, width), lambda i: (0, 0)),
-        ],
-        out_specs=[
-            pl.BlockSpec((rows, width), lambda i: (i, 0)),
-            pl.BlockSpec((rows, lanes), lambda i: (i, 0)),
-            pl.BlockSpec((parts, rows, piece), lambda i: (0, i, 0)),
-        ],
+        in_specs=[whole, whole, whole, whole, pl.BlockSpec(memory_space=pltpu.SMEM)],
+        out_specs=[whole, whole, whole],
         out_shape=[
             jax.ShapeDtypeStruct((seqs, width), jnp.bfloat16),
             jax.ShapeDtypeStruct((seqs, lanes), jnp.float32),
-            jax.ShapeDtypeStruct((parts, seqs, piece), jnp.bfloat16),
+            jax.ShapeDtypeStruct((parts, seqs + 16, piece), jnp.bfloat16),
         ],
         compiler_params=pltpu.CompilerParams(vmem_limit_bytes=vmem_limit),
         name="norm_rows",
-    )(last_column, hidden, gain_row)
-
-
-def score_kernel(blocks, pairs, window, own_ref, emb_ref, q_ref, d_ref, s_ref, wide, picked):
-    seqs = emb_ref.shape[0]
-    chunk = 256
+    )(last_row, hidden, gain_row, pair_owner, hard_negatives)
+
+
+def score_kernel(
+    blocks, pairs, window, emb_ref, q_ref, d_ref, s_ref, own_ref, listed_ref, wide, picked, own, sem
+):
+    seqs = emb_ref.shape[1] - 16
+    facts = emb_ref[:, seqs:, :].astype(jnp.float32)
+    own_ref[...] = (facts[:, 0, :] + 256.0 * facts[:, 1, :]).astype(jnp.int32)
+    listed_ref[...] = facts[:, 2, :lanes].astype(jnp.int32)
+    fetch = pltpu.make_async_copy(own_ref, own, sem)
+    fetch.start()
 
     def widen(step, carry):
-        at = pl.multiple_of(step * chunk, chunk)
-        wide[pl.ds(at, chunk), :] = emb_ref[pl.ds(at, chunk), :].astype(jnp.float32)
+        at = pl.multiple_of(step * seqs, seqs)
+        wide[pl.ds(at, seqs), :] = emb_ref[step, :seqs, :].astype(jnp.float32)
         return carry
 
-    lax.fori_loop(0, seqs // chunk, widen, 0)
+    lax.fori_loop(0, emb_ref.shape[0], widen, 0)
+    fetch.wait()
+    unroll = 16
 
     def pick_block(block, carry):
         def pick_rows(step, inner):
-            base = pl.multiple_of(step * 8, 8)
-            for k in range(8):
-                picked[pl.ds(base + k, 1), :] = wide[pl.ds(own_ref[block, base + k], 1), :]
+            base = pl.multiple_of(step * unroll, unroll)
+            rows = [wide[pl.ds(own[block, base + k], 1), :] for k in range(unroll)]
+            for k in range(unroll):
+                picked[pl.ds(base + k, 1), :] = rows[k]
             return inner
 
-        lax.fori_loop(0, 2 * pairs // 8, pick_rows, 0)
+        lax.fori_loop(0, 2 * pairs // unroll, pick_rows, 0)
         at = pl.multiple_of(block * pairs, pairs)
         q_ref[pl.ds(at, pairs), :] = picked[:pairs, :].astype(jnp.bfloat16)
         d_ref[pl.ds(at, pairs), :] = picked[pairs:, :].astype(jnp.bfloat16)
@@ -90,76 +122,84 @@
 
     def score_block(block, carry):
         at = pl.multiple_of(block * pairs, pairs)
-        queries = q_ref[pl.ds(at, pairs), :]
+        tiles = inverse_temp * lax.dot_general(
+            q_ref[pl.ds(at, pairs), :],
+            d_ref[pl.ds(at, (window + 1) * pairs), :],
+            (((1,), (1,)), ((), ())),
+            preferred_element_type=jnp.float32,
+        )
         for column in range(window + 1):
-            there = pl.multiple_of(at + column * pairs, pairs)
-            documents = d_ref[pl.ds(there, pairs), :]
-            tile = inverse_temp * lax.dot_general(
-                queries, documents, (((1,), (1,)), ((), ())), preferred_element_type=jnp.float32
-            )
             row = pl.multiple_of((column * blocks + block) * fine, fine)
+            tile = tiles[:, column * pairs : (column + 1) * pairs]
             s_ref[:, pl.ds(row, fine), :] = tile.reshape(groups, fine, pairs)
         return carry
 
     lax.fori_loop(0, blocks, score_block, 0)
 
 
-def score_call(own, embedded, blocks, pairs, window):
-    seqs, piece = embedded.shape
+def score_call(embedded, blocks, pairs, window):
+    parts, rows, piece = embedded.shape
     fine = pairs // blocks
     tiles = blocks * (window + 1)
     whole = pl.BlockSpec(memory_space=pltpu.VMEM)
     return pl.pallas_call(
         functools.partial(score_kernel, blocks, pairs, window),
-        in_specs=[pl.BlockSpec(memory_space=pltpu.SMEM), whole],
-        out_specs=[whole, whole, whole],
+        in_specs=[whole],
+        out_specs=[whole] * 5,
         out_shape=[
             jax.ShapeDtypeStruct((blocks * pairs, piece), jnp.bfloat16),
             jax.ShapeDtypeStruct(((blocks + window) * pairs, piece), jnp.bfloat16),
             jax.ShapeDtypeStruct((blocks, tiles * fine, pairs), jnp.float32),
+            jax.ShapeDtypeStruct((blocks, 2 * pairs), jnp.int32),
+            jax.ShapeDtypeStruct((blocks, lanes), jnp.int32),
         ],
         scratch_shapes=[
-            pltpu.VMEM((seqs, piece), jnp.float32),
+            pltpu.VMEM((parts * (rows - 16), piece), jnp.float32),
             pltpu.VMEM((2 * pairs, piece), jnp.float32),
+            pltpu.SMEM((blocks, 2 * pairs), jnp.int32),
+            pltpu.SemaphoreType.DMA,
         ],
         compiler_params=pltpu.CompilerParams(vmem_limit_bytes=vmem_limit),
         name="partial_scores",
-    )(own, embedded)
-
-
-def softmax_kernel(blocks, window, listed_ref, s_ref, c_ref, loss_ref):
+    )(embedded)
+
+
+def softmax_kernel(blocks, window, listed_ref, s_ref, c_ref):
     fine = s_ref.shape[2]
     pairs = s_ref.shape[3]
     first = lax.axis_index("pb") * fine
     rows = lax.broadcasted_iota(jnp.int32, (fine, pairs), 0) + first
     target = lax.broadcasted_iota(jnp.int32, (fine, pairs), 1) == rows
-
-    def one_block(block):
-        listed = [True] + [listed_ref[block, offset] >= 0 for offset in range(window)]
+    lane = lax.broadcasted_iota(jnp.int32, (16, pairs), 1)
+
+    def one_block(block, losses):
         tiles = [s_ref[0, block]]
         for offset in range(window):
-            tiles.append(jnp.where(listed[offset + 1], s_ref[offset + 1, block], -jnp.inf))
+            named = listed_ref[block, offset] > 0
+            tiles.append(jnp.where(named, s_ref[offset + 1, block], -jnp.inf))
         top = functools.reduce(jnp.maximum, tiles)
         row_max = jnp.max(top, axis=1, keepdims=True)
         total = functools.reduce(jnp.add, [jnp.exp(tile - row_max) for tile in tiles])
         log_total = row_max + jnp.log(jnp.sum(total, axis=1, keepdims=True))
         positive = jnp.sum(jnp.where(target, tiles[0], 0.0), axis=1, keepdims=True)
-        loss_ref[pl.ds(block, 1), :] = jnp.broadcast_to(
-            jnp.sum(log_total - positive, axis=0, keepdims=True), (1, pairs)
-        )
+        loss = jnp.sum(log_total - positive, axis=0, keepdims=True)
         shares = [jnp.exp(tile - log_total) for tile in tiles]
         shares[0] = shares[0] - jnp.where(target, 1.0, 0.0)
-        return [inverse_temp * share for share in shares]
-
-    def two_blocks(step, carry):
-        even = one_block(2 * step)
-        odd = one_block(2 * step + 1)
+        return [inverse_temp * share for share in shares], jnp.where(lane == block, loss, losses)
+
+    def two_blocks(step, losses):
+        even, losses = one_block(2 * step, losses)
+        odd, losses = one_block(2 * step + 1, losses)
         for column in range(window + 1):
             both = jnp.concatenate([even[column], odd[column]], axis=0)
-            c_ref[column, step] = both.astype(jnp.bfloat16)
-        return carry
-
-    lax.fori_loop(0, blocks // 2, two_blocks, 0)
+            c_ref[column * (blocks // 2) + step] = both.astype(jnp.bfloat16)
+        return losses
+
+    losses = lax.fori_loop(0, blocks // 2, two_blocks, jnp.zeros((16, pairs), jnp.float32))
+    coarse = losses.astype(jnp.bfloat16).astype(jnp.float32)
+    rank = lax.broadcasted_iota(jnp.int32, (16, pairs), 0)
+    both = jnp.where(rank == 0, coarse, jnp.where(rank == 1, losses - coarse, 0.0))
+    c_ref[(window + 1) * (blocks // 2)] = both.astype(jnp.bfloat16)
 
 
 def softmax_call(listed, scores, blocks, window):
@@ -168,31 +208,38 @@
     return pl.pallas_call(
         functools.partial(softmax_kernel, blocks, window),
         in_specs=[pl.BlockSpec(memory_space=pltpu.SMEM), whole],
-        out_specs=[whole, whole],
-        out_shape=[
-            jax.ShapeDtypeStruct((window + 1, blocks // 2, 2 * fine, pairs), jnp.bfloat16),
-            jax.ShapeDtypeStruct((blocks, pairs), jnp.float32),
-        ],
+        out_specs=whole,
+        out_shape=jax.ShapeDtypeStruct(
+            ((window + 1) * blocks // 2 + 1, 2 * fine, pairs), jnp.bfloat16
+        ),
         compiler_params=pltpu.CompilerParams(vmem_limit_bytes=vmem_limit),
         name="softmax_rows",
     )(listed, scores)
 
 
-def grad_kernel(blocks, pairs, window, own_ref, c_ref, q_ref, d_ref, out_ref, wide, dsum, picked):
+def grad_kernel(
+    blocks, pairs, window, own_ref, c_ref, q_ref, d_ref, out_ref, loss_ref, wide, dsum, picked
+):
     fine = pairs // blocks
     seqs = wide.shape[0]
+    unroll = 16
+    half_blocks = blocks // 2
+    coarse = c_ref[:, (window + 1) * half_blocks].astype(jnp.float32)
+    losses = jnp.sum(coarse[:, 0, :] + coarse[:, 1, :], axis=0, keepdims=True) / pairs
+    lane = lax.broadcasted_iota(jnp.int32, losses.shape, 1)
+    mine = jnp.where(lane == lax.axis_index("pb"), losses, 0.0)
+    loss_ref[...] = jnp.broadcast_to(jnp.sum(mine, axis=1, keepdims=True), loss_ref.shape)
     dsum[...] = jnp.zeros_like(dsum)
 
     def scatter_rows(block, offset):
         def step_rows(step, inner):
-            base = pl.multiple_of(step * 8, 8)
-            for k in range(8):
-                wide[pl.ds(own_ref[block, offset + base + k], 1), :] = picked[
-                    pl.ds(base + k, 1), :
-                ]
+            base = pl.multiple_of(step * unroll, unroll)
+            rows = [picked[pl.ds(base + k, 1), :] for k in range(unroll)]
+            for k in range(unroll):
+                wide[pl.ds(own_ref[block, offset + base + k], 1), :] = rows[k]
             return inner
 
-        lax.fori_loop(0, pairs // 8, step_rows, 0)
+        lax.fori_loop(0, pairs // unroll, step_rows, 0)
 
     def one_block(block, coefficients):
         at = pl.multiple_of(block * pairs, pairs)
@@ -210,7 +257,10 @@
         )
 
     def two_blocks(step, carry):
-        pieces = [c_ref[:, column, step].astype(jnp.float32) for column in range(window + 1)]
+        pieces = [
+            c_ref[:, column * half_blocks + step].astype(jnp.float32)
+            for column in range(window + 1)
+        ]
         for half in range(2):
             coefficients = jnp.concatenate(
                 [
@@ -222,7 +272,7 @@
             one_block(2 * step + half, coefficients)
         return carry
 
-    lax.fori_loop(0, blocks // 2, two_blocks, 0)
+    lax.fori_loop(0, half_blocks, two_blocks, 0)
     dsum[: window * pairs, :] += dsum[blocks * pairs :, :]
 
     def doc_block(block, carry):
@@ -249,8 +299,11 @@
     return pl.pallas_call(
         functools.partial(grad_kernel, blocks, pairs, window),
         in_specs=[pl.BlockSpec(memory_space=pltpu.SMEM), whole, whole, whole],
-        out_specs=whole,
-        out_shape=jax.ShapeDtypeStruct((blocks, seqs // blocks, piece), jnp.bfloat16),
+        out_specs=[whole, whole],
+        out_shape=[
+            jax.ShapeDtypeStruct((blocks, seqs // blocks, piece), jnp.bfloat16),
+            jax.ShapeDtypeStruct((1, lanes), jnp.float32),
+        ],
         scratch_shapes=[
             pltpu.VMEM((seqs, piece), jnp.float32),
             pltpu.VMEM(((blocks + window) * pairs, piece), jnp.float32),
@@ -297,31 +350,23 @@
 
 def feature_plan(hidden, final_gain, last_row, pair_owner, hard_negatives):
     devices = lax.axis_size("pb")
-    seqs, width = hidden.shape
+    width = hidden.shape[1]
     pairs = pair_owner.shape[0]
     window = hard_negatives.shape[1]
-    piece = width // devices
     fine = pairs // devices
-    facts = jnp.concatenate([pair_owner.T.reshape(-1), hard_negatives[0]]).reshape(1, -1)
-    every = lax.all_gather(facts, "pb", axis=0, tiled=True)
-    own = every[:, : 2 * pairs]
-    listed = every[:, 2 * pairs :]
     normed, inverse, embedding = norm_call(
-        last_row.reshape(seqs, 1), hidden, final_gain.reshape(1, width), devices
+        last_row, hidden, final_gain.reshape(1, width), pair_owner, hard_negatives, devices
     )
     embedded = lax.all_to_all(embedding, "pb", split_axis=0, concat_axis=0, tiled=True)
-    queries, documents, partial_scores = score_call(
-        own, embedded.reshape(devices * seqs, piece), devices, pairs, window
-    )
+    queries, documents, partial_scores, own, listed = score_call(embedded, devices, pairs, window)
     scores = lax.psum_scatter(partial_scores, "pb", scatter_dimension=0, tiled=False)
-    coefficients, losses = softmax_call(
+    coefficients = softmax_call(
         listed, scores.reshape(window + 1, devices, fine, pairs), devices, window
     )
-    block_loss = lax.psum_scatter(losses[:, 0], "pb", scatter_dimension=0, tiled=True) / pairs
     shared = lax.all_gather(coefficients, "pb", axis=0, tiled=False)
-    grads = grad_call(own, shared, queries, documents, devices, pairs, window)
+    grads, loss = grad_call(own, shared, queries, documents, devices, pairs, window)
     returned = lax.all_to_all(grads, "pb", split_axis=0, concat_axis=0, tiled=True)
-    return project_call(returned, normed, inverse), block_loss
+    return project_call(returned, normed, inverse), loss[0, :1]
 
 
 def from_behind(value, axis, steps):

time: 393 us -> 328 us (0.83)
  blocking collectives: 146 us -> 112 us
  starting transfers between devices: 11.5 us -> 0.08 us
  local copies, waits for them, and re-layouts: 8.67 us -> 2.72 us
  Pallas kernels: 84.9 us -> 79.1 us
    unnamed x2 -> x0, blocking collectives: 146 us -> none
    all_to_all x0 -> x2, blocking collectives: none -> 112 us  [the longest x1 59.3 us: feature_plan(): lax.all_to_all(embedding, 'pb', split_axis=0, concat_axis=0, tiled=True)]
    all_to_all x2 -> x0, starting transfers between devices: 11.4 us -> none  [the longest x1 7.49 us: feature_plan(): lax.all_to_all(embedding, 'pb', split_axis=0, concat_axis=0, tiled=True)]
  transfers between devices with their start and end apart: 4 -> 2, of which waited for: 2 -> 2; matrix products, arithmetic and copies ran while one was open for 1% -> 0% of each run, Pallas kernels for 0% -> 0%
where the time goes in v2:
time: 328 us; the launch traced here: 327 us
  waiting for transfers between devices  120 us (37%)
  blocking collectives  112 us (34%)
  Pallas kernels  79.1 us (24%)
  between operations  14 us (4%)
    reduce_scatter x1, waiting for transfers between devices, feature_plan(): lax.psum_scatter(partial_scores, 'pb', scatter_dimension=0, tiled=False)  75.8 us
    all_to_all x1, blocking collectives, feature_plan(): lax.all_to_all(embedding, 'pb', split_axis=0, concat_axis=0, tiled=True)  59.3 us
    all_to_all x1, blocking collectives, feature_plan(): lax.all_to_all(grads, 'pb', split_axis=0, concat_axis=0, tiled=True)  52.2 us
    all_gather x1, waiting for transfers between devices, feature_plan(): shared = lax.all_gather(coefficients, 'pb', axis=0, tiled=False)  43.9 us
    pallas_call x1, Pallas kernels, grad_call(): pl.pallas_call(functools.partial(grad_kernel, blocks, pairs, window), in_...  33.1 us
    pallas_call x1, Pallas kernels, score_call(): pl.pallas_call(functools.partial(score_kernel, blocks, pairs, window), in...  29.8 us
    pallas_call x1, Pallas kernels, project_call(): pl.pallas_call(project_kernel, grid=(seqs // rows,), in_specs=[pl.BlockSp...  7.36 us
  transfers between devices with their start and end apart: 2, of which 2 were waited for; matrix products, arithmetic and copies ran while one was open for 0% of the time, Pallas kernels for 0%

profile of v2, /device:TPU:1, one launch (start us, length us, event | category | flops | bytes accessed | tf_op | source)
XLA Modules:
  0.0 327.3 jit_solution(12993282234789369130)
XLA Ops:
  7.2 0.0 reduce-scatter.2.cloned.1.call-start
  7.2 1.3 reshape.7.gain_ref
  8.5 1.4 copy.8.owner_ref
  9.9 5.7 %norm_rows.1 = (bf16[256,4096]{1,0:T(8,128)(2,1)}, f32[256,128]{1,0:T(8,128)}, bf16[16,272,256]{2,1,0:T(8,128)(2,1)}) custom-call(s32[1,256]{1,0:T(1,128)} %last_ref.1, bf16[256,4096]{1,0:T(8,128)(2,1)} %hidden_ref.1, bf16[1,4096]{1,0:T(2,128)(2,1)} %reshape.7.gain_ref, s32[128,2]{1,0:T(8,128)} %copy.8.owner_ref, s32[1,4]{1,0:T(1,128)} %negative_ref.1), custom_call_target="tpu_custom_call" | custom-call | tf_op jit(solution)/shard_map/norm_rows/pallas_call | solution.py:71
  15.6 59.3 %all_to_all.10.emb_ref = bf16[16,272,256]{2,1,0:T(8,128)(2,1)} all-to-all(bf16[16,272,256]{2,1,0:T(8,128)(2,1)} %get-tuple-element.12), channel_id=1, replica_groups=mesh['groups'=2,'pb'=16] {'pb'}, dimensions={0} | all-to-all | bytes 4456448 | tf_op jit(solution)/shard_map/all_to_all | solution.py:360
  74.9 29.8 %partial_scores.1 = (bf16[2048,256]{1,0:T(8,128)(2,1)}, bf16[2560,256]{1,0:T(8,128)(2,1)}, f32[16,640,128]{2,1,0:T(8,128)}, s32[16,256]{1,0:T(8,128)}, s32[16,128]{1,0:T(8,128)}) custom-call(bf16[16,272,256]{2,1,0:T(8,128)(2,1)} %all_to_all.10.emb_ref), custom_call_target="tpu_custom_call" | custom-call | tf_op jit(solution)/shard_map/partial_scores/pallas_call | solution.py:145
  104.7 0.0 reduce-scatter.2.cloned.1.call-update
  104.8 0.0 all-gather.3.cloned.1.call-start
  104.8 75.8 %reduce-scatter.2.cloned.1.call-done = f32[1,640,128]{2,1,0:T(8,128)} async-done(((f32[16,640,128]{2,1,0:T(8,128)}), f32[1,640,128]{2,1,0:T(8,128)}) %reduce-scatter.2.cloned.1.call-update) | async-done | bytes 327696 | tf_op jit(solution)/shard_map/reduce_scatter | solution.py:362
  180.6 3.2 softmax_rows.1
  183.8 0.0 all-gather.3.cloned.1.call-update
  183.8 43.9 %all-gather.3.cloned.1.call-done = bf16[656,16,128]{2,1,0:T(8,128)(2,1)} async-done(((bf16[41,16,128]{2,1,0:T(8,128)(2,1)}), bf16[656,16,128]{2,1,0:T(8,128)(2,1)}) %all-gather.3.cloned.1.call-update) | async-done | bytes 2686992 | tf_op jit(solution)/shard_map/all_gather | solution.py:366
  227.8 33.1 %slice_grads.1 = (bf16[16,256,256]{2,1,0:T(8,128)(2,1)}, f32[1,128]{1,0:T(1,128)}) custom-call(s32[16,256]{1,0:T(8,128)} %get-tuple-element.13.own_ref, bf16[16,41,16,128]{3,2,1,0:T(8,128)(2,1)} %bitcast.4, bf16[2048,256]{1,0:T(8,128)(2,1)} %get-tuple-element.16.q_ref, bf16[2560,256]{1,0:T(8,128)(2,1)} %get-tuple-element.17.d_ref), custom_call_target="tpu_custom_call" | custom-call | tf_op jit(solution)/shard_map/slice_grads/pallas_call | solution.py:299
  260.9 52.2 %all_to_all.11.grad_ref = bf16[16,256,256]{2,1,0:T(8,128)(2,1)} all-to-all(bf16[16,256,256]{2,1,0:T(8,128)(2,1)} %get-tuple-element.18), channel_id=1, replica_groups=mesh['groups'=2,'pb'=16] {'pb'}, dimensions={0} | all-to-all | bytes 4194304 | tf_op jit(solution)/shard_map/all_to_all | solution.py:368
  313.1 7.4 %project_out.1 = f32[256,4096]{1,0:T(8,128)} custom-call(bf16[16,256,256]{2,1,0:T(8,128)(2,1)} %all_to_all.11.grad_ref, bf16[256,4096]{1,0:T(8,128)(2,1)} %get-tuple-element.19.normed_ref, f32[256,128]{1,0:T(8,128)} %get-tuple-element.20.inv_ref), custom_call_target="tpu_custom_call" | custom-call | tf_op jit(solution)/shard_map/project_out/pallas_call | solution.py:336
Async XLA Ops:
  7.2 173.4 %reduce-scatter.2.cloned.1.call-start = ((), (), s32[]{:S(2)}) async-start(), calls=%async_computation.3 | async-start | bytes 5570560 | tf_op jit(solution)/shard_map/reduce_scatter | solution.py:362
  104.8 123.0 %all-gather.3.cloned.1.call-start = ((), (), s32[]{:S(2)}) async-start(), calls=%async_computation.4 | async-start | bytes 2854912 | tf_op jit(solution)/shard_map/all_gather | solution.py:366
Sparse Core Ops, SparseCore 0:
  104.9 75.6 reduce-scatter.1
  184.0 43.7 all-gather.2

commit v3 on v2

--- a/solution.py
+++ b/solution.py
@@ -12,6 +12,17 @@
 unit_eps = 1e-06
 lanes = 128
 vmem_limit = 56 * 1024 * 1024
+
+
+def spread(target, at, value):
+    count, width = value.shape
+    for part in range(width // lanes):
+        target[pl.ds(at, count), part, :] = value[:, part * lanes : (part + 1) * lanes]
+
+
+def gathered(source, at, count):
+    parts = [source[pl.ds(at, count), part, :] for part in range(source.shape[1])]
+    return jnp.concatenate(parts, axis=1)
 
 
 def norm_kernel(last_ref, hidden_ref, gain_ref, owner_ref, negative_ref, normed_ref, inv_ref, emb_ref):
@@ -94,7 +105,7 @@
 
     def widen(step, carry):
         at = pl.multiple_of(step * seqs, seqs)
-        wide[pl.ds(at, seqs), :] = emb_ref[step, :seqs, :].astype(jnp.float32)
+        spread(wide, at, emb_ref[step, :seqs, :].astype(jnp.float32))
         return carry
 
     lax.fori_loop(0, emb_ref.shape[0], widen, 0)
@@ -104,15 +115,15 @@
     def pick_block(block, carry):
         def pick_rows(step, inner):
             base = pl.multiple_of(step * unroll, unroll)
-            rows = [wide[pl.ds(own[block, base + k], 1), :] for k in range(unroll)]
+            rows = [wide[own[block, base + k]] for k in range(unroll)]
             for k in range(unroll):
-                picked[pl.ds(base + k, 1), :] = rows[k]
+                picked[base + k] = rows[k]
             return inner
 
         lax.fori_loop(0, 2 * pairs // unroll, pick_rows, 0)
         at = pl.multiple_of(block * pairs, pairs)
-        q_ref[pl.ds(at, pairs), :] = picked[:pairs, :].astype(jnp.bfloat16)
-        d_ref[pl.ds(at, pairs), :] = picked[pairs:, :].astype(jnp.bfloat16)
+        q_ref[pl.ds(at, pairs), :] = gathered(picked, 0, pairs).astype(jnp.bfloat16)
+        d_ref[pl.ds(at, pairs), :] = gathered(picked, pairs, pairs).astype(jnp.bfloat16)
         return carry
 
     lax.fori_loop(0, blocks, pick_block, 0)
@@ -154,8 +165,8 @@
             jax.ShapeDtypeStruct((blocks, lanes), jnp.int32),
         ],
         scratch_shapes=[
-            pltpu.VMEM((parts * (rows - 16), piece), jnp.float32),
-            pltpu.VMEM((2 * pairs, piece), jnp.float32),
+            pltpu.VMEM((parts * (rows - 16), piece // lanes, lanes), jnp.float32),
+            pltpu.VMEM((2 * pairs, piece // lanes, lanes), jnp.float32),
             pltpu.SMEM((blocks, 2 * pairs), jnp.int32),
             pltpu.SemaphoreType.DMA,
         ],
@@ -234,20 +245,21 @@
     def scatter_rows(block, offset):
         def step_rows(step, inner):
             base = pl.multiple_of(step * unroll, unroll)
-            rows = [picked[pl.ds(base + k, 1), :] for k in range(unroll)]
+            rows = [picked[base + k] for k in range(unroll)]
             for k in range(unroll):
-                wide[pl.ds(own_ref[block, offset + base + k], 1), :] = rows[k]
+                wide[own_ref[block, offset + base + k]] = rows[k]
             return inner
 
         lax.fori_loop(0, pairs // unroll, step_rows, 0)
 
     def one_block(block, coefficients):
         at = pl.multiple_of(block * pairs, pairs)
-        picked[...] = jnp.dot(
+        summed = jnp.dot(
             coefficients,
             d_ref[pl.ds(at, (window + 1) * pairs), :],
             preferred_element_type=jnp.float32,
         )
+        spread(picked, 0, summed)
         scatter_rows(block, 0)
         dsum[pl.ds(at, (window + 1) * pairs), :] += lax.dot_general(
             coefficients,
@@ -277,7 +289,7 @@
 
     def doc_block(block, carry):
         at = pl.multiple_of(block * pairs, pairs)
-        picked[...] = dsum[pl.ds(at, pairs), :]
+        spread(picked, 0, dsum[pl.ds(at, pairs), :])
         scatter_rows(block, pairs)
         return carry
 
@@ -286,7 +298,7 @@
 
     def narrow(part, carry):
         at = pl.multiple_of(part * slots, slots)
-        out_ref[part] = wide[pl.ds(at, slots), :].astype(jnp.bfloat16)
+        out_ref[part] = gathered(wide, at, slots).astype(jnp.bfloat16)
         return carry
 
     lax.fori_loop(0, seqs // slots, narrow, 0)
@@ -305,9 +317,9 @@
             jax.ShapeDtypeStruct((1, lanes), jnp.float32),
         ],
         scratch_shapes=[
-            pltpu.VMEM((seqs, piece), jnp.float32),
+            pltpu.VMEM((seqs, piece // lanes, lanes), jnp.float32),
             pltpu.VMEM(((blocks + window) * pairs, piece), jnp.float32),
-            pltpu.VMEM((pairs, piece), jnp.float32),
+            pltpu.VMEM((pairs, piece // lanes, lanes), jnp.float32),
         ],
         compiler_params=pltpu.CompilerParams(vmem_limit_bytes=vmem_limit),
         name="slice_grads",

time: 328 us -> 318 us (0.970)
  Pallas kernels: 79.1 us -> 69.8 us
    pallas_call x1, Pallas kernels: 33.1 us -> 28 us  [grad_call(): pl.pallas_call(functools.partial(grad_kernel, blocks, pairs, window), in_...]
    pallas_call x1, Pallas kernels: 29.8 us -> 25.5 us  [score_call(): pl.pallas_call(functools.partial(score_kernel, blocks, pairs, window), in...]
where the time goes in v3:
time: 318 us
  waiting for transfers between devices  120 us (38%)
  blocking collectives  112 us (35%)
  Pallas kernels  69.8 us (22%)
  between operations  14 us (4%)
    reduce_scatter x1, waiting for transfers between devices, feature_plan(): lax.psum_scatter(partial_scores, 'pb', scatter_dimension=0, tiled=False)  75.7 us
    all_to_all x1, blocking collectives, feature_plan(): lax.all_to_all(embedding, 'pb', split_axis=0, concat_axis=0, tiled=True)  59.3 us
    all_to_all x1, blocking collectives, feature_plan(): lax.all_to_all(grads, 'pb', split_axis=0, concat_axis=0, tiled=True)  52.2 us
    all_gather x1, waiting for transfers between devices, feature_plan(): shared = lax.all_gather(coefficients, 'pb', axis=0, tiled=False)  44.1 us
    pallas_call x1, Pallas kernels, grad_call(): pl.pallas_call(functools.partial(grad_kernel, blocks, pairs, window), in_...  28 us
    pallas_call x1, Pallas kernels, score_call(): pl.pallas_call(functools.partial(score_kernel, blocks, pairs, window), in...  25.5 us
    pallas_call x1, Pallas kernels, project_call(): pl.pallas_call(project_kernel, grid=(seqs // rows,), in_specs=[pl.BlockSp...  7.36 us
  transfers between devices with their start and end apart: 2, of which 2 were waited for; matrix products, arithmetic and copies ran while one was open for 0% of the time, Pallas kernels for 0%

profile of v3, /device:TPU:1, one launch (start us, length us, event | category | flops | bytes accessed | tf_op | source)
XLA Modules:
  0.0 318.0 jit_solution(8399901176512788957)
XLA Ops:
  7.2 0.0 reduce-scatter.2.cloned.1.call-start
  7.2 1.3 reshape.7.gain_ref
  8.5 1.4 copy.8.owner_ref
  9.9 5.7 %norm_rows.1 = (bf16[256,4096]{1,0:T(8,128)(2,1)}, f32[256,128]{1,0:T(8,128)}, bf16[16,272,256]{2,1,0:T(8,128)(2,1)}) custom-call(s32[1,256]{1,0:T(1,128)} %last_ref.1, bf16[256,4096]{1,0:T(8,128)(2,1)} %hidden_ref.1, bf16[1,4096]{1,0:T(2,128)(2,1)} %reshape.7.gain_ref, s32[128,2]{1,0:T(8,128)} %copy.8.owner_ref, s32[1,4]{1,0:T(1,128)} %negative_ref.1), custom_call_target="tpu_custom_call" | custom-call | tf_op jit(solution)/shard_map/norm_rows/pallas_call | solution.py:82
  15.6 59.3 %all_to_all.10.emb_ref = bf16[16,272,256]{2,1,0:T(8,128)(2,1)} all-to-all(bf16[16,272,256]{2,1,0:T(8,128)(2,1)} %get-tuple-element.12), channel_id=1, replica_groups=mesh['groups'=2,'pb'=16] {'pb'}, dimensions={0} | all-to-all | bytes 4456448 | tf_op jit(solution)/shard_map/all_to_all | solution.py:372
  74.9 25.5 %partial_scores.1 = (bf16[2048,256]{1,0:T(8,128)(2,1)}, bf16[2560,256]{1,0:T(8,128)(2,1)}, f32[16,640,128]{2,1,0:T(8,128)}, s32[16,256]{1,0:T(8,128)}, s32[16,128]{1,0:T(8,128)}) custom-call(bf16[16,272,256]{2,1,0:T(8,128)(2,1)} %all_to_all.10.emb_ref), custom_call_target="tpu_custom_call" | custom-call | tf_op jit(solution)/shard_map/partial_scores/pallas_call | solution.py:156
  100.4 0.0 reduce-scatter.2.cloned.1.call-update
  100.4 0.0 all-gather.3.cloned.1.call-start
  100.5 75.7 %reduce-scatter.2.cloned.1.call-done = f32[1,640,128]{2,1,0:T(8,128)} async-done(((f32[16,640,128]{2,1,0:T(8,128)}), f32[1,640,128]{2,1,0:T(8,128)}) %reduce-scatter.2.cloned.1.call-update) | async-done | bytes 327696 | tf_op jit(solution)/shard_map/reduce_scatter | solution.py:374
  176.2 3.2 %softmax_rows.1 = bf16[41,16,128]{2,1,0:T(8,128)(2,1)} custom-call(s32[16,128]{1,0:T(8,128)} %get-tuple-element.14.listed_ref, f32[5,16,8,128]{3,2,1,0:T(8,128)} %bitcast.5), custom_call_target="tpu_custom_call" | custom-call | tf_op jit(solution)/shard_map/softmax_rows/pallas_call | solution.py:219
  179.4 0.0 all-gather.3.cloned.1.call-update
  179.4 44.1 %all-gather.3.cloned.1.call-done = bf16[656,16,128]{2,1,0:T(8,128)(2,1)} async-done(((bf16[41,16,128]{2,1,0:T(8,128)(2,1)}), bf16[656,16,128]{2,1,0:T(8,128)(2,1)}) %all-gather.3.cloned.1.call-update) | async-done | bytes 2686992 | tf_op jit(solution)/shard_map/all_gather | solution.py:378
  223.5 28.0 %slice_grads.1 = (bf16[16,256,256]{2,1,0:T(8,128)(2,1)}, f32[1,128]{1,0:T(1,128)}) custom-call(s32[16,256]{1,0:T(8,128)} %get-tuple-element.13.own_ref, bf16[16,41,16,128]{3,2,1,0:T(8,128)(2,1)} %bitcast.4, bf16[2048,256]{1,0:T(8,128)(2,1)} %get-tuple-element.16.q_ref, bf16[2560,256]{1,0:T(8,128)(2,1)} %get-tuple-element.17.d_ref), custom_call_target="tpu_custom_call" | custom-call | tf_op jit(solution)/shard_map/slice_grads/pallas_call | solution.py:311
  251.5 52.2 %all_to_all.11.grad_ref = bf16[16,256,256]{2,1,0:T(8,128)(2,1)} all-to-all(bf16[16,256,256]{2,1,0:T(8,128)(2,1)} %get-tuple-element.18), channel_id=1, replica_groups=mesh['groups'=2,'pb'=16] {'pb'}, dimensions={0} | all-to-all | bytes 4194304 | tf_op jit(solution)/shard_map/all_to_all | solution.py:380
  303.8 7.4 %project_out.1 = f32[256,4096]{1,0:T(8,128)} custom-call(bf16[16,256,256]{2,1,0:T(8,128)(2,1)} %all_to_all.11.grad_ref, bf16[256,4096]{1,0:T(8,128)(2,1)} %get-tuple-element.19.normed_ref, f32[256,128]{1,0:T(8,128)} %get-tuple-element.20.inv_ref), custom_call_target="tpu_custom_call" | custom-call | tf_op jit(solution)/shard_map/project_out/pallas_call | solution.py:348
Async XLA Ops:
  7.2 169.0 %reduce-scatter.2.cloned.1.call-start = ((), (), s32[]{:S(2)}) async-start(), calls=%async_computation.3 | async-start | bytes 5570560 | tf_op jit(solution)/shard_map/reduce_scatter | solution.py:374
  100.4 123.1 %all-gather.3.cloned.1.call-start = ((), (), s32[]{:S(2)}) async-start(), calls=%async_computation.4 | async-start | bytes 2854912 | tf_op jit(solution)/shard_map/all_gather | solution.py:378
Sparse Core Ops, SparseCore 0:
  100.6 75.5 reduce-scatter.1
  179.6 43.8 all-gather.2

commit v4 on v3

--- a/solution.py
+++ b/solution.py
@@ -94,14 +94,33 @@
 
 
 def score_kernel(
-    blocks, pairs, window, emb_ref, q_ref, d_ref, s_ref, own_ref, listed_ref, wide, picked, own, sem
+    blocks,
+    pairs,
+    window,
+    emb_ref,
+    q_ref,
+    d_ref,
+    s_ref,
+    own_ref,
+    place_ref,
+    wide,
+    picked,
+    tiles,
+    facts,
+    own,
+    named,
+    sems,
 ):
     seqs = emb_ref.shape[1] - 16
-    facts = emb_ref[:, seqs:, :].astype(jnp.float32)
-    own_ref[...] = (facts[:, 0, :] + 256.0 * facts[:, 1, :]).astype(jnp.int32)
-    listed_ref[...] = facts[:, 2, :lanes].astype(jnp.int32)
-    fetch = pltpu.make_async_copy(own_ref, own, sem)
-    fetch.start()
+    sent = emb_ref[:, seqs:, :].astype(jnp.float32)
+    own_ref[...] = (sent[:, 0, :] + 256.0 * sent[:, 1, :]).astype(jnp.int32)
+    facts[...] = sent[:, 2, :lanes].astype(jnp.int32)
+    fetches = [
+        pltpu.make_async_copy(own_ref, own, sems.at[0]),
+        pltpu.make_async_copy(facts, named, sems.at[1]),
+    ]
+    for fetch in fetches:
+        fetch.start()
 
     def widen(step, carry):
         at = pl.multiple_of(step * seqs, seqs)
@@ -109,7 +128,18 @@
         return carry
 
     lax.fori_loop(0, emb_ref.shape[0], widen, 0)
-    fetch.wait()
+    for fetch in fetches:
+        fetch.wait()
+
+    def place(block, count):
+        place_ref[0, block] = block
+        for offset in range(window):
+            present = named[block, offset] > 0
+            place_ref[offset + 1, block] = jnp.where(present, count, -1)
+            count = count + present.astype(jnp.int32)
+        return count
+
+    lax.fori_loop(0, blocks, place, blocks)
     unroll = 16
 
     def pick_block(block, carry):
@@ -131,166 +161,203 @@
     groups = s_ref.shape[0]
     fine = pairs // groups
 
-    def score_block(block, carry):
-        at = pl.multiple_of(block * pairs, pairs)
-        tiles = inverse_temp * lax.dot_general(
-            q_ref[pl.ds(at, pairs), :],
-            d_ref[pl.ds(at, (window + 1) * pairs), :],
+    def score_blocks(step, carry):
+        at = pl.multiple_of(step * 2 * pairs, 2 * pairs)
+        tiles[...] = inverse_temp * lax.dot_general(
+            q_ref[pl.ds(at, 2 * pairs), :],
+            d_ref[pl.ds(at, (window + 2) * pairs), :],
             (((1,), (1,)), ((), ())),
             preferred_element_type=jnp.float32,
         )
-        for column in range(window + 1):
-            row = pl.multiple_of((column * blocks + block) * fine, fine)
-            tile = tiles[:, column * pairs : (column + 1) * pairs]
-            s_ref[:, pl.ds(row, fine), :] = tile.reshape(groups, fine, pairs)
+        for half in range(2):
+            for column in range(window + 1):
+                spot = place_ref[column, 2 * step + half]
+
+                @pl.when(spot >= 0)
+                def _():
+                    row = pl.multiple_of(spot * fine, fine)
+                    tile = tiles[
+                        half * pairs : (half + 1) * pairs,
+                        (half + column) * pairs : (half + column + 1) * pairs,
+                    ]
+                    s_ref[:, pl.ds(row, fine), :] = tile.reshape(groups, fine, pairs)
+
         return carry
 
-    lax.fori_loop(0, blocks, score_block, 0)
-
-
-def score_call(embedded, blocks, pairs, window):
+    lax.fori_loop(0, blocks // 2, score_blocks, 0)
+
+
+def score_call(embedded, room, blocks, pairs, window):
     parts, rows, piece = embedded.shape
     fine = pairs // blocks
-    tiles = blocks * (window + 1)
     whole = pl.BlockSpec(memory_space=pltpu.VMEM)
+    scalars = pl.BlockSpec(memory_space=pltpu.SMEM)
     return pl.pallas_call(
         functools.partial(score_kernel, blocks, pairs, window),
         in_specs=[whole],
-        out_specs=[whole] * 5,
+        out_specs=[whole, whole, whole, whole, scalars],
         out_shape=[
             jax.ShapeDtypeStruct((blocks * pairs, piece), jnp.bfloat16),
             jax.ShapeDtypeStruct(((blocks + window) * pairs, piece), jnp.bfloat16),
-            jax.ShapeDtypeStruct((blocks, tiles * fine, pairs), jnp.float32),
+            jax.ShapeDtypeStruct((blocks, room * fine, pairs), jnp.float32),
             jax.ShapeDtypeStruct((blocks, 2 * pairs), jnp.int32),
-            jax.ShapeDtypeStruct((blocks, lanes), jnp.int32),
+            jax.ShapeDtypeStruct((window + 1, blocks), jnp.int32),
         ],
         scratch_shapes=[
             pltpu.VMEM((parts * (rows - 16), piece // lanes, lanes), jnp.float32),
             pltpu.VMEM((2 * pairs, piece // lanes, lanes), jnp.float32),
+            pltpu.VMEM((2 * pairs, (window + 2) * pairs), jnp.float32),
+            pltpu.VMEM((blocks, lanes), jnp.int32),
             pltpu.SMEM((blocks, 2 * pairs), jnp.int32),
-            pltpu.SemaphoreType.DMA,
+            pltpu.SMEM((blocks, lanes), jnp.int32),
+            pltpu.SemaphoreType.DMA((2,)),
         ],
         compiler_params=pltpu.CompilerParams(vmem_limit_bytes=vmem_limit),
         name="partial_scores",
     )(embedded)
 
 
-def softmax_kernel(blocks, window, listed_ref, s_ref, c_ref):
-    fine = s_ref.shape[2]
-    pairs = s_ref.shape[3]
-    first = lax.axis_index("pb") * fine
-    rows = lax.broadcasted_iota(jnp.int32, (fine, pairs), 0) + first
-    target = lax.broadcasted_iota(jnp.int32, (fine, pairs), 1) == rows
-    lane = lax.broadcasted_iota(jnp.int32, (16, pairs), 1)
-
-    def one_block(block, losses):
-        tiles = [s_ref[0, block]]
-        for offset in range(window):
-            named = listed_ref[block, offset] > 0
-            tiles.append(jnp.where(named, s_ref[offset + 1, block], -jnp.inf))
-        top = functools.reduce(jnp.maximum, tiles)
-        row_max = jnp.max(top, axis=1, keepdims=True)
-        total = functools.reduce(jnp.add, [jnp.exp(tile - row_max) for tile in tiles])
-        log_total = row_max + jnp.log(jnp.sum(total, axis=1, keepdims=True))
-        positive = jnp.sum(jnp.where(target, tiles[0], 0.0), axis=1, keepdims=True)
-        loss = jnp.sum(log_total - positive, axis=0, keepdims=True)
-        shares = [jnp.exp(tile - log_total) for tile in tiles]
-        shares[0] = shares[0] - jnp.where(target, 1.0, 0.0)
-        return [inverse_temp * share for share in shares], jnp.where(lane == block, loss, losses)
-
-    def two_blocks(step, losses):
-        even, losses = one_block(2 * step, losses)
-        odd, losses = one_block(2 * step + 1, losses)
+def softmax_kernel(blocks, window, place_ref, s_ref, c_ref, packed, masked):
+    fine, pairs = s_ref.shape[1:]
+    count = blocks * fine
+    for block in range(blocks):
         for column in range(window + 1):
-            both = jnp.concatenate([even[column], odd[column]], axis=0)
-            c_ref[column * (blocks // 2) + step] = both.astype(jnp.bfloat16)
-        return losses
-
-    losses = lax.fori_loop(0, blocks // 2, two_blocks, jnp.zeros((16, pairs), jnp.float32))
+            spot = place_ref[column, block]
+            tile = s_ref[jnp.maximum(spot, 0)]
+            masked[block * fine : (block + 1) * fine, column * pairs : (column + 1) * pairs] = (
+                jnp.where(spot >= 0, tile, -jnp.inf)
+            )
+    row = lax.broadcasted_iota(jnp.int32, (count, pairs), 0)
+    lane = lax.broadcasted_iota(jnp.int32, (count, pairs), 1)
+    target = lane == lax.axis_index("pb") * fine + row % fine
+    pieces = [masked[:, column * pairs : (column + 1) * pairs] for column in range(window + 1)]
+    row_max = jnp.max(functools.reduce(jnp.maximum, pieces), axis=1, keepdims=True)
+    total = functools.reduce(jnp.add, [jnp.exp(piece - row_max) for piece in pieces])
+    log_total = row_max + jnp.log(jnp.sum(total, axis=1, keepdims=True))
+    positive = jnp.sum(jnp.where(target, pieces[0], 0.0), axis=1, keepdims=True)
+    for column, piece in enumerate(pieces):
+        share = jnp.exp(piece - log_total)
+        if column == 0:
+            share = share - jnp.where(target, 1.0, 0.0)
+        masked[:, column * pairs : (column + 1) * pairs] = inverse_temp * share
+    for block in range(blocks):
+        for column in range(window + 1):
+            spot = place_ref[column, block]
+
+            @pl.when(spot >= 0)
+            def _():
+                packed[spot] = masked[
+                    block * fine : (block + 1) * fine, column * pairs : (column + 1) * pairs
+                ]
+
+    room = packed.shape[0]
+    for step in range(room // 2):
+        both = jnp.concatenate([packed[2 * step], packed[2 * step + 1]], axis=0)
+        c_ref[step] = both.astype(jnp.bfloat16)
+    losses = jnp.sum(
+        jnp.where(lane == row // fine, log_total - positive, 0.0), axis=0, keepdims=True
+    )
     coarse = losses.astype(jnp.bfloat16).astype(jnp.float32)
-    rank = lax.broadcasted_iota(jnp.int32, (16, pairs), 0)
+    rank = lax.broadcasted_iota(jnp.int32, (2 * fine, pairs), 0)
     both = jnp.where(rank == 0, coarse, jnp.where(rank == 1, losses - coarse, 0.0))
-    c_ref[(window + 1) * (blocks // 2)] = both.astype(jnp.bfloat16)
-
-
-def softmax_call(listed, scores, blocks, window):
-    fine, pairs = scores.shape[2:]
+    c_ref[room // 2] = both.astype(jnp.bfloat16)
+
+
+def softmax_call(place, scores, blocks, window):
+    room, fine, pairs = scores.shape
     whole = pl.BlockSpec(memory_space=pltpu.VMEM)
     return pl.pallas_call(
         functools.partial(softmax_kernel, blocks, window),
         in_specs=[pl.BlockSpec(memory_space=pltpu.SMEM), whole],
         out_specs=whole,
-        out_shape=jax.ShapeDtypeStruct(
-            ((window + 1) * blocks // 2 + 1, 2 * fine, pairs), jnp.bfloat16
-        ),
+        out_shape=jax.ShapeDtypeStruct((room // 2 + 1, 2 * fine, pairs), jnp.bfloat16),
+        scratch_shapes=[
+            pltpu.VMEM((room, fine, pairs), jnp.float32),
+            pltpu.VMEM((blocks * fine, (window + 1) * pairs), jnp.float32),
+        ],
         compiler_params=pltpu.CompilerParams(vmem_limit_bytes=vmem_limit),
         name="softmax_rows",
-    )(listed, scores)
+    )(place, scores)
 
 
 def grad_kernel(
-    blocks, pairs, window, own_ref, c_ref, q_ref, d_ref, out_ref, loss_ref, wide, dsum, picked
+    blocks,
+    pairs,
+    window,
+    own_ref,
+    place_ref,
+    c_ref,
+    q_ref,
+    d_ref,
+    out_ref,
+    loss_ref,
+    wide,
+    dsum,
+    picked,
+    packed,
+    square,
 ):
     fine = pairs // blocks
     seqs = wide.shape[0]
+    room = packed.shape[1]
     unroll = 16
-    half_blocks = blocks // 2
-    coarse = c_ref[:, (window + 1) * half_blocks].astype(jnp.float32)
-    losses = jnp.sum(coarse[:, 0, :] + coarse[:, 1, :], axis=0, keepdims=True) / pairs
+    sent = c_ref[:, room // 2].astype(jnp.float32)
+    losses = jnp.sum(sent[:, 0, :] + sent[:, 1, :], axis=0, keepdims=True) / pairs
     lane = lax.broadcasted_iota(jnp.int32, losses.shape, 1)
     mine = jnp.where(lane == lax.axis_index("pb"), losses, 0.0)
     loss_ref[...] = jnp.broadcast_to(jnp.sum(mine, axis=1, keepdims=True), loss_ref.shape)
     dsum[...] = jnp.zeros_like(dsum)
-
-    def scatter_rows(block, offset):
+    square[...] = jnp.zeros_like(square)
+
+    def unpack(step, carry):
+        both = c_ref[:, step].astype(jnp.float32)
+        packed[:, 2 * step] = both[:, :fine]
+        packed[:, 2 * step + 1] = both[:, fine:]
+        return carry
+
+    lax.fori_loop(0, room // 2, unpack, 0)
+
+    def scatter_rows(block, offset, start):
         def step_rows(step, inner):
             base = pl.multiple_of(step * unroll, unroll)
-            rows = [picked[base + k] for k in range(unroll)]
+            rows = [picked[start + base + k] for k in range(unroll)]
             for k in range(unroll):
                 wide[own_ref[block, offset + base + k]] = rows[k]
             return inner
 
         lax.fori_loop(0, pairs // unroll, step_rows, 0)
 
-    def one_block(block, coefficients):
-        at = pl.multiple_of(block * pairs, pairs)
-        summed = jnp.dot(
+    def two_blocks(step, carry):
+        for half in range(2):
+            for column in range(window + 1):
+                spot = place_ref[column, 2 * step + half]
+                tile = packed[:, jnp.maximum(spot, 0)].reshape(pairs, pairs)
+                square[
+                    half * pairs : (half + 1) * pairs,
+                    (half + column) * pairs : (half + column + 1) * pairs,
+                ] = jnp.where(spot >= 0, tile, 0.0).astype(jnp.bfloat16)
+        at = pl.multiple_of(step * 2 * pairs, 2 * pairs)
+        there = pl.ds(at, (window + 2) * pairs)
+        coefficients = square[...]
+        summed = jnp.dot(coefficients, d_ref[there, :], preferred_element_type=jnp.float32)
+        spread(picked, 0, summed)
+        dsum[there, :] += lax.dot_general(
             coefficients,
-            d_ref[pl.ds(at, (window + 1) * pairs), :],
-            preferred_element_type=jnp.float32,
-        )
-        spread(picked, 0, summed)
-        scatter_rows(block, 0)
-        dsum[pl.ds(at, (window + 1) * pairs), :] += lax.dot_general(
-            coefficients,
-            q_ref[pl.ds(at, pairs), :],
+            q_ref[pl.ds(at, 2 * pairs), :],
             (((0,), (0,)), ((), ())),
             preferred_element_type=jnp.float32,
         )
-
-    def two_blocks(step, carry):
-        pieces = [
-            c_ref[:, column * half_blocks + step].astype(jnp.float32)
-            for column in range(window + 1)
-        ]
         for half in range(2):
-            coefficients = jnp.concatenate(
-                [
-                    piece[:, half * fine : (half + 1) * fine].reshape(pairs, pairs)
-                    for piece in pieces
-                ],
-                axis=1,
-            ).astype(jnp.bfloat16)
-            one_block(2 * step + half, coefficients)
+            scatter_rows(2 * step + half, 0, half * pairs)
         return carry
 
-    lax.fori_loop(0, half_blocks, two_blocks, 0)
+    lax.fori_loop(0, blocks // 2, two_blocks, 0)
     dsum[: window * pairs, :] += dsum[blocks * pairs :, :]
 
     def doc_block(block, carry):
         at = pl.multiple_of(block * pairs, pairs)
         spread(picked, 0, dsum[pl.ds(at, pairs), :])
-        scatter_rows(block, pairs)
+        scatter_rows(block, pairs, 0)
         return carry
 
     lax.fori_loop(0, blocks, doc_block, 0)
@@ -304,13 +371,15 @@
     lax.fori_loop(0, seqs // slots, narrow, 0)
 
 
-def grad_call(own, coefficients, queries, documents, blocks, pairs, window):
+def grad_call(own, place, coefficients, queries, documents, blocks, pairs, window):
     count, piece = queries.shape
     seqs = 2 * count
+    room = 2 * (coefficients.shape[1] - 1)
     whole = pl.BlockSpec(memory_space=pltpu.VMEM)
+    scalars = pl.BlockSpec(memory_space=pltpu.SMEM)
     return pl.pallas_call(
         functools.partial(grad_kernel, blocks, pairs, window),
-        in_specs=[pl.BlockSpec(memory_space=pltpu.SMEM), whole, whole, whole],
+        in_specs=[scalars, scalars, whole, whole, whole],
         out_specs=[whole, whole],
         out_shape=[
             jax.ShapeDtypeStruct((blocks, seqs // blocks, piece), jnp.bfloat16),
@@ -319,11 +388,13 @@
         scratch_shapes=[
             pltpu.VMEM((seqs, piece // lanes, lanes), jnp.float32),
             pltpu.VMEM(((blocks + window) * pairs, piece), jnp.float32),
-            pltpu.VMEM((pairs, piece // lanes, lanes), jnp.float32),
+            pltpu.VMEM((2 * pairs, piece // lanes, lanes), jnp.float32),
+            pltpu.VMEM((blocks, room, pairs // blocks, pairs), jnp.float32),
+            pltpu.VMEM((2 * pairs, (window + 2) * pairs), jnp.bfloat16),
         ],
         compiler_params=pltpu.CompilerParams(vmem_limit_bytes=vmem_limit),
         name="slice_grads",
-    )(own, coefficients, queries, documents)
+    )(own, place, coefficients, queries, documents)
 
 
 def project_kernel(grad_ref, normed_ref, inv_ref, out_ref):
@@ -360,25 +431,41 @@
     )(returned, normed, inverse)
 
 
+def middle(embedded, room, devices, pairs, window):
+    fine = pairs // devices
+    queries, documents, partial_scores, own, place = score_call(
+        embedded, room, devices, pairs, window
+    )
+    scores = lax.psum_scatter(partial_scores, "pb", scatter_dimension=0, tiled=False)
+    coefficients = softmax_call(place, scores.reshape(room, fine, pairs), devices, window)
+    shared = lax.all_gather(coefficients, "pb", axis=0, tiled=False)
+    grads, loss = grad_call(own, place, shared, queries, documents, devices, pairs, window)
+    return grads, loss[0, :1]
+
+
 def feature_plan(hidden, final_gain, last_row, pair_owner, hard_negatives):
     devices = lax.axis_size("pb")
-    width = hidden.shape[1]
+    seqs, width = hidden.shape
     pairs = pair_owner.shape[0]
     window = hard_negatives.shape[1]
-    fine = pairs // devices
     normed, inverse, embedding = norm_call(
         last_row, hidden, final_gain.reshape(1, width), pair_owner, hard_negatives, devices
     )
     embedded = lax.all_to_all(embedding, "pb", split_axis=0, concat_axis=0, tiled=True)
-    queries, documents, partial_scores, own, listed = score_call(embedded, devices, pairs, window)
-    scores = lax.psum_scatter(partial_scores, "pb", scatter_dimension=0, tiled=False)
-    coefficients = softmax_call(
-        listed, scores.reshape(window + 1, devices, fine, pairs), devices, window
-    )
-    shared = lax.all_gather(coefficients, "pb", axis=0, tiled=False)
-    grads, loss = grad_call(own, shared, queries, documents, devices, pairs, window)
+    most = devices * (window + 1)
+    rooms = [most * part // 20 for part in (10, 11, 12, 13, 14, 16, 20)]
+    used = devices + jnp.sum(embedded[:, seqs + 2, :window].astype(jnp.float32))
+    level = sum((used > room).astype(jnp.int32) for room in rooms[:-1])
+    grads, loss = lax.switch(
+        level,
+        [
+            functools.partial(middle, room=room, devices=devices, pairs=pairs, window=window)
+            for room in rooms
+        ],
+        embedded,
+    )
     returned = lax.all_to_all(grads, "pb", split_axis=0, concat_axis=0, tiled=True)
-    return project_call(returned, normed, inverse), loss[0, :1]
+    return project_call(returned, normed, inverse), loss
 
 
 def from_behind(value, axis, steps):

time: 318 us -> 295 us (0.928)
  waiting for transfers between devices: 120 us -> 104 us
  Pallas kernels: 69.8 us -> 61.6 us
    reduce_scatter x1, waiting for transfers between devices: 75.7 us -> 63.1 us  [middle(): lax.psum_scatter(partial_scores, 'pb', scatter_dimension=0, tiled=False)]
    pallas_call x1, Pallas kernels: 28 us -> 23 us  [grad_call(): pl.pallas_call(functools.partial(grad_kernel, blocks, pairs, window), in_...]
where the time goes in v4:
time: 295 us; the launch traced here: 294 us
  blocking collectives  110 us (37%)
  waiting for transfers between devices  104 us (35%)
  Pallas kernels  61.6 us (21%)
  between operations  14.7 us (5%)
    reduce_scatter x1, waiting for transfers between devices, middle(): lax.psum_scatter(partial_scores, 'pb', scatter_dimension=0, tiled=False)  63.1 us
    all_to_all x1, blocking collectives, feature_plan(): lax.all_to_all(embedding, 'pb', split_axis=0, concat_axis=0, tiled=True)  59.2 us
    all_to_all x1, blocking collectives, feature_plan(): lax.all_to_all(grads, 'pb', split_axis=0, concat_axis=0, tiled=True)  51.3 us
    all_gather x1, waiting for transfers between devices, middle(): shared = lax.all_gather(coefficients, 'pb', axis=0, tiled=False)  40.9 us
    pallas_call x1, Pallas kernels, grad_call(): pl.pallas_call(functools.partial(grad_kernel, blocks, pairs, window), in_...  23 us
    pallas_call x1, Pallas kernels, score_call(): pl.pallas_call(functools.partial(score_kernel, blocks, pairs, window), in...  23 us
    pallas_call x1, Pallas kernels, project_call(): pl.pallas_call(project_kernel, grid=(seqs // rows,), in_specs=[pl.BlockSp...  7.36 us
  transfers between devices with their start and end apart: 2, of which 2 were waited for; matrix products, arithmetic and copies ran while one was open for 0% of the time, Pallas kernels for 0%

profile of v4, /device:TPU:1, one launch (start us, length us, event | category | flops | bytes accessed | tf_op | source)
XLA Modules:
  0.0 294.2 jit_solution(17616341897040220217)
XLA Ops:
  7.2 1.3 reshape.8.gain_ref
  8.5 1.4 copy.8.owner_ref
  9.9 5.7 %norm_rows.1 = (bf16[256,4096]{1,0:T(8,128)(2,1)}, f32[256,128]{1,0:T(8,128)}, bf16[16,272,256]{2,1,0:T(8,128)(2,1)}) custom-call(s32[1,256]{1,0:T(1,128)} %last_ref.1, bf16[256,4096]{1,0:T(8,128)(2,1)} %hidden_ref.1, bf16[1,4096]{1,0:T(2,128)(2,1)} %reshape.8.gain_ref, s32[128,2]{1,0:T(8,128)} %copy.8.owner_ref, s32[1,4]{1,0:T(1,128)} %negative_ref.1), custom_call_target="tpu_custom_call" | custom-call | tf_op jit(solution)/shard_map/norm_rows/pallas_call | solution.py:82
  15.6 59.2 %all_to_all.31 = bf16[16,272,256]{2,1,0:T(8,128)(2,1)S(1)} all-to-all(bf16[16,272,256]{2,1,0:T(8,128)(2,1)} %get-tuple-element.63), channel_id=1, replica_groups=mesh['groups'=2,'pb'=16] {'pb'}, dimensions={0} | all-to-all | bytes 4456448 | tf_op jit(solution)/shard_map/all_to_all | solution.py:454
  74.8 0.6 fusion
  76.1 152.7 %conditional.1 = (bf16[16,256,256]{2,1,0:T(8,128)(2,1)S(1)}, f32[1]{0:T(128)}) conditional(s32[]{:T(128)} %clamp.3, bf16[16,272,256]{2,1,0:T(8,128)(2,1)S(1)} %all_to_all.31, bf16[16,272,256]{2,1,0:T(8,128)(2,1)S(1)} %all_to_all.31, bf16[16,272,256]{2,1,0:T(8,128)(2,1)S(1)} %all_to_all.31, ...), branch_computations={%region_1.0_spmd, %region_3.0_spmd, %region_5.0_spmd, %region_7.0_... | conditional | bytes 25276512 | solution.py:459
  76.1 0.0 reduce-scatter.10.cloned.1.call-start
  76.1 23.0 %partial_scores.8 = (bf16[2048,256]{1,0:T(8,128)(2,1)}, bf16[2560,256]{1,0:T(8,128)(2,1)}, f32[16,352,128]{2,1,0:T(8,128)}, s32[16,256]{1,0:T(8,128)}, s32[5,16]{1,0:T(8,128)}) custom-call(bf16[16,272,256]{2,1,0:T(8,128)(2,1)S(1)} %emb_ref.1), custom_call_target="tpu_custom_call" | custom-call | tf_op jit(solution)/shard_map/cond/branch_1_fun/partial_scores/pallas_call | solution.py:195
  99.1 0.0 reduce-scatter.10.cloned.1.call-update
  99.2 0.0 all-gather.17.cloned.1.call-start
  99.2 63.1 %reduce-scatter.10.cloned.1.call-done = f32[1,352,128]{2,1,0:T(8,128)} async-done(((f32[16,352,128]{2,1,0:T(8,128)}), f32[1,352,128]{2,1,0:T(8,128)}) %reduce-scatter.10.cloned.1.call-update) | async-done | bytes 180240 | tf_op jit(solution)/shard_map/cond/branch_1_fun/reduce_scatter | solution.py:439
  162.3 2.5 softmax_rows.8
  164.8 0.0 all-gather.17.cloned.1.call-update
  164.9 40.9 %all-gather.17.cloned.1.call-done = bf16[368,16,128]{2,1,0:T(8,128)(2,1)} async-done(((bf16[23,16,128]{2,1,0:T(8,128)(2,1)}), bf16[368,16,128]{2,1,0:T(8,128)(2,1)}) %all-gather.17.cloned.1.call-update) | async-done | bytes 1507344 | tf_op jit(solution)/shard_map/cond/branch_1_fun/all_gather | solution.py:441
  205.8 23.0 %slice_grads.8 = (bf16[16,256,256]{2,1,0:T(8,128)(2,1)S(1)}, f32[1,128]{1,0:T(1,128)}) custom-call(s32[16,256]{1,0:T(8,128)} %get-tuple-element.14.own_ref, s32[5,16]{1,0:T(8,128)} %get-tuple-element.15.place_ref, bf16[16,23,16,128]{3,2,1,0:T(8,128)(2,1)} %bitcast.33, bf16[2048,256]{1,0:T(8,128)(2,1)} %get-tuple-element.17.q_ref, ...), custom_call_target="tpu_custom_call" | custom-call | tf_op jit(solution)/shard_map/cond/branch_1_fun/slice_grads/pallas_call | solution.py:380
  228.8 51.3 %all_to_all.32.grad_ref = bf16[16,256,256]{2,1,0:T(8,128)(2,1)} all-to-all(bf16[16,256,256]{2,1,0:T(8,128)(2,1)S(1)} %get-tuple-element.64), channel_id=1, replica_groups=mesh['groups'=2,'pb'=16] {'pb'}, dimensions={0} | all-to-all | bytes 4194304 | tf_op jit(solution)/shard_map/all_to_all | solution.py:467
  280.0 7.4 %project_out.1 = f32[256,4096]{1,0:T(8,128)} custom-call(bf16[16,256,256]{2,1,0:T(8,128)(2,1)} %all_to_all.32.grad_ref, bf16[256,4096]{1,0:T(8,128)(2,1)} %get-tuple-element.65.normed_ref, f32[256,128]{1,0:T(8,128)} %get-tuple-element.66.inv_ref), custom_call_target="tpu_custom_call" | custom-call | tf_op jit(solution)/shard_map/project_out/pallas_call | solution.py:419
Async XLA Ops:
  76.1 86.2 %reduce-scatter.10.cloned.1.call-start = ((), (), s32[]{:S(2)}) async-start(), calls=%async_computation.11 | async-start | bytes 3063808 | tf_op jit(solution)/shard_map/cond/branch_1_fun/reduce_scatter | solution.py:439
  99.2 106.6 %all-gather.17.cloned.1.call-start = ((), (), s32[]{:S(2)}) async-start(), calls=%async_computation.12 | async-start | bytes 1601536 | tf_op jit(solution)/shard_map/cond/branch_1_fun/all_gather | solution.py:441
Sparse Core Ops, SparseCore 0:
  99.3 62.9 reduce-scatter.9
  165.3 40.4 all-gather.16

commit v5 on v4

--- a/solution.py
+++ b/solution.py
@@ -11,6 +11,8 @@
 token_eps = 1e-05
 unit_eps = 1e-06
 lanes = 128
+bound_steps = 256.0
+code_steps = 32000.0
 vmem_limit = 56 * 1024 * 1024
 
 
@@ -28,7 +30,7 @@
 def norm_kernel(last_ref, hidden_ref, gain_ref, owner_ref, negative_ref, normed_ref, inv_ref, emb_ref):
     seqs, width = normed_ref.shape
     parts, _, piece = emb_ref.shape
-    pairs = owner_ref.shape[0]
+    pairs = owner_ref.shape[1]
     cuts = [slice(part * piece, (part + 1) * piece) for part in range(parts)]
     sources = lax.broadcasted_iota(jnp.int32, (seqs, seqs), 0)
     pick = jnp.where(sources == last_ref[...], 1.0, 0.0).astype(jnp.bfloat16)
@@ -49,20 +51,19 @@
     total = jnp.zeros((seqs, lanes), jnp.float32)
     for cut in cuts:
         values = normed_ref[:, cut].astype(jnp.float32)
-        normed = (values * scale * gain_ref[:, cut].astype(jnp.float32)).astype(jnp.bfloat16)
+        gain = gain_ref[cut].astype(jnp.float32).reshape(1, piece)
+        normed = (values * scale * gain).astype(jnp.bfloat16)
         normed_ref[:, cut] = normed
         pooled = normed.astype(jnp.float32)
         total = total + folded(pooled * pooled)
     inverse = lax.rsqrt(jnp.sum(total, axis=-1, keepdims=True) + unit_eps)
     inv_ref[...] = jnp.broadcast_to(inverse, inv_ref.shape)
 
-    lane = lax.broadcasted_iota(jnp.int32, (pairs, lanes), 1)
-    columns = jnp.where(lane == 0, owner_ref[:, :1], jnp.where(lane == 1, owner_ref[:, 1:], 0))
-    owners = columns.astype(jnp.float32).T
+    owners = owner_ref[...].astype(jnp.float32)
     high = jnp.floor(owners * (1.0 / 256.0))
     low = owners - 256.0 * high
-    row = lax.broadcasted_iota(jnp.int32, (16, lanes), 0)
-    spot = lax.broadcasted_iota(jnp.int32, (16, lanes), 1)
+    row = lax.broadcasted_iota(jnp.int32, (16, pairs), 0)
+    spot = lax.broadcasted_iota(jnp.int32, (16, pairs), 1)
     left = jnp.where(row == 0, low[:1], jnp.where(row == 1, high[:1], 0.0))
     right = jnp.where(row == 0, low[1:2], jnp.where(row == 1, high[1:2], 0.0))
     for offset in range(negative_ref.shape[1]):
@@ -75,7 +76,7 @@
         emb_ref[part, seqs:] = facts
 
 
-def norm_call(last_row, hidden, gain_row, pair_owner, hard_negatives, parts):
+def norm_call(last_row, hidden, gain, owners, hard_negatives, parts):
     seqs, width = hidden.shape
     piece = width // parts
     whole = pl.BlockSpec(memory_space=pltpu.VMEM)
@@ -90,7 +91,7 @@
         ],
         compiler_params=pltpu.CompilerParams(vmem_limit_bytes=vmem_limit),
         name="norm_rows",
-    )(last_row, hidden, gain_row, pair_owner, hard_negatives)
+    )(last_row, hidden, gain, owners, hard_negatives)
 
 
 def score_kernel(
@@ -109,6 +110,7 @@
     facts,
     own,
     named,
+    sums,
     sems,
 ):
     seqs = emb_ref.shape[1] - 16
@@ -161,7 +163,7 @@
     groups = s_ref.shape[0]
     fine = pairs // groups
 
-    def score_blocks(step, carry):
+    def score_blocks(step, top):
         at = pl.multiple_of(step * 2 * pairs, 2 * pairs)
         tiles[...] = inverse_temp * lax.dot_general(
             q_ref[pl.ds(at, 2 * pairs), :],
@@ -180,11 +182,29 @@
                         half * pairs : (half + 1) * pairs,
                         (half + column) * pairs : (half + column + 1) * pairs,
                     ]
-                    s_ref[:, pl.ds(row, fine), :] = tile.reshape(groups, fine, pairs)
-
-        return carry
-
-    lax.fori_loop(0, blocks // 2, score_blocks, 0)
+                    sums[:, pl.ds(row, fine), :] = tile.reshape(groups, fine, pairs)
+
+        used = tiles[...]
+        for at in range(0, used.shape[1], pairs):
+            size = jnp.abs(used[:, at : at + pairs]).reshape(-1, fine, pairs)
+            top = jnp.maximum(top, jnp.max(size, axis=0))
+        return top
+
+    top = lax.fori_loop(0, blocks // 2, score_blocks, jnp.zeros((fine, pairs), jnp.float32))
+    top = jnp.max(jnp.max(top, axis=1, keepdims=True), axis=0, keepdims=True)
+    bound = jnp.ceil(top * bound_steps) + 1.0
+    scale = code_steps * bound_steps / bound
+    room = s_ref.shape[1] - 1
+
+    def encode(step, carry):
+        at = pl.multiple_of(step * 2 * fine, 2 * fine)
+        codes = jnp.round(sums[:, pl.ds(at, 2 * fine), :] * scale)
+        s_ref[:, step] = codes.astype(jnp.int32).astype(jnp.int16)
+        return carry
+
+    lax.fori_loop(0, room, encode, 0)
+    sent_bound = jnp.broadcast_to(bound, (groups * 2 * fine, pairs)).astype(jnp.int32)
+    s_ref[:, room] = sent_bound.astype(jnp.int16).reshape(groups, 2 * fine, pairs)
 
 
 def score_call(embedded, room, blocks, pairs, window):
@@ -199,7 +219,7 @@
         out_shape=[
             jax.ShapeDtypeStruct((blocks * pairs, piece), jnp.bfloat16),
             jax.ShapeDtypeStruct(((blocks + window) * pairs, piece), jnp.bfloat16),
-            jax.ShapeDtypeStruct((blocks, room * fine, pairs), jnp.float32),
+            jax.ShapeDtypeStruct((blocks, room // 2 + 1, 2 * fine, pairs), jnp.int16),
             jax.ShapeDtypeStruct((blocks, 2 * pairs), jnp.int32),
             jax.ShapeDtypeStruct((window + 1, blocks), jnp.int32),
         ],
@@ -210,6 +230,7 @@
             pltpu.VMEM((blocks, lanes), jnp.int32),
             pltpu.SMEM((blocks, 2 * pairs), jnp.int32),
             pltpu.SMEM((blocks, lanes), jnp.int32),
+            pltpu.VMEM((blocks, room * fine, pairs), jnp.float32),
             pltpu.SemaphoreType.DMA((2,)),
         ],
         compiler_params=pltpu.CompilerParams(vmem_limit_bytes=vmem_limit),
@@ -218,12 +239,23 @@
 
 
 def softmax_kernel(blocks, window, place_ref, s_ref, c_ref, packed, masked):
-    fine, pairs = s_ref.shape[1:]
+    room, fine, pairs = packed.shape
     count = blocks * fine
+    bound = s_ref[:, room // 2].astype(jnp.int32).astype(jnp.float32)
+    scale = bound * (1.0 / (code_steps * bound_steps))
+
+    def decode(step, carry):
+        codes = s_ref[:, step].astype(jnp.int32).astype(jnp.float32)
+        both = jnp.sum(codes * scale, axis=0)
+        packed[2 * step] = both[:fine]
+        packed[2 * step + 1] = both[fine:]
+        return carry
+
+    lax.fori_loop(0, room // 2, decode, 0)
     for block in range(blocks):
         for column in range(window + 1):
             spot = place_ref[column, block]
-            tile = s_ref[jnp.maximum(spot, 0)]
+            tile = packed[jnp.maximum(spot, 0)]
             masked[block * fine : (block + 1) * fine, column * pairs : (column + 1) * pairs] = (
                 jnp.where(spot >= 0, tile, -jnp.inf)
             )
@@ -250,7 +282,6 @@
                     block * fine : (block + 1) * fine, column * pairs : (column + 1) * pairs
                 ]
 
-    room = packed.shape[0]
     for step in range(room // 2):
         both = jnp.concatenate([packed[2 * step], packed[2 * step + 1]], axis=0)
         c_ref[step] = both.astype(jnp.bfloat16)
@@ -264,7 +295,8 @@
 
 
 def softmax_call(place, scores, blocks, window):
-    room, fine, pairs = scores.shape
+    _, steps, fine, pairs = scores.shape
+    room, fine = 2 * (steps - 1), fine // 2
     whole = pl.BlockSpec(memory_space=pltpu.VMEM)
     return pl.pallas_call(
         functools.partial(softmax_kernel, blocks, window),
@@ -286,7 +318,8 @@
     window,
     own_ref,
     place_ref,
-    c_ref,
+    mine_ref,
+    other_ref,
     q_ref,
     d_ref,
     out_ref,
@@ -301,8 +334,11 @@
     seqs = wide.shape[0]
     room = packed.shape[1]
     unroll = 16
-    sent = c_ref[:, room // 2].astype(jnp.float32)
-    losses = jnp.sum(sent[:, 0, :] + sent[:, 1, :], axis=0, keepdims=True) / pairs
+    losses = 0.0
+    for half in (mine_ref, other_ref):
+        sent = half[:, room // 2].astype(jnp.float32)
+        losses = losses + jnp.sum(sent[:, 0, :] + sent[:, 1, :], axis=0, keepdims=True) / pairs
+    core = lax.axis_index("pb") % 2
     lane = lax.broadcasted_iota(jnp.int32, losses.shape, 1)
     mine = jnp.where(lane == lax.axis_index("pb"), losses, 0.0)
     loss_ref[...] = jnp.broadcast_to(jnp.sum(mine, axis=1, keepdims=True), loss_ref.shape)
@@ -310,9 +346,11 @@
     square[...] = jnp.zeros_like(square)
 
     def unpack(step, carry):
-        both = c_ref[:, step].astype(jnp.float32)
-        packed[:, 2 * step] = both[:, :fine]
-        packed[:, 2 * step + 1] = both[:, fine:]
+        for half, at in ((mine_ref, core), (other_ref, 1 - core)):
+            both = half[:, step].astype(jnp.float32)
+            for chip in range(blocks // 2):
+                packed[2 * chip + at, 2 * step] = both[chip, :fine]
+                packed[2 * chip + at, 2 * step + 1] = both[chip, fine:]
         return carry
 
     lax.fori_loop(0, room // 2, unpack, 0)
@@ -371,15 +409,15 @@
     lax.fori_loop(0, seqs // slots, narrow, 0)
 
 
-def grad_call(own, place, coefficients, queries, documents, blocks, pairs, window):
+def grad_call(own, place, mine, other, queries, documents, blocks, pairs, window):
     count, piece = queries.shape
     seqs = 2 * count
-    room = 2 * (coefficients.shape[1] - 1)
+    room = 2 * (mine.shape[1] - 1)
     whole = pl.BlockSpec(memory_space=pltpu.VMEM)
     scalars = pl.BlockSpec(memory_space=pltpu.SMEM)
     return pl.pallas_call(
         functools.partial(grad_kernel, blocks, pairs, window),
-        in_specs=[scalars, scalars, whole, whole, whole],
+        in_specs=[scalars, scalars, whole, whole, whole, whole],
         out_specs=[whole, whole],
         out_shape=[
             jax.ShapeDtypeStruct((blocks, seqs // blocks, piece), jnp.bfloat16),
@@ -394,7 +432,7 @@
         ],
         compiler_params=pltpu.CompilerParams(vmem_limit_bytes=vmem_limit),
         name="slice_grads",
-    )(own, place, coefficients, queries, documents)
+    )(own, place, mine, other, queries, documents)
 
 
 def project_kernel(grad_ref, normed_ref, inv_ref, out_ref):
@@ -432,14 +470,15 @@
 
 
 def middle(embedded, room, devices, pairs, window):
-    fine = pairs // devices
     queries, documents, partial_scores, own, place = score_call(
         embedded, room, devices, pairs, window
     )
-    scores = lax.psum_scatter(partial_scores, "pb", scatter_dimension=0, tiled=False)
-    coefficients = softmax_call(place, scores.reshape(room, fine, pairs), devices, window)
-    shared = lax.all_gather(coefficients, "pb", axis=0, tiled=False)
-    grads, loss = grad_call(own, place, shared, queries, documents, devices, pairs, window)
+    scores = lax.all_to_all(partial_scores, "pb", split_axis=0, concat_axis=0, tiled=True)
+    coefficients = softmax_call(place, scores, devices, window)
+    same_core = [list(range(core, devices, 2)) for core in range(2)]
+    mine = lax.all_gather(coefficients, "pb", axis_index_groups=same_core, axis=0, tiled=False)
+    other = lax.ppermute(mine, "pb", [(at, at ^ 1) for at in range(devices)])
+    grads, loss = grad_call(own, place, mine, other, queries, documents, devices, pairs, window)
     return grads, loss[0, :1]
 
 
@@ -449,7 +488,7 @@
     pairs = pair_owner.shape[0]
     window = hard_negatives.shape[1]
     normed, inverse, embedding = norm_call(
-        last_row, hidden, final_gain.reshape(1, width), pair_owner, hard_negatives, devices
+        last_row, hidden, final_gain, pair_owner.T, hard_negatives, devices
     )
     embedded = lax.all_to_all(embedding, "pb", split_axis=0, concat_axis=0, tiled=True)
     most = devices * (window + 1)

time: 295 us -> 270 us (0.915)
  waiting for transfers between devices: 104 us -> 1.96 us
  blocking collectives: 110 us -> 181 us
  starting transfers between devices: 0.08 us -> 6.02 us
    reduce_scatter x1 -> x0, waiting for transfers between devices: 63.1 us -> none  [middle(): lax.psum_scatter(partial_scores, 'pb', scatter_dimension=0, tiled=False)]
    all_to_all x0 -> x1, blocking collectives: none -> 43.9 us  [middle(): lax.all_to_all(partial_scores, 'pb', split_axis=0, concat_axis=0, tiled=T...]
    all_gather x1 -> x0, waiting for transfers between devices: 40.9 us -> none  [middle(): shared = lax.all_gather(coefficients, 'pb', axis=0, tiled=False)]
    all_gather x0 -> x1, blocking collectives: none -> 26.9 us  [middle(): lax.all_gather(coefficients, 'pb', axis_index_groups=same_core, axis=0, t...]
    ppermute x0 -> x1, starting transfers between devices: none -> 6.02 us  [middle(): other = lax.ppermute(mine, 'pb', [(at, at ^ 1) for at in range(devices)])]
  transfers between devices with their start and end apart: 2 -> 1, of which waited for: 2 -> 1; matrix products, arithmetic and copies ran while one was open for 0% -> 0% of each run, Pallas kernels for 0% -> 0%
where the time goes in v5:
time: 270 us; the launch traced here: 269 us
  blocking collectives  181 us (67%)
  Pallas kernels  63.2 us (23%)
  between operations  14.7 us (5%)
  starting transfers between devices  6.02 us (2%)
    all_to_all x1, blocking collectives, feature_plan(): lax.all_to_all(embedding, 'pb', split_axis=0, concat_axis=0, tiled=True)  59.2 us
    all_to_all x1, blocking collectives, feature_plan(): lax.all_to_all(grads, 'pb', split_axis=0, concat_axis=0, tiled=True)  51.2 us
    all_to_all x1, blocking collectives, middle(): lax.all_to_all(partial_scores, 'pb', split_axis=0, concat_axis=0, tiled=T...  43.9 us
    all_gather x1, blocking collectives, middle(): lax.all_gather(coefficients, 'pb', axis_index_groups=same_core, axis=0, t...  26.9 us
    pallas_call x1, Pallas kernels, score_call(): pl.pallas_call(functools.partial(score_kernel, blocks, pairs, window), in...  23.3 us
    pallas_call x1, Pallas kernels, grad_call(): pl.pallas_call(functools.partial(grad_kernel, blocks, pairs, window), in_...  23.1 us
    pallas_call x1, Pallas kernels, project_call(): pl.pallas_call(project_kernel, grid=(seqs // rows,), in_specs=[pl.BlockSp...  7.36 us
    ppermute x1, starting transfers between devices, middle(): other = lax.ppermute(mine, 'pb', [(at, at ^ 1) for at in range(devices)])  6.02 us
  transfers between devices with their start and end apart: 1, of which 1 were waited for; matrix products, arithmetic and copies ran while one was open for 0% of the time, Pallas kernels for 0%

profile of v5, /device:TPU:1, one launch (start us, length us, event | category | flops | bytes accessed | tf_op | source)
XLA Modules:
  0.0 268.6 jit_solution(16682812405923513163)
XLA Ops:
  7.2 5.7 %norm_rows.1 = (bf16[256,4096]{1,0:T(8,128)(2,1)}, f32[256,128]{1,0:T(8,128)}, bf16[16,272,256]{2,1,0:T(8,128)(2,1)}) custom-call(s32[1,256]{1,0:T(1,128)} %last_ref.1, bf16[256,4096]{1,0:T(8,128)(2,1)} %hidden_ref.1, bf16[4096]{0:T(1024)(128)(2,1)} %gain_ref.1, s32[2,128]{1,0:T(2,128)} %bitcast.36, s32[1,4]{1,0:T(1,128)} %negative_ref.1), custom_call_target="tpu_custom_call" | custom-call | tf_op jit(solution)/shard_map/norm_rows/pallas_call | solution.py:83
  12.8 59.2 %all_to_all.66 = bf16[16,272,256]{2,1,0:T(8,128)(2,1)S(1)} all-to-all(bf16[16,272,256]{2,1,0:T(8,128)(2,1)} %get-tuple-element.63), channel_id=1, replica_groups=mesh['groups'=2,'pb'=16] {'pb'}, dimensions={0} | all-to-all | bytes 4456448 | tf_op jit(solution)/shard_map/all_to_all | solution.py:493
  72.0 0.6 fusion
  73.3 129.9 %conditional.1 = (bf16[16,256,256]{2,1,0:T(8,128)(2,1)S(1)}, f32[1]{0:T(128)}) conditional(s32[]{:T(128)} %clamp.3, bf16[16,272,256]{2,1,0:T(8,128)(2,1)S(1)} %all_to_all.66, bf16[16,272,256]{2,1,0:T(8,128)(2,1)S(1)} %all_to_all.66, bf16[16,272,256]{2,1,0:T(8,128)(2,1)S(1)} %all_to_all.66, ...), branch_computations={%region_1.0_spmd, %region_2.0_spmd, %region_3.0_spmd, %region_4.0_... | conditional | bytes 20656252 | solution.py:498
  73.3 23.3 %partial_scores.9 = (bf16[2048,256]{1,0:T(8,128)(2,1)}, bf16[2560,256]{1,0:T(8,128)(2,1)}, s16[16,25,16,128]{3,2,1,0:T(8,128)(2,1)}, s32[16,256]{1,0:T(8,128)}, s32[5,16]{1,0:T(8,128)}) custom-call(bf16[16,272,256]{2,1,0:T(8,128)(2,1)S(1)} %emb_ref.2), custom_call_target="tpu_custom_call" | custom-call | tf_op jit(solution)/shard_map/cond/branch_2_fun/partial_scores/pallas_call | solution.py:215
  96.7 43.9 %all_to_all.61.s_ref = s16[16,25,16,128]{3,2,1,0:T(8,128)(2,1)} all-to-all(s16[16,25,16,128]{3,2,1,0:T(8,128)(2,1)} %get-tuple-element.23), channel_id=1, replica_groups=mesh['groups'=2,'pb'=16] {'pb'}, dimensions={0} | all-to-all | bytes 3276800 | tf_op jit(solution)/shard_map/cond/branch_2_fun/all_to_all | solution.py:476
  140.6 3.7 %softmax_rows.9 = bf16[25,16,128]{2,1,0:T(8,128)(2,1)} custom-call(s32[5,16]{1,0:T(8,128)} %get-tuple-element.22.place_ref, s16[16,25,16,128]{3,2,1,0:T(8,128)(2,1)} %all_to_all.61.s_ref), custom_call_target="tpu_custom_call" | custom-call | tf_op jit(solution)/shard_map/cond/branch_2_fun/softmax_rows/pallas_call | solution.py:301
  144.3 26.9 %all-gather.2 = bf16[200,16,128]{2,1,0:T(8,128)(2,1)S(1)} all-gather(bf16[25,16,128]{2,1,0:T(8,128)(2,1)} %softmax_rows.9), channel_id=4, replica_groups={{0,2,4,6,8,10,12,14},{1,3,5,7,9,11,13,15},{16,18,20,22,24,26,28,30},{17..., dimensions={0}, use_global_device_ids=true | all-gather | bytes 921600 | tf_op jit(solution)/shard_map/cond/branch_2_fun/all_gather | solution.py:479
  171.2 0.0 copy-start.2
  171.2 6.0 %collective-permute-start.2 = (bf16[8,25,16,128]{3,2,1,0:T(8,128)(2,1)S(1)}, bf16[8,25,16,128]{3,2,1,0:T(8,128)(2,1)S(1)}, u32[]{:S(2)}, u32[]{:S(2)}) collective-permute-start(bf16[8,25,16,128]{3,2,1,0:T(8,128)(2,1)S(1)} %bitcast.26), channel_id=1, source_target_pairs={{0,1},{1,0},{2,3},{3,2},{4,5},{5,4},{6,7},{7,6},{8,9},{9,8},{10,11... | collective-permute-start | bytes 2457608 | tf_op jit(solution)/shard_map/cond/branch_2_fun/ppermute | solution.py:480
  177.3 2.0 collective-permute-done.2.other_ref
  179.2 0.0 copy-start.9
  179.2 0.0 copy-done.2
  179.2 0.9 copy-done.9
  180.1 23.1 %slice_grads.9 = (bf16[16,256,256]{2,1,0:T(8,128)(2,1)S(1)}, f32[1,128]{1,0:T(1,128)}) custom-call(s32[16,256]{1,0:T(8,128)} %get-tuple-element.21.own_ref, s32[5,16]{1,0:T(8,128)} %get-tuple-element.22.place_ref, bf16[8,25,16,128]{3,2,1,0:T(8,128)(2,1)} %bitcast.27, bf16[8,25,16,128]{3,2,1,0:T(8,128)(2,1)} %copy-done.9, ...), custom_call_target="tpu_custom_call" | custom-call | tf_op jit(solution)/shard_map/cond/branch_2_fun/slice_grads/pallas_call | solution.py:418
  203.2 51.2 %all_to_all.67.grad_ref = bf16[16,256,256]{2,1,0:T(8,128)(2,1)} all-to-all(bf16[16,256,256]{2,1,0:T(8,128)(2,1)S(1)} %get-tuple-element.64), channel_id=1, replica_groups=mesh['groups'=2,'pb'=16] {'pb'}, dimensions={0} | all-to-all | bytes 4194304 | tf_op jit(solution)/shard_map/all_to_all | solution.py:506
  254.4 7.4 %project_out.1 = f32[256,4096]{1,0:T(8,128)} custom-call(bf16[16,256,256]{2,1,0:T(8,128)(2,1)} %all_to_all.67.grad_ref, bf16[256,4096]{1,0:T(8,128)(2,1)} %get-tuple-element.65.normed_ref, f32[256,128]{1,0:T(8,128)} %get-tuple-element.66.inv_ref), custom_call_target="tpu_custom_call" | custom-call | tf_op jit(solution)/shard_map/project_out/pallas_call | solution.py:457
Async XLA Ops:
  171.2 8.0 %copy-start.2 = (bf16[200,16,128]{2,1,0:T(8,128)(2,1)}, bf16[200,16,128]{2,1,0:T(8,128)(2,1)S(1)}, u32[]{:S(2)}) copy-start(bf16[200,16,128]{2,1,0:T(8,128)(2,1)S(1)} %all-gather.2) | copy-start | bytes 2457604 | tf_op jit(solution)/shard_map/cond
  171.2 8.0 %collective-permute-start.2 = (bf16[8,25,16,128]{3,2,1,0:T(8,128)(2,1)S(1)}, bf16[8,25,16,128]{3,2,1,0:T(8,128)(2,1)S(1)}, u32[]{:S(2)}, u32[]{:S(2)}) collective-permute-start(bf16[8,25,16,128]{3,2,1,0:T(8,128)(2,1)S(1)} %bitcast.26), channel_id=1, source_target_pairs={{0,1},{1,0},{2,3},{3,2},{4,5},{5,4},{6,7},{7,6},{8,9},{9,8},{10,11... | collective-permute-start | bytes 2457608 | tf_op jit(solution)/shard_map/cond/branch_2_fun/ppermute | solution.py:480
  179.2 0.9 copy-start.9

commit v6 on v5

--- a/solution.py
+++ b/solution.py
@@ -101,7 +101,8 @@
     emb_ref,
     q_ref,
     d_ref,
-    s_ref,
+    mine_ref,
+    other_ref,
     own_ref,
     place_ref,
     wide,
@@ -141,7 +142,15 @@
             count = count + present.astype(jnp.int32)
         return count
 
-    lax.fori_loop(0, blocks, place, blocks)
+    used = lax.fori_loop(0, blocks, place, blocks)
+    fine = pairs // blocks
+
+    def clear(spot, carry):
+        empty = jnp.zeros((2, blocks // 2, fine, pairs), jnp.float32)
+        sums[:, :, pl.ds(pl.multiple_of(spot * fine, fine), fine), :] = empty
+        return carry
+
+    lax.fori_loop(used, sums.shape[2] // fine, clear, 0)
     unroll = 16
 
     def pick_block(block, carry):
@@ -160,10 +169,9 @@
 
     lax.fori_loop(0, blocks, pick_block, 0)
     d_ref[blocks * pairs :, :] = d_ref[: window * pairs, :]
-    groups = s_ref.shape[0]
-    fine = pairs // groups
-
-    def score_blocks(step, top):
+    core = lax.axis_index("pb") % 2
+
+    def score_blocks(step, carry):
         at = pl.multiple_of(step * 2 * pairs, 2 * pairs)
         tiles[...] = inverse_temp * lax.dot_general(
             q_ref[pl.ds(at, 2 * pairs), :],
@@ -182,29 +190,20 @@
                         half * pairs : (half + 1) * pairs,
                         (half + column) * pairs : (half + column + 1) * pairs,
                     ]
-                    sums[:, pl.ds(row, fine), :] = tile.reshape(groups, fine, pairs)
-
-        used = tiles[...]
-        for at in range(0, used.shape[1], pairs):
-            size = jnp.abs(used[:, at : at + pairs]).reshape(-1, fine, pairs)
-            top = jnp.maximum(top, jnp.max(size, axis=0))
-        return top
-
-    top = lax.fori_loop(0, blocks // 2, score_blocks, jnp.zeros((fine, pairs), jnp.float32))
-    top = jnp.max(jnp.max(top, axis=1, keepdims=True), axis=0, keepdims=True)
-    bound = jnp.ceil(top * bound_steps) + 1.0
-    scale = code_steps * bound_steps / bound
-    room = s_ref.shape[1] - 1
-
-    def encode(step, carry):
-        at = pl.multiple_of(step * 2 * fine, 2 * fine)
-        codes = jnp.round(sums[:, pl.ds(at, 2 * fine), :] * scale)
-        s_ref[:, step] = codes.astype(jnp.int32).astype(jnp.int16)
-        return carry
-
-    lax.fori_loop(0, room, encode, 0)
-    sent_bound = jnp.broadcast_to(bound, (groups * 2 * fine, pairs)).astype(jnp.int32)
-    s_ref[:, room] = sent_bound.astype(jnp.int16).reshape(groups, 2 * fine, pairs)
+                    parted = tile.reshape(blocks // 2, 2, fine, pairs)
+                    for parity in range(2):
+                        sums[parity, :, pl.ds(row, fine), :] = parted[:, parity]
+
+        return carry
+
+    lax.fori_loop(0, blocks // 2, score_blocks, 0)
+
+    def part(chip, carry):
+        mine_ref[chip] = sums[core, chip]
+        other_ref[chip] = sums[1 - core, chip]
+        return carry
+
+    lax.fori_loop(0, blocks // 2, part, 0)
 
 
 def score_call(embedded, room, blocks, pairs, window):
@@ -215,11 +214,12 @@
     return pl.pallas_call(
         functools.partial(score_kernel, blocks, pairs, window),
         in_specs=[whole],
-        out_specs=[whole, whole, whole, whole, scalars],
+        out_specs=[whole, whole, whole, whole, whole, scalars],
         out_shape=[
             jax.ShapeDtypeStruct((blocks * pairs, piece), jnp.bfloat16),
             jax.ShapeDtypeStruct(((blocks + window) * pairs, piece), jnp.bfloat16),
-            jax.ShapeDtypeStruct((blocks, room // 2 + 1, 2 * fine, pairs), jnp.int16),
+            jax.ShapeDtypeStruct((blocks // 2, room * fine, pairs), jnp.float32),
+            jax.ShapeDtypeStruct((blocks // 2, room * fine, pairs), jnp.float32),
             jax.ShapeDtypeStruct((blocks, 2 * pairs), jnp.int32),
             jax.ShapeDtypeStruct((window + 1, blocks), jnp.int32),
         ],
@@ -230,7 +230,7 @@
             pltpu.VMEM((blocks, lanes), jnp.int32),
             pltpu.SMEM((blocks, 2 * pairs), jnp.int32),
             pltpu.SMEM((blocks, lanes), jnp.int32),
-            pltpu.VMEM((blocks, room * fine, pairs), jnp.float32),
+            pltpu.VMEM((2, blocks // 2, room * fine, pairs), jnp.float32),
             pltpu.SemaphoreType.DMA((2,)),
         ],
         compiler_params=pltpu.CompilerParams(vmem_limit_bytes=vmem_limit),
@@ -238,15 +238,62 @@
     )(embedded)
 
 
-def softmax_kernel(blocks, window, place_ref, s_ref, c_ref, packed, masked):
+def merge_kernel(mine_ref, other_ref, own_ref, *code_refs):
+    chips, rows, pairs = mine_ref.shape
+    steps = code_refs[0].shape[0] - 1
+    fine = rows // steps // 2
+    chip = lax.axis_index("pb") // 2
+
+    def largest(step, top):
+        at = pl.multiple_of(step * 2 * fine, 2 * fine)
+        size = jnp.abs(mine_ref[:, pl.ds(at, 2 * fine), :] + other_ref[:, pl.ds(at, 2 * fine), :])
+        return jnp.maximum(top, jnp.max(size, axis=0))
+
+    top = lax.fori_loop(0, steps, largest, jnp.zeros((2 * fine, pairs), jnp.float32))
+    top = jnp.max(jnp.max(top, axis=1, keepdims=True), axis=0, keepdims=True)
+    bound = jnp.ceil(jnp.minimum(top, 100.0) * bound_steps) + 1.0
+    scale = code_steps * bound_steps / bound
+    own_ref[...] = mine_ref[chip] + other_ref[chip]
+    for hop, code_ref in enumerate(code_refs):
+        target = chip ^ (hop + 1)
+
+        def encode(step, carry):
+            at = pl.multiple_of(step * 2 * fine, 2 * fine)
+            there = pl.ds(at, 2 * fine)
+            codes = jnp.round((mine_ref[target, there, :] + other_ref[target, there, :]) * scale)
+            code_ref[step] = codes.astype(jnp.int32).astype(jnp.int16)
+            return carry
+
+        lax.fori_loop(0, steps, encode, 0)
+        code_ref[steps] = jnp.broadcast_to(bound, (2 * fine, pairs)).astype(jnp.int32).astype(jnp.int16)
+
+
+def merge_call(mine, other, blocks):
+    chips, rows, pairs = mine.shape
+    fine = pairs // blocks
+    whole = pl.BlockSpec(memory_space=pltpu.VMEM)
+    coded = jax.ShapeDtypeStruct((rows // (2 * fine) + 1, 2 * fine, pairs), jnp.int16)
+    return pl.pallas_call(
+        merge_kernel,
+        in_specs=[whole, whole],
+        out_specs=[whole] * chips,
+        out_shape=[jax.ShapeDtypeStruct((rows, pairs), jnp.float32)] + [coded] * (chips - 1),
+        compiler_params=pltpu.CompilerParams(vmem_limit_bytes=vmem_limit),
+        name="merge_scores",
+    )(mine, other)
+
+
+def softmax_kernel(blocks, window, place_ref, own_ref, *refs):
+    code_refs, (c_ref, packed, masked) = refs[:-3], refs[-3:]
     room, fine, pairs = packed.shape
     count = blocks * fine
-    bound = s_ref[:, room // 2].astype(jnp.int32).astype(jnp.float32)
-    scale = bound * (1.0 / (code_steps * bound_steps))
+    unit = 1.0 / (code_steps * bound_steps)
+    scales = [ref[room // 2].astype(jnp.int32).astype(jnp.float32) * unit for ref in code_refs]
 
     def decode(step, carry):
-        codes = s_ref[:, step].astype(jnp.int32).astype(jnp.float32)
-        both = jnp.sum(codes * scale, axis=0)
+        both = own_ref[pl.ds(pl.multiple_of(step * 2 * fine, 2 * fine), 2 * fine), :]
+        for ref, scale in zip(code_refs, scales):
+            both = both + ref[step].astype(jnp.int32).astype(jnp.float32) * scale
         packed[2 * step] = both[:fine]
         packed[2 * step + 1] = both[fine:]
         return carry
@@ -294,13 +341,13 @@
     c_ref[room // 2] = both.astype(jnp.bfloat16)
 
 
-def softmax_call(place, scores, blocks, window):
-    _, steps, fine, pairs = scores.shape
+def softmax_call(place, own_scores, codes, blocks, window):
+    steps, fine, pairs = codes[0].shape
     room, fine = 2 * (steps - 1), fine // 2
     whole = pl.BlockSpec(memory_space=pltpu.VMEM)
     return pl.pallas_call(
         functools.partial(softmax_kernel, blocks, window),
-        in_specs=[pl.BlockSpec(memory_space=pltpu.SMEM), whole],
+        in_specs=[pl.BlockSpec(memory_space=pltpu.SMEM), whole] + [whole] * len(codes),
         out_specs=whole,
         out_shape=jax.ShapeDtypeStruct((room // 2 + 1, 2 * fine, pairs), jnp.bfloat16),
         scratch_shapes=[
@@ -309,7 +356,7 @@
         ],
         compiler_params=pltpu.CompilerParams(vmem_limit_bytes=vmem_limit),
         name="softmax_rows",
-    )(place, scores)
+    )(place, own_scores, *codes)
 
 
 def grad_kernel(
@@ -318,39 +365,33 @@
     window,
     own_ref,
     place_ref,
-    mine_ref,
-    other_ref,
     q_ref,
     d_ref,
-    out_ref,
-    loss_ref,
-    wide,
-    dsum,
-    picked,
-    packed,
-    square,
+    *refs,
 ):
+    part_refs, (out_ref, loss_ref, wide, dsum, picked, packed, square) = refs[:-7], refs[-7:]
     fine = pairs // blocks
     seqs = wide.shape[0]
     room = packed.shape[1]
+    me = lax.axis_index("pb")
+    masks = swap_masks(blocks)
     unroll = 16
     losses = 0.0
-    for half in (mine_ref, other_ref):
-        sent = half[:, room // 2].astype(jnp.float32)
+    for part in part_refs:
+        sent = part[:, room // 2].astype(jnp.float32)
         losses = losses + jnp.sum(sent[:, 0, :] + sent[:, 1, :], axis=0, keepdims=True) / pairs
-    core = lax.axis_index("pb") % 2
     lane = lax.broadcasted_iota(jnp.int32, losses.shape, 1)
-    mine = jnp.where(lane == lax.axis_index("pb"), losses, 0.0)
+    mine = jnp.where(lane == me, losses, 0.0)
     loss_ref[...] = jnp.broadcast_to(jnp.sum(mine, axis=1, keepdims=True), loss_ref.shape)
     dsum[...] = jnp.zeros_like(dsum)
     square[...] = jnp.zeros_like(square)
 
     def unpack(step, carry):
-        for half, at in ((mine_ref, core), (other_ref, 1 - core)):
-            both = half[:, step].astype(jnp.float32)
-            for chip in range(blocks // 2):
-                packed[2 * chip + at, 2 * step] = both[chip, :fine]
-                packed[2 * chip + at, 2 * step + 1] = both[chip, fine:]
+        for part, mask in zip(part_refs, masks):
+            both = part[:, step].astype(jnp.float32)
+            for at, apart in enumerate(mask):
+                packed[me ^ apart, 2 * step] = both[at, :fine]
+                packed[me ^ apart, 2 * step + 1] = both[at, fine:]
         return carry
 
     lax.fori_loop(0, room // 2, unpack, 0)
@@ -409,15 +450,15 @@
     lax.fori_loop(0, seqs // slots, narrow, 0)
 
 
-def grad_call(own, place, mine, other, queries, documents, blocks, pairs, window):
+def grad_call(own, place, parts, queries, documents, blocks, pairs, window):
     count, piece = queries.shape
     seqs = 2 * count
-    room = 2 * (mine.shape[1] - 1)
+    room = 2 * (parts[0].shape[1] - 1)
     whole = pl.BlockSpec(memory_space=pltpu.VMEM)
     scalars = pl.BlockSpec(memory_space=pltpu.SMEM)
     return pl.pallas_call(
         functools.partial(grad_kernel, blocks, pairs, window),
-        in_specs=[scalars, scalars, whole, whole, whole, whole],
+        in_specs=[scalars, scalars, whole, whole] + [whole] * len(parts),
         out_specs=[whole, whole],
         out_shape=[
             jax.ShapeDtypeStruct((blocks, seqs // blocks, piece), jnp.bfloat16),
@@ -432,7 +473,7 @@
         ],
         compiler_params=pltpu.CompilerParams(vmem_limit_bytes=vmem_limit),
         name="slice_grads",
-    )(own, place, mine, other, queries, documents)
+    )(own, place, queries, documents, *parts)
 
 
 def project_kernel(grad_ref, normed_ref, inv_ref, out_ref):
@@ -469,16 +510,41 @@
     )(returned, normed, inverse)
 
 
+def swapped(value, apart):
+    pairs = [(at, at ^ apart) for at in range(lax.axis_size("pb"))]
+    return lax.ppermute(value, "pb", pairs)
+
+
+def swap_steps(devices):
+    return [1 << bit for bit in reversed(range(devices.bit_length() - 1))]
+
+
+def swap_masks(devices):
+    known, masks = [0], [[0]]
+    for apart in swap_steps(devices):
+        masks.append([mask ^ apart for mask in known])
+        known = known + masks[-1]
+    return masks
+
+
+def gather_all(value):
+    held = value[None]
+    parts = [held]
+    for apart in swap_steps(lax.axis_size("pb")):
+        arrived = swapped(held, apart)
+        parts.append(arrived)
+        held = jnp.concatenate([held, arrived], axis=0)
+    return parts
+
+
 def middle(embedded, room, devices, pairs, window):
-    queries, documents, partial_scores, own, place = score_call(
+    queries, documents, mine, other, own, place = score_call(
         embedded, room, devices, pairs, window
     )
-    scores = lax.all_to_all(partial_scores, "pb", split_axis=0, concat_axis=0, tiled=True)
-    coefficients = softmax_call(place, scores, devices, window)
-    same_core = [list(range(core, devices, 2)) for core in range(2)]
-    mine = lax.all_gather(coefficients, "pb", axis_index_groups=same_core, axis=0, tiled=False)
-    other = lax.ppermute(mine, "pb", [(at, at ^ 1) for at in range(devices)])
-    grads, loss = grad_call(own, place, mine, other, queries, documents, devices, pairs, window)
+    own_scores, *codes = merge_call(mine, swapped(other, 1), devices)
+    codes = [swapped(code, 2 * (hop + 1)) for hop, code in enumerate(codes)]
+    parts = gather_all(softmax_call(place, own_scores, codes, devices, window))
+    grads, loss = grad_call(own, place, parts, queries, documents, devices, pairs, window)
     return grads, loss[0, :1]
 
 

time: 270 us -> 241 us (0.89)
  blocking collectives: 181 us -> 110 us
  waiting for transfers between devices: 1.96 us -> 29.1 us
  starting transfers between devices: 6.02 us -> 23.7 us
  between operations: 14.7 us -> 1.3 us
  Pallas kernels: 63.2 us -> 68 us
  other arithmetic: 0.62 us -> 3.68 us
    all_to_all x1 -> x0, blocking collectives: 43.9 us -> none  [middle(): lax.all_to_all(partial_scores, 'pb', split_axis=0, concat_axis=0, tiled=T...]
    ppermute x1 -> x12, waiting for transfers between devices: 1.96 us -> 29.1 us  [swapped(): return lax.ppermute(value, 'pb', pairs)]
    all_gather x1 -> x0, blocking collectives: 26.9 us -> none  [middle(): lax.all_gather(coefficients, 'pb', axis_index_groups=same_core, axis=0, t...]
    ppermute x1 -> x12, starting transfers between devices: 6.02 us -> 23.7 us  [swapped(): return lax.ppermute(value, 'pb', pairs)]
    pallas_call x0 -> x1, Pallas kernels: none -> 4.88 us  [merge_call(): pl.pallas_call(merge_kernel, in_specs=[whole, whole], out_specs=[whole] *...]
    concatenate x0 -> x3, other arithmetic: none -> 3.06 us  [gather_all(): held = jnp.concatenate([held, arrived], axis=0)]
  transfers between devices with their start and end apart: 1 -> 12, of which waited for: 1 -> 7; matrix products, arithmetic and copies ran while one was open for 0% -> 0% of each run, Pallas kernels for 0% -> 0%
where the time goes in v6:
time: 241 us; the launch traced here: 239 us
  blocking collectives  110 us (46%)
  Pallas kernels  68 us (28%)
  waiting for transfers between devices  29.1 us (12%)
  starting transfers between devices  23.7 us (10%)
  other arithmetic  3.68 us (2%)
  local copies, waits for them, and re-layouts  2.79 us (1%)
    all_to_all x1, blocking collectives, feature_plan(): lax.all_to_all(embedding, 'pb', split_axis=0, concat_axis=0, tiled=True)  59.2 us
    all_to_all x1, blocking collectives, feature_plan(): lax.all_to_all(grads, 'pb', split_axis=0, concat_axis=0, tiled=True)  51.2 us
    ppermute x12, waiting for transfers between devices, swapped(): return lax.ppermute(value, 'pb', pairs)  29.1 us
    ppermute x12, starting transfers between devices, swapped(): return lax.ppermute(value, 'pb', pairs)  23.7 us
    pallas_call x1, Pallas kernels, score_call(): pl.pallas_call(functools.partial(score_kernel, blocks, pairs, window), in...  23.4 us
    pallas_call x1, Pallas kernels, grad_call(): pl.pallas_call(functools.partial(grad_kernel, blocks, pairs, window), in_...  23.4 us
    pallas_call x1, Pallas kernels, project_call(): pl.pallas_call(project_kernel, grid=(seqs // rows,), in_specs=[pl.BlockSp...  7.36 us
    pallas_call x1, Pallas kernels, norm_call(): pl.pallas_call(norm_kernel, in_specs=[whole, whole, whole, whole, pl.Bloc...  5.66 us
  transfers between devices with their start and end apart: 12, of which 7 were waited for; matrix products, arithmetic and copies ran while one was open for 0% of the time, Pallas kernels for 0%

profile of v6, /device:TPU:1, one launch (start us, length us, event | category | flops | bytes accessed | tf_op | source)
XLA Modules:
  0.0 239.3 jit_solution(10503958807784991192)
XLA Ops:
  0.6 5.7 %norm_rows.1 = (bf16[256,4096]{1,0:T(8,128)(2,1)}, f32[256,128]{1,0:T(8,128)}, bf16[16,272,256]{2,1,0:T(8,128)(2,1)}) custom-call(s32[1,256]{1,0:T(1,128)} %last_ref.1, bf16[256,4096]{1,0:T(8,128)(2,1)} %hidden_ref.1, bf16[4096]{0:T(1024)(128)(2,1)} %gain_ref.1, s32[2,128]{1,0:T(2,128)} %bitcast.57, s32[1,4]{1,0:T(1,128)} %negative_ref.1), custom_call_target="tpu_custom_call" | custom-call | tf_op jit(solution)/shard_map/norm_rows/pallas_call | solution.py:83
  6.3 59.2 %all_to_all.31 = bf16[16,272,256]{2,1,0:T(8,128)(2,1)S(1)} all-to-all(bf16[16,272,256]{2,1,0:T(8,128)(2,1)} %get-tuple-element.126), channel_id=1, replica_groups=mesh['groups'=2,'pb'=16] {'pb'}, dimensions={0} | all-to-all | bytes 4456448 | tf_op jit(solution)/shard_map/all_to_all | solution.py:559
  65.5 0.6 fusion
  66.8 113.9 %conditional.1 = (bf16[16,256,256]{2,1,0:T(8,128)(2,1)S(1)}, f32[1]{0:T(128)}) conditional(s32[]{:T(128)} %clamp.3, bf16[16,272,256]{2,1,0:T(8,128)(2,1)S(1)} %all_to_all.31, bf16[16,272,256]{2,1,0:T(8,128)(2,1)S(1)} %all_to_all.31, bf16[16,272,256]{2,1,0:T(8,128)(2,1)S(1)} %all_to_all.31, ...), branch_computations={%region_1.0_spmd, %region_2.0_spmd, %region_3.0_spmd, %region_4.0_... | conditional | flops 2854912 | bytes 55903068 | solution.py:564
  67.0 23.4 %partial_scores.10 = (bf16[2048,256]{1,0:T(8,128)(2,1)}, bf16[2560,256]{1,0:T(8,128)(2,1)}, f32[8,416,128]{2,1,0:T(8,128)}, f32[8,416,128]{2,1,0:T(8,128)}, s32[16,256]{1,0:T(8,128)}, /*index=5*/s32[5,16]{1,0:T(8,128)}) custom-call(bf16[16,272,256]{2,1,0:T(8,128)(2,1)S(1)} %emb_ref.3), custom_call_target="tpu_custom_call" | custom-call | tf_op jit(solution)/shard_map/cond/branch_3_fun/partial_scores/pallas_call | solution.py:214
  90.7 3.6 %collective-permute-done.36.other_ref = f32[8,416,128]{2,1,0:T(8,128)S(1)} collective-permute-done((f32[8,416,128]{2,1,0:T(8,128)}, f32[8,416,128]{2,1,0:T(8,128)S(1)}, u32[]{:S(2)}, u32[]{:S(2)}) %collective-permute-start.36) | collective-permute-done | bytes 1703968 | tf_op jit(solution)/shard_map/cond/branch_3_fun/ppermute | solution.py:515
  94.3 1.2 copy-done.19
  95.5 4.9 %merge_scores.10 = (f32[416,128]{1,0:T(8,128)}, s16[27,16,128]{2,1,0:T(8,128)(2,1)}, s16[27,16,128]{2,1,0:T(8,128)(2,1)}, s16[27,16,128]{2,1,0:T(8,128)(2,1)}, s...) custom-call(f32[8,416,128]{2,1,0:T(8,128)} %get-tuple-element.59.min, ...), custom_call_target="tpu_custom_call" | custom-call | tf_op jit(solution)/shard_map/cond/branch_3_fun/merge_scores/pallas_call | solution.py:276
  100.8 0.5 collective-permute-start.38
  101.2 1.8 collective-permute-start.39
  103.0 0.8 collective-permute-start.40
  103.9 1.6 collective-permute-start.41
  105.5 1.5 collective-permute-start.42
  107.0 2.6 %collective-permute-start.43 = (s16[27,16,128]{2,1,0:T(8,128)(2,1)}, s16[27,16,128]{2,1,0:T(8,128)(2,1)S(1)}, u32[]{:S(2)}, u32[]{:S(2)}) collective-permute-start(s16[27,16,128]{2,1,0:T(8,128)(2,1)} %get-tuple-element.68), channel_id=1, source_target_pairs={{0,14},{1,15},{2,12},{3,13},{4,10},{5,11},{6,8},{7,9},{8,6},{9,7},... | collective-permute-start | bytes 331784 | tf_op jit(solution)/shard_map/cond/branch_3_fun/ppermute | solution.py:515
  109.6 1.0 collective-permute-done.39.refs_2_
  110.6 9.9 %collective-permute-done.41.refs_4_ = s16[27,16,128]{2,1,0:T(8,128)(2,1)S(1)} collective-permute-done((s16[27,16,128]{2,1,0:T(8,128)(2,1)}, s16[27,16,128]{2,1,0:T(8,128)(2,1)S(1)}, u32[]{:S(2)}, u32[]{:S(2)}) %collective-permute-start.41) | collective-permute-done | bytes 110624 | tf_op jit(solution)/shard_map/cond/branch_3_fun/ppermute | solution.py:515
  120.5 0.6 copy-done.63
  121.2 3.2 %softmax_rows.10 = bf16[27,16,128]{2,1,0:T(8,128)(2,1)} custom-call(s32[5,16]{1,0:T(8,128)} %get-tuple-element.56.place_ref, f32[416,128]{1,0:T(8,128)} %get-tuple-element.61.own_ref, s16[27,16,128]{2,1,0:T(8,128)(2,1)} %copy-done.59, s16[27,16,128]{2,1,0:T(8,128)(2,1)} %copy-done.60, s16[27,16,128]{2,1,0:T(8,128)(2,1)} %copy-done.61, ...), custom_call_target="tpu_custom_call" | custom-call | tf_op jit(solution)/shard_map/cond/branch_3_fun/softmax_rows/pallas_call | solution.py:348
  124.4 5.5 %collective-permute-start.44 = (bf16[1,27,16,128]{3,2,1,0:T(8,128)(2,1)}, bf16[1,27,16,128]{3,2,1,0:T(8,128)(2,1)S(1)}, u32[]{:S(2)}, u32[]{:S(2)}) collective-permute-start(bf16[1,27,16,128]{3,2,1,0:T(8,128)(2,1)} %bitcast.37), channel_id=1, source_target_pairs={{0,8},{1,9},{2,10},{3,11},{4,12},{5,13},{6,14},{7,15},{8,0},{9,1},... | collective-permute-start | bytes 331784 | tf_op jit(solution)/shard_map/cond/branch_3_fun/ppermute | solution.py:515
  129.9 2.3 collective-permute-done.44.refs_1_
  132.2 1.0 pad_maximum_fusion.11
  133.2 2.0 collective-permute-start.45
  135.2 3.3 %collective-permute-done.45.refs_2_ = bf16[2,27,16,128]{3,2,1,0:T(8,128)(2,1)S(1)} collective-permute-done((bf16[2,27,16,128]{3,2,1,0:T(8,128)(2,1)S(1)}, bf16[2,27,16,128]{3,2,1,0:T(8,128)(2,1)S(1)}, u32[]{:S(2)}, u32[]{:S(2)}) %collective-permute-start.45) | collective-permute-done | bytes 221216 | tf_op jit(solution)/shard_map/cond/branch_3_fun/ppermute | solution.py:515
  138.5 1.0 pad_maximum_fusion.10
  139.9 6.9 %collective-permute-done.46.refs_3_ = bf16[4,27,16,128]{3,2,1,0:T(8,128)(2,1)S(1)} collective-permute-done((bf16[4,27,16,128]{3,2,1,0:T(8,128)(2,1)S(1)}, bf16[4,27,16,128]{3,2,1,0:T(8,128)(2,1)S(1)}, u32[]{:S(2)}, u32[]{:S(2)}) %collective-permute-start.46) | collective-permute-done | bytes 442400 | tf_op jit(solution)/shard_map/cond/branch_3_fun/ppermute | solution.py:515
  146.8 1.1 pad_maximum_fusion.9
  147.9 6.5 %collective-permute-start.47 = (bf16[8,27,16,128]{3,2,1,0:T(8,128)(2,1)S(1)}, bf16[8,27,16,128]{3,2,1,0:T(8,128)(2,1)S(1)}, u32[]{:S(2)}, u32[]{:S(2)}) collective-permute-start(bf16[8,27,16,128]{3,2,1,0:T(8,128)(2,1)S(1)} %pad_maximum_fusion.9), channel_id=1, source_target_pairs={{0,1},{1,0},{2,3},{3,2},{4,5},{5,4},{6,7},{7,6},{8,9},{9,8},{10,11... | collective-permute-start | bytes 2654216 | tf_op jit(solution)/shard_map/cond/branch_3_fun/ppermute | solution.py:515
  154.3 2.1 collective-permute-done.47.refs_4_
  156.4 0.9 copy-done.34
  157.3 23.4 %slice_grads.10 = (bf16[16,256,256]{2,1,0:T(8,128)(2,1)S(1)}, f32[1,128]{1,0:T(1,128)}) custom-call(s32[16,256]{1,0:T(8,128)} %get-tuple-element.55.own_ref, s32[5,16]{1,0:T(8,128)} %get-tuple-element.56.place_ref, bf16[2048,256]{1,0:T(8,128)(2,1)} %get-tuple-element.57.q_ref, bf16[2560,256]{1,0:T(8,128)(2,1)} %get-tuple-element.58.d_ref, ...), custom_call_target="tpu_custom_call" | custom-call | tf_op jit(solution)/shard_map/cond/branch_3_fun/slice_grads/pallas_call | solution.py:459
  180.7 51.2 %all_to_all.32.grad_ref = bf16[16,256,256]{2,1,0:T(8,128)(2,1)} all-to-all(bf16[16,256,256]{2,1,0:T(8,128)(2,1)S(1)} %get-tuple-element.127), channel_id=1, replica_groups=mesh['groups'=2,'pb'=16] {'pb'}, dimensions={0} | all-to-all | bytes 4194304 | tf_op jit(solution)/shard_map/all_to_all | solution.py:572
  231.9 7.4 %project_out.1 = f32[256,4096]{1,0:T(8,128)} custom-call(bf16[16,256,256]{2,1,0:T(8,128)(2,1)} %all_to_all.32.grad_ref, bf16[256,4096]{1,0:T(8,128)(2,1)} %get-tuple-element.128.normed_ref, f32[256,128]{1,0:T(8,128)} %get-tuple-element.129.inv_ref), custom_call_target="tpu_custom_call" | custom-call | tf_op jit(solution)/shard_map/project_out/pallas_call | solution.py:498
  (29 shorter events, 1.1 us)
Async XLA Ops:
  90.5 3.9 %collective-permute-start.36 = (f32[8,416,128]{2,1,0:T(8,128)}, f32[8,416,128]{2,1,0:T(8,128)S(1)}, u32[]{:S(2)}, u32[]{:S(2)}) collective-permute-start(f32[8,416,128]{2,1,0:T(8,128)} %get-tuple-element.60), channel_id=1, source_target_pairs={{0,1},{1,0},{2,3},{3,2},{4,5},{5,4},{6,7},{7,6},{8,9},{9,8},{10,11... | collective-permute-start | bytes 5111816 | tf_op jit(solution)/shard_map/cond/branch_3_fun/ppermute | solution.py:515
  94.3 1.2 copy-start.19
  100.4 5.1 %collective-permute-start.37 = (s16[27,16,128]{2,1,0:T(8,128)(2,1)}, s16[27,16,128]{2,1,0:T(8,128)(2,1)S(1)}, u32[]{:S(2)}, u32[]{:S(2)}) collective-permute-start(s16[27,16,128]{2,1,0:T(8,128)(2,1)} %get-tuple-element.62), channel_id=1, source_target_pairs={{0,2},{1,3},{2,0},{3,1},{4,6},{5,7},{6,4},{7,5},{8,10},{9,11},{10,... | collective-permute-start | bytes 331784 | tf_op jit(solution)/shard_map/cond/branch_3_fun/ppermute | solution.py:515
  100.8 6.2 %collective-permute-start.38 = (s16[27,16,128]{2,1,0:T(8,128)(2,1)}, s16[27,16,128]{2,1,0:T(8,128)(2,1)S(1)}, u32[]{:S(2)}, u32[]{:S(2)}) collective-permute-start(s16[27,16,128]{2,1,0:T(8,128)(2,1)} %get-tuple-element.63), channel_id=1, source_target_pairs={{0,4},{1,5},{2,6},{3,7},{4,0},{5,1},{6,2},{7,3},{8,12},{9,13},{10,... | collective-permute-start | bytes 331784 | tf_op jit(solution)/shard_map/cond/branch_3_fun/ppermute | solution.py:515
  101.2 9.3 %collective-permute-start.39 = (s16[27,16,128]{2,1,0:T(8,128)(2,1)}, s16[27,16,128]{2,1,0:T(8,128)(2,1)S(1)}, u32[]{:S(2)}, u32[]{:S(2)}) collective-permute-start(s16[27,16,128]{2,1,0:T(8,128)(2,1)} %get-tuple-element.64), channel_id=1, source_target_pairs={{0,6},{1,7},{2,4},{3,5},{4,2},{5,3},{6,0},{7,1},{8,14},{9,15},{10,... | collective-permute-start | bytes 331784 | tf_op jit(solution)/shard_map/cond/branch_3_fun/ppermute | solution.py:515
  103.0 7.5 %collective-permute-start.40 = (s16[27,16,128]{2,1,0:T(8,128)(2,1)}, s16[27,16,128]{2,1,0:T(8,128)(2,1)S(1)}, u32[]{:S(2)}, u32[]{:S(2)}) collective-permute-start(s16[27,16,128]{2,1,0:T(8,128)(2,1)} %get-tuple-element.65), channel_id=1, source_target_pairs={{0,8},{1,9},{2,10},{3,11},{4,12},{5,13},{6,14},{7,15},{8,0},{9,1},... | collective-permute-start | bytes 331784 | tf_op jit(solution)/shard_map/cond/branch_3_fun/ppermute | solution.py:515
  103.9 16.6 %collective-permute-start.41 = (s16[27,16,128]{2,1,0:T(8,128)(2,1)}, s16[27,16,128]{2,1,0:T(8,128)(2,1)S(1)}, u32[]{:S(2)}, u32[]{:S(2)}) collective-permute-start(s16[27,16,128]{2,1,0:T(8,128)(2,1)} %get-tuple-element.66), channel_id=1, source_target_pairs={{0,10},{1,11},{2,8},{3,9},{4,14},{5,15},{6,12},{7,13},{8,2},{9,3},... | collective-permute-start | bytes 331784 | tf_op jit(solution)/shard_map/cond/branch_3_fun/ppermute | solution.py:515
  105.5 15.0 %copy-start.59 = (s16[27,16,128]{2,1,0:T(8,128)(2,1)}, s16[27,16,128]{2,1,0:T(8,128)(2,1)S(1)}, u32[]{:S(2)}) copy-start(s16[27,16,128]{2,1,0:T(8,128)(2,1)S(1)} %collective-permute-done.37.refs_0_) | copy-start | bytes 331780 | tf_op jit(solution)/shard_map/cond
  105.5 14.9 %collective-permute-start.42 = (s16[27,16,128]{2,1,0:T(8,128)(2,1)}, s16[27,16,128]{2,1,0:T(8,128)(2,1)S(1)}, u32[]{:S(2)}, u32[]{:S(2)}) collective-permute-start(s16[27,16,128]{2,1,0:T(8,128)(2,1)} %get-tuple-element.67), channel_id=1, source_target_pairs={{0,12},{1,13},{2,14},{3,15},{4,8},{5,9},{6,10},{7,11},{8,4},{9,5},... | collective-permute-start | bytes 331784 | tf_op jit(solution)/shard_map/cond/branch_3_fun/ppermute | solution.py:515
  107.0 13.4 %copy-start.60 = (s16[27,16,128]{2,1,0:T(8,128)(2,1)}, s16[27,16,128]{2,1,0:T(8,128)(2,1)S(1)}, u32[]{:S(2)}) copy-start(s16[27,16,128]{2,1,0:T(8,128)(2,1)S(1)} %collective-permute-done.38.refs_1_) | copy-start | bytes 331780 | tf_op jit(solution)/shard_map/cond
  107.0 13.4 %collective-permute-start.43 = (s16[27,16,128]{2,1,0:T(8,128)(2,1)}, s16[27,16,128]{2,1,0:T(8,128)(2,1)S(1)}, u32[]{:S(2)}, u32[]{:S(2)}) collective-permute-start(s16[27,16,128]{2,1,0:T(8,128)(2,1)} %get-tuple-element.68), channel_id=1, source_target_pairs={{0,14},{1,15},{2,12},{3,13},{4,10},{5,11},{6,8},{7,9},{8,6},{9,7},... | collective-permute-start | bytes 331784 | tf_op jit(solution)/shard_map/cond/branch_3_fun/ppermute | solution.py:515
  110.6 9.9 %copy-start.61 = (s16[27,16,128]{2,1,0:T(8,128)(2,1)}, s16[27,16,128]{2,1,0:T(8,128)(2,1)S(1)}, u32[]{:S(2)}) copy-start(s16[27,16,128]{2,1,0:T(8,128)(2,1)S(1)} %collective-permute-done.39.refs_2_) | copy-start | bytes 331780 | tf_op jit(solution)/shard_map/cond
  110.6 9.9 %copy-start.62 = (s16[27,16,128]{2,1,0:T(8,128)(2,1)}, s16[27,16,128]{2,1,0:T(8,128)(2,1)S(1)}, u32[]{:S(2)}) copy-start(s16[27,16,128]{2,1,0:T(8,128)(2,1)S(1)} %collective-permute-done.40.refs_3_) | copy-start | bytes 331780 | tf_op jit(solution)/shard_map/cond
  120.4 0.6 copy-start.63
  120.4 0.7 copy-start.64
  120.5 0.7 copy-start.65
  124.4 7.8 %collective-permute-start.44 = (bf16[1,27,16,128]{3,2,1,0:T(8,128)(2,1)}, bf16[1,27,16,128]{3,2,1,0:T(8,128)(2,1)S(1)}, u32[]{:S(2)}, u32[]{:S(2)}) collective-permute-start(bf16[1,27,16,128]{3,2,1,0:T(8,128)(2,1)} %bitcast.37), channel_id=1, source_target_pairs={{0,8},{1,9},{2,10},{3,11},{4,12},{5,13},{6,14},{7,15},{8,0},{9,1},... | collective-permute-start | bytes 331784 | tf_op jit(solution)/shard_map/cond/branch_3_fun/ppermute | solution.py:515
  132.2 15.6 %copy-start.17 = (bf16[1,27,16,128]{3,2,1,0:T(8,128)(2,1)}, bf16[1,27,16,128]{3,2,1,0:T(8,128)(2,1)S(1)}, u32[]{:S(2)}) copy-start(bf16[1,27,16,128]{3,2,1,0:T(8,128)(2,1)S(1)} %collective-permute-done.44.refs_1_) | copy-start | bytes 331780 | tf_op jit(solution)/shard_map/cond
  133.2 5.3 %collective-permute-start.45 = (bf16[2,27,16,128]{3,2,1,0:T(8,128)(2,1)S(1)}, bf16[2,27,16,128]{3,2,1,0:T(8,128)(2,1)S(1)}, u32[]{:S(2)}, u32[]{:S(2)}) collective-permute-start(bf16[2,27,16,128]{3,2,1,0:T(8,128)(2,1)S(1)} %pad_maximum_fusion.11), channel_id=1, source_target_pairs={{0,4},{1,5},{2,6},{3,7},{4,0},{5,1},{6,2},{7,3},{8,12},{9,13},{10,... | collective-permute-start | bytes 663560 | tf_op jit(solution)/shard_map/cond/branch_3_fun/ppermute | solution.py:515
  138.5 17.9 %copy-start.12 = (bf16[2,27,16,128]{3,2,1,0:T(8,128)(2,1)}, bf16[2,27,16,128]{3,2,1,0:T(8,128)(2,1)S(1)}, u32[]{:S(2)}) copy-start(bf16[2,27,16,128]{3,2,1,0:T(8,128)(2,1)S(1)} %collective-permute-done.45.refs_2_) | copy-start | bytes 663556 | tf_op jit(solution)/shard_map/cond
  139.5 7.2 %collective-permute-start.46 = (bf16[4,27,16,128]{3,2,1,0:T(8,128)(2,1)S(1)}, bf16[4,27,16,128]{3,2,1,0:T(8,128)(2,1)S(1)}, u32[]{:S(2)}, u32[]{:S(2)}) collective-permute-start(bf16[4,27,16,128]{3,2,1,0:T(8,128)(2,1)S(1)} %pad_maximum_fusion.10), channel_id=1, source_target_pairs={{0,2},{1,3},{2,0},{3,1},{4,6},{5,7},{6,4},{7,5},{8,10},{9,11},{10,... | collective-permute-start | bytes 1327112 | tf_op jit(solution)/shard_map/cond/branch_3_fun/ppermute | solution.py:515
  146.8 9.7 %copy-start.18 = (bf16[4,27,16,128]{3,2,1,0:T(8,128)(2,1)}, bf16[4,27,16,128]{3,2,1,0:T(8,128)(2,1)S(1)}, u32[]{:S(2)}) copy-start(bf16[4,27,16,128]{3,2,1,0:T(8,128)(2,1)S(1)} %collective-permute-done.46.refs_3_) | copy-start | bytes 1327108 | tf_op jit(solution)/shard_map/cond
  147.9 8.6 %collective-permute-start.47 = (bf16[8,27,16,128]{3,2,1,0:T(8,128)(2,1)S(1)}, bf16[8,27,16,128]{3,2,1,0:T(8,128)(2,1)S(1)}, u32[]{:S(2)}, u32[]{:S(2)}) collective-permute-start(bf16[8,27,16,128]{3,2,1,0:T(8,128)(2,1)S(1)} %pad_maximum_fusion.9), channel_id=1, source_target_pairs={{0,1},{1,0},{2,3},{3,2},{4,5},{5,4},{6,7},{7,6},{8,9},{9,8},{10,11... | collective-permute-start | bytes 2654216 | tf_op jit(solution)/shard_map/cond/branch_3_fun/ppermute | solution.py:515
  156.4 0.9 copy-start.34

commit v7 on v6

--- a/solution.py
+++ b/solution.py
@@ -17,19 +17,26 @@
 
 
 def spread(target, at, value):
-    count, width = value.shape
-    for part in range(width // lanes):
-        target[pl.ds(at, count), part, :] = value[:, part * lanes : (part + 1) * lanes]
+    count = value.shape[0]
+    for half in range(2):
+        target[pl.ds(2 * at + half, count, stride=2), :] = value[:, half * lanes : (half + 1) * lanes]
 
 
 def gathered(source, at, count):
-    parts = [source[pl.ds(at, count), part, :] for part in range(source.shape[1])]
-    return jnp.concatenate(parts, axis=1)
-
-
-def norm_kernel(last_ref, hidden_ref, gain_ref, owner_ref, negative_ref, normed_ref, inv_ref, emb_ref):
+    halves = [source[pl.ds(2 * at + half, count, stride=2), :] for half in range(2)]
+    return jnp.concatenate(halves, axis=1)
+
+
+def row_pair(index):
+    return pl.ds(pl.multiple_of(2 * index, 2), 2)
+
+
+def norm_kernel(
+    last_ref, hidden_ref, gain_ref, owner_ref, negative_ref, normed_ref, inv_ref, *emb_refs
+):
     seqs, width = normed_ref.shape
-    parts, _, piece = emb_ref.shape
+    parts = len(emb_refs)
+    piece = emb_refs[0].shape[1]
     pairs = owner_ref.shape[1]
     cuts = [slice(part * piece, (part + 1) * piece) for part in range(parts)]
     sources = lax.broadcasted_iota(jnp.int32, (seqs, seqs), 0)
@@ -71,9 +78,11 @@
         left = jnp.where((row == 2) & (spot == offset), named, left)
     facts = jnp.concatenate([left, right], axis=1).astype(jnp.bfloat16)
 
-    for part, cut in enumerate(cuts):
-        emb_ref[part, :seqs] = (normed_ref[:, cut].astype(jnp.float32) * inverse).astype(jnp.bfloat16)
-        emb_ref[part, seqs:] = facts
+    me = lax.axis_index("pb")
+    for apart, emb_ref in enumerate(emb_refs):
+        cut = pl.ds(pl.multiple_of((me ^ apart) * piece, piece), piece)
+        emb_ref[:seqs] = (normed_ref[:, cut].astype(jnp.float32) * inverse).astype(jnp.bfloat16)
+        emb_ref[seqs:] = facts
 
 
 def norm_call(last_row, hidden, gain, owners, hard_negatives, parts):
@@ -83,12 +92,12 @@
     return pl.pallas_call(
         norm_kernel,
         in_specs=[whole, whole, whole, whole, pl.BlockSpec(memory_space=pltpu.SMEM)],
-        out_specs=[whole, whole, whole],
+        out_specs=[whole] * (parts + 2),
         out_shape=[
             jax.ShapeDtypeStruct((seqs, width), jnp.bfloat16),
             jax.ShapeDtypeStruct((seqs, lanes), jnp.float32),
-            jax.ShapeDtypeStruct((parts, seqs + 16, piece), jnp.bfloat16),
-        ],
+        ]
+        + [jax.ShapeDtypeStruct((seqs + 16, piece), jnp.bfloat16)] * parts,
         compiler_params=pltpu.CompilerParams(vmem_limit_bytes=vmem_limit),
         name="norm_rows",
     )(last_row, hidden, gain, owners, hard_negatives)
@@ -98,26 +107,17 @@
     blocks,
     pairs,
     window,
-    emb_ref,
-    q_ref,
-    d_ref,
-    mine_ref,
-    other_ref,
-    own_ref,
-    place_ref,
-    wide,
-    picked,
-    tiles,
-    facts,
-    own,
-    named,
-    sums,
-    sems,
+    *refs,
 ):
-    seqs = emb_ref.shape[1] - 16
-    sent = emb_ref[:, seqs:, :].astype(jnp.float32)
-    own_ref[...] = (sent[:, 0, :] + 256.0 * sent[:, 1, :]).astype(jnp.int32)
-    facts[...] = sent[:, 2, :lanes].astype(jnp.int32)
+    emb_refs, (q_ref, d_ref, mine_ref, other_ref, own_ref, place_ref) = refs[:-14], refs[-14:-8]
+    wide, picked, tiles, facts, own, named, sums, sems = refs[-8:]
+    seqs = emb_refs[0].shape[0] - 16
+    me = lax.axis_index("pb")
+    for apart, emb_ref in enumerate(emb_refs):
+        sent = emb_ref[seqs:, :].astype(jnp.float32)
+        at = pl.ds(me ^ apart, 1)
+        own_ref[at, :] = (sent[0:1] + 256.0 * sent[1:2]).astype(jnp.int32)
+        facts[at, :] = sent[2:3, :lanes].astype(jnp.int32)
     fetches = [
         pltpu.make_async_copy(own_ref, own, sems.at[0]),
         pltpu.make_async_copy(facts, named, sems.at[1]),
@@ -125,12 +125,9 @@
     for fetch in fetches:
         fetch.start()
 
-    def widen(step, carry):
-        at = pl.multiple_of(step * seqs, seqs)
-        spread(wide, at, emb_ref[step, :seqs, :].astype(jnp.float32))
-        return carry
-
-    lax.fori_loop(0, emb_ref.shape[0], widen, 0)
+    for apart, emb_ref in enumerate(emb_refs):
+        at = pl.multiple_of((me ^ apart) * seqs, seqs)
+        spread(wide, at, emb_ref[:seqs, :].astype(jnp.float32))
     for fetch in fetches:
         fetch.wait()
 
@@ -156,9 +153,9 @@
     def pick_block(block, carry):
         def pick_rows(step, inner):
             base = pl.multiple_of(step * unroll, unroll)
-            rows = [wide[own[block, base + k]] for k in range(unroll)]
+            rows = [wide[row_pair(own[block, base + k]), :] for k in range(unroll)]
             for k in range(unroll):
-                picked[base + k] = rows[k]
+                picked[row_pair(base + k), :] = rows[k]
             return inner
 
         lax.fori_loop(0, 2 * pairs // unroll, pick_rows, 0)
@@ -169,7 +166,7 @@
 
     lax.fori_loop(0, blocks, pick_block, 0)
     d_ref[blocks * pairs :, :] = d_ref[: window * pairs, :]
-    core = lax.axis_index("pb") % 2
+    core = me % 2
 
     def score_blocks(step, carry):
         at = pl.multiple_of(step * 2 * pairs, 2 * pairs)
@@ -207,13 +204,13 @@
 
 
 def score_call(embedded, room, blocks, pairs, window):
-    parts, rows, piece = embedded.shape
+    rows, piece = embedded[0].shape
     fine = pairs // blocks
     whole = pl.BlockSpec(memory_space=pltpu.VMEM)
     scalars = pl.BlockSpec(memory_space=pltpu.SMEM)
     return pl.pallas_call(
         functools.partial(score_kernel, blocks, pairs, window),
-        in_specs=[whole],
+        in_specs=[whole] * blocks,
         out_specs=[whole, whole, whole, whole, whole, scalars],
         out_shape=[
             jax.ShapeDtypeStruct((blocks * pairs, piece), jnp.bfloat16),
@@ -224,8 +221,8 @@
             jax.ShapeDtypeStruct((window + 1, blocks), jnp.int32),
         ],
         scratch_shapes=[
-            pltpu.VMEM((parts * (rows - 16), piece // lanes, lanes), jnp.float32),
-            pltpu.VMEM((2 * pairs, piece // lanes, lanes), jnp.float32),
+            pltpu.VMEM((2 * blocks * (rows - 16), lanes), jnp.float32),
+            pltpu.VMEM((4 * pairs, lanes), jnp.float32),
             pltpu.VMEM((2 * pairs, (window + 2) * pairs), jnp.float32),
             pltpu.VMEM((blocks, lanes), jnp.int32),
             pltpu.SMEM((blocks, 2 * pairs), jnp.int32),
@@ -235,7 +232,7 @@
         ],
         compiler_params=pltpu.CompilerParams(vmem_limit_bytes=vmem_limit),
         name="partial_scores",
-    )(embedded)
+    )(*embedded)
 
 
 def merge_kernel(mine_ref, other_ref, own_ref, *code_refs):
@@ -369,9 +366,9 @@
     d_ref,
     *refs,
 ):
-    part_refs, (out_ref, loss_ref, wide, dsum, picked, packed, square) = refs[:-7], refs[-7:]
+    part_refs, out_refs = refs[: -blocks - 6], refs[-blocks - 6 : -6]
+    loss_ref, wide, dsum, picked, packed, square = refs[-6:]
     fine = pairs // blocks
-    seqs = wide.shape[0]
     room = packed.shape[1]
     me = lax.axis_index("pb")
     masks = swap_masks(blocks)
@@ -399,9 +396,9 @@
     def scatter_rows(block, offset, start):
         def step_rows(step, inner):
             base = pl.multiple_of(step * unroll, unroll)
-            rows = [picked[start + base + k] for k in range(unroll)]
+            rows = [picked[row_pair(start + base + k), :] for k in range(unroll)]
             for k in range(unroll):
-                wide[own_ref[block, offset + base + k]] = rows[k]
+                wide[row_pair(own_ref[block, offset + base + k]), :] = rows[k]
             return inner
 
         lax.fori_loop(0, pairs // unroll, step_rows, 0)
@@ -440,14 +437,10 @@
         return carry
 
     lax.fori_loop(0, blocks, doc_block, 0)
-    slots = out_ref.shape[1]
-
-    def narrow(part, carry):
-        at = pl.multiple_of(part * slots, slots)
-        out_ref[part] = gathered(wide, at, slots).astype(jnp.bfloat16)
-        return carry
-
-    lax.fori_loop(0, seqs // slots, narrow, 0)
+    slots = out_refs[0].shape[0]
+    for apart, out_ref in enumerate(out_refs):
+        at = pl.multiple_of((me ^ apart) * slots, slots)
+        out_ref[...] = gathered(wide, at, slots).astype(jnp.bfloat16)
 
 
 def grad_call(own, place, parts, queries, documents, blocks, pairs, window):
@@ -459,15 +452,13 @@
     return pl.pallas_call(
         functools.partial(grad_kernel, blocks, pairs, window),
         in_specs=[scalars, scalars, whole, whole] + [whole] * len(parts),
-        out_specs=[whole, whole],
-        out_shape=[
-            jax.ShapeDtypeStruct((blocks, seqs // blocks, piece), jnp.bfloat16),
-            jax.ShapeDtypeStruct((1, lanes), jnp.float32),
-        ],
+        out_specs=[whole] * (blocks + 1),
+        out_shape=[jax.ShapeDtypeStruct((seqs // blocks, piece), jnp.bfloat16)] * blocks
+        + [jax.ShapeDtypeStruct((1, lanes), jnp.float32)],
         scratch_shapes=[
-            pltpu.VMEM((seqs, piece // lanes, lanes), jnp.float32),
+            pltpu.VMEM((2 * seqs, lanes), jnp.float32),
             pltpu.VMEM(((blocks + window) * pairs, piece), jnp.float32),
-            pltpu.VMEM((2 * pairs, piece // lanes, lanes), jnp.float32),
+            pltpu.VMEM((4 * pairs, lanes), jnp.float32),
             pltpu.VMEM((blocks, room, pairs // blocks, pairs), jnp.float32),
             pltpu.VMEM((2 * pairs, (window + 2) * pairs), jnp.bfloat16),
         ],
@@ -476,38 +467,41 @@
     )(own, place, queries, documents, *parts)
 
 
-def project_kernel(grad_ref, normed_ref, inv_ref, out_ref):
-    parts, _, piece = grad_ref.shape
+def project_kernel(normed_ref, inv_ref, *refs):
+    grad_refs, out_ref = refs[:-1], refs[-1]
+    piece = grad_refs[0].shape[1]
+    me = lax.axis_index("pb")
     inverse = inv_ref[:, :1]
+    cuts = [
+        pl.ds(pl.multiple_of((me ^ apart) * piece, piece), piece) for apart in range(len(grad_refs))
+    ]
     total = 0.0
-    for part in range(parts):
-        cut = slice(part * piece, (part + 1) * piece)
+    for cut, grad_ref in zip(cuts, grad_refs):
         unit = normed_ref[:, cut].astype(jnp.float32) * inverse
-        total = total + unit * grad_ref[part].astype(jnp.float32)
+        total = total + unit * grad_ref[...].astype(jnp.float32)
     along = jnp.sum(total, axis=-1, keepdims=True)
-    for part in range(parts):
-        cut = slice(part * piece, (part + 1) * piece)
+    for cut, grad_ref in zip(cuts, grad_refs):
         unit = normed_ref[:, cut].astype(jnp.float32) * inverse
-        out_ref[:, cut] = grad_ref[part].astype(jnp.float32) - unit * along
+        out_ref[:, cut] = grad_ref[...].astype(jnp.float32) - unit * along
 
 
 def project_call(returned, normed, inverse):
-    parts, seqs, piece = returned.shape
+    seqs, piece = returned[0].shape
     width = normed.shape[1]
-    rows = 32
+    rows = 64
     return pl.pallas_call(
         project_kernel,
         grid=(seqs // rows,),
         in_specs=[
-            pl.BlockSpec((parts, rows, piece), lambda i: (0, i, 0)),
             pl.BlockSpec((rows, width), lambda i: (i, 0)),
             pl.BlockSpec((rows, lanes), lambda i: (i, 0)),
-        ],
+        ]
+        + [pl.BlockSpec((rows, piece), lambda i: (i, 0))] * len(returned),
         out_specs=pl.BlockSpec((rows, width), lambda i: (i, 0)),
         out_shape=jax.ShapeDtypeStruct((seqs, width), jnp.float32),
         compiler_params=pltpu.CompilerParams(vmem_limit_bytes=vmem_limit),
         name="project_out",
-    )(returned, normed, inverse)
+    )(normed, inverse, *returned)
 
 
 def swapped(value, apart):
@@ -537,6 +531,13 @@
     return parts
 
 
+def exchange(blocks):
+    arrived = {0: blocks[0]}
+    for apart in reversed(range(1, len(blocks))):
+        arrived[apart] = swapped(blocks[apart], apart)
+    return [arrived[apart] for apart in range(len(blocks))]
+
+
 def middle(embedded, room, devices, pairs, window):
     queries, documents, mine, other, own, place = score_call(
         embedded, room, devices, pairs, window
@@ -544,7 +545,7 @@
     own_scores, *codes = merge_call(mine, swapped(other, 1), devices)
     codes = [swapped(code, 2 * (hop + 1)) for hop, code in enumerate(codes)]
     parts = gather_all(softmax_call(place, own_scores, codes, devices, window))
-    grads, loss = grad_call(own, place, parts, queries, documents, devices, pairs, window)
+    *grads, loss = grad_call(own, place, parts, queries, documents, devices, pairs, window)
     return grads, loss[0, :1]
 
 
@@ -553,13 +554,14 @@
     seqs, width = hidden.shape
     pairs = pair_owner.shape[0]
     window = hard_negatives.shape[1]
-    normed, inverse, embedding = norm_call(
+    normed, inverse, *embedding = norm_call(
         last_row, hidden, final_gain, pair_owner.T, hard_negatives, devices
     )
-    embedded = lax.all_to_all(embedding, "pb", split_axis=0, concat_axis=0, tiled=True)
+    embedded = exchange(embedding)
     most = devices * (window + 1)
     rooms = [most * part // 20 for part in (10, 11, 12, 13, 14, 16, 20)]
-    used = devices + jnp.sum(embedded[:, seqs + 2, :window].astype(jnp.float32))
+    flags = sum(block[seqs + 2, :window].astype(jnp.float32) for block in embedded)
+    used = devices + jnp.sum(flags)
     level = sum((used > room).astype(jnp.int32) for room in rooms[:-1])
     grads, loss = lax.switch(
         level,
@@ -569,8 +571,7 @@
         ],
         embedded,
     )
-    returned = lax.all_to_all(grads, "pb", split_axis=0, concat_axis=0, tiled=True)
-    return project_call(returned, normed, inverse), loss
+    return project_call(exchange(grads), normed, inverse), loss
 
 
 def from_behind(value, axis, steps):

time: 241 us -> 240 us (level)
  blocking collectives: 110 us -> 0 us
  starting transfers between devices: 23.7 us -> 102 us
  waiting for transfers between devices: 29.1 us -> 68.9 us
  Pallas kernels: 68 us -> 58.9 us
    all_to_all x2 -> x0, blocking collectives: 110 us -> none  [the longest x1 59.2 us: feature_plan(): lax.all_to_all(embedding, 'pb', split_axis=0, concat_axis=0, tiled=True)]
    ppermute x12 -> x42, starting transfers between devices: 23.7 us -> 102 us  [swapped(): return lax.ppermute(value, 'pb', pairs)]
    ppermute x12 -> x42, waiting for transfers between devices: 29.1 us -> 68.9 us  [swapped(): return lax.ppermute(value, 'pb', pairs)]
    pallas_call x1, Pallas kernels: 23.4 us -> 20 us  [grad_call(): pl.pallas_call(functools.partial(grad_kernel, blocks, pairs, window), in_...]
    pallas_call x1, Pallas kernels: 23.4 us -> 20.1 us  [score_call(): pl.pallas_call(functools.partial(score_kernel, blocks, pairs, window), in...]
  transfers between devices with their start and end apart: 12 -> 42, of which waited for: 7 -> 20; matrix products, arithmetic and copies ran while one was open for 0% -> 0% of each run, Pallas kernels for 0% -> 0%
where the time goes in v7:
time: 240 us; the launch traced here: 239 us
  starting transfers between devices  102 us (42%)
  waiting for transfers between devices  68.9 us (29%)
  Pallas kernels  58.9 us (25%)
  other arithmetic  3.65 us (2%)
  local copies, waits for them, and re-layouts  3.32 us (1%)
    ppermute x42, starting transfers between devices, swapped(): return lax.ppermute(value, 'pb', pairs)  102 us
    ppermute x42, waiting for transfers between devices, swapped(): return lax.ppermute(value, 'pb', pairs)  68.9 us
    pallas_call x1, Pallas kernels, score_call(): pl.pallas_call(functools.partial(score_kernel, blocks, pairs, window), in...  20.1 us
    pallas_call x1, Pallas kernels, grad_call(): pl.pallas_call(functools.partial(grad_kernel, blocks, pairs, window), in_...  20 us
    pallas_call x1, Pallas kernels, project_call(): pl.pallas_call(project_kernel, grid=(seqs // rows,), in_specs=[pl.BlockSp...  5.51 us
    pallas_call x1, Pallas kernels, norm_call(): pl.pallas_call(norm_kernel, in_specs=[whole, whole, whole, whole, pl.Bloc...  5.49 us
  transfers between devices with their start and end apart: 42, of which 20 were waited for; matrix products, arithmetic and copies ran while one was open for 0% of the time, Pallas kernels for 0%

profile of v7, /device:TPU:1, one launch (start us, length us, event | category | flops | bytes accessed | tf_op | source)
XLA Modules:
  0.0 239.0 jit_solution(17942887403889597692)
XLA Ops:
  0.6 5.5 %norm_rows.1 = (bf16[256,4096]{1,0:T(8,128)(2,1)}, f32[256,128]{1,0:T(8,128)}, bf16[272,256]{1,0:T(8,128)(2,1)S(1)}, bf16[272,256]{1,0:T(8,128)(2,1)}, bf16[272,...) custom-call(s32[1,256]{1,0:T(1,128)} %last_ref.1, ...), custom_call_target="tpu_custom_call" | custom-call | tf_op jit(solution)/shard_map/norm_rows/pallas_call | solution.py:92
  6.2 2.7 %collective-permute-start.85 = (bf16[272,256]{1,0:T(8,128)(2,1)}, bf16[272,256]{1,0:T(8,128)(2,1)S(1)}, u32[]{:S(2)}, u32[]{:S(2)}) collective-permute-start(bf16[272,256]{1,0:T(8,128)(2,1)} %get-tuple-element.476), channel_id=1, source_target_pairs={{0,2},{1,3},{2,0},{3,1},{4,6},{5,7},{6,4},{7,5},{8,10},{9,11},{10,... | collective-permute-start | bytes 417800 | tf_op jit(solution)/shard_map/ppermute | solution.py:509
  13.4 3.1 %collective-permute-start.90 = (bf16[272,256]{1,0:T(8,128)(2,1)}, bf16[272,256]{1,0:T(8,128)(2,1)S(1)}, u32[]{:S(2)}, u32[]{:S(2)}) collective-permute-start(bf16[272,256]{1,0:T(8,128)(2,1)} %get-tuple-element.481), channel_id=1, source_target_pairs={{0,7},{1,6},{2,5},{3,4},{4,3},{5,2},{6,1},{7,0},{8,15},{9,14},{10,... | collective-permute-start | bytes 417800 | tf_op jit(solution)/shard_map/ppermute | solution.py:509
  19.0 3.3 %collective-permute-start.93 = (bf16[272,256]{1,0:T(8,128)(2,1)}, bf16[272,256]{1,0:T(8,128)(2,1)S(1)}, u32[]{:S(2)}, u32[]{:S(2)}) collective-permute-start(bf16[272,256]{1,0:T(8,128)(2,1)} %get-tuple-element.484), channel_id=1, source_target_pairs={{0,10},{1,11},{2,8},{3,9},{4,14},{5,15},{6,12},{7,13},{8,2},{9,3},... | collective-permute-start | bytes 417800 | tf_op jit(solution)/shard_map/ppermute | solution.py:509
  22.3 4.8 %collective-permute-done.89 = bf16[272,256]{1,0:T(8,128)(2,1)S(1)} collective-permute-done((bf16[272,256]{1,0:T(8,128)(2,1)}, bf16[272,256]{1,0:T(8,128)(2,1)S(1)}, u32[]{:S(2)}, u32[]{:S(2)}) %collective-permute-start.89) | collective-permute-done | bytes 139296 | tf_op jit(solution)/shard_map/ppermute | solution.py:509
  34.3 9.9 %collective-permute-done.92 = bf16[272,256]{1,0:T(8,128)(2,1)S(1)} collective-permute-done((bf16[272,256]{1,0:T(8,128)(2,1)}, bf16[272,256]{1,0:T(8,128)(2,1)S(1)}, u32[]{:S(2)}, u32[]{:S(2)}) %collective-permute-start.92) | collective-permute-done | bytes 139296 | tf_op jit(solution)/shard_map/ppermute | solution.py:509
  44.2 4.6 %collective-permute-start.97 = (bf16[272,256]{1,0:T(8,128)(2,1)}, bf16[272,256]{1,0:T(8,128)(2,1)S(1)}, u32[]{:S(2)}, u32[]{:S(2)}) collective-permute-start(bf16[272,256]{1,0:T(8,128)(2,1)} %get-tuple-element.488), channel_id=1, source_target_pairs={{0,14},{1,15},{2,12},{3,13},{4,10},{5,11},{6,8},{7,9},{8,6},{9,7},... | collective-permute-start | bytes 417800 | tf_op jit(solution)/shard_map/ppermute | solution.py:509
  48.9 3.2 %collective-permute-start.98 = (bf16[272,256]{1,0:T(8,128)(2,1)}, bf16[272,256]{1,0:T(8,128)(2,1)S(1)}, u32[]{:S(2)}, u32[]{:S(2)}) collective-permute-start(bf16[272,256]{1,0:T(8,128)(2,1)} %get-tuple-element.489), channel_id=1, source_target_pairs={{0,15},{1,14},{2,13},{3,12},{4,11},{5,10},{6,9},{7,8},{8,7},{9,6},... | collective-permute-start | bytes 417800 | tf_op jit(solution)/shard_map/ppermute | solution.py:509
  54.5 2.7 %collective-permute-done.98 = bf16[272,256]{1,0:T(8,128)(2,1)S(1)} collective-permute-done((bf16[272,256]{1,0:T(8,128)(2,1)}, bf16[272,256]{1,0:T(8,128)(2,1)S(1)}, u32[]{:S(2)}, u32[]{:S(2)}) %collective-permute-start.98) | collective-permute-done | bytes 139296 | tf_op jit(solution)/shard_map/ppermute | solution.py:509
  58.5 115.5 %conditional.1 = ((bf16[256,256]{1,0:T(8,128)(2,1)S(1)}, bf16[256,256]{1,0:T(8,128)(2,1)S(1)}, bf16[256,256]{1,0:T(8,128)(2,1)S(1)}, bf16[256,256]{1,0:T(8,128)(...) conditional(s32[]{:T(128)} %clamp.3, ...), branch_computations={%region_1.0_spmd, %region_2.0_spmd, %region_3.0_spmd, %region_4.0_... | conditional | flops 2854912 | bytes 55903060 | solution.py:566
  58.7 20.1 %partial_scores.9 = (bf16[2048,256]{1,0:T(8,128)(2,1)}, bf16[2560,256]{1,0:T(8,128)(2,1)}, f32[8,384,128]{2,1,0:T(8,128)}, f32[8,384,128]{2,1,0:T(8,128)}, s32[16,256]{1,0:T(8,128)}, /*index=5*/s32[5,16]{1,0:T(8,128)}) custom-call(bf16[272,256]{1,0:T(8,128)(2,1)S(1)} %get-tuple-element.285.refs_0_, bf16[272,256]{1,0:T(8,128)(2,1)S(1)} %get-tuple-element.286.refs_1_, ...), custom_call_target="tpu_custom_call" | custom-call | tf_op jit(solution)/shard_map/cond/branch_2_fun/partial_scores/pallas_call | solution.py:211
  79.0 3.5 %collective-permute-done.24.other_ref = f32[8,384,128]{2,1,0:T(8,128)S(1)} collective-permute-done((f32[8,384,128]{2,1,0:T(8,128)}, f32[8,384,128]{2,1,0:T(8,128)S(1)}, u32[]{:S(2)}, u32[]{:S(2)}) %collective-permute-start.24) | collective-permute-done | bytes 1572896 | tf_op jit(solution)/shard_map/cond/branch_2_fun/ppermute | solution.py:509
  83.6 4.6 %merge_scores.9 = (f32[384,128]{1,0:T(8,128)}, s16[25,16,128]{2,1,0:T(8,128)(2,1)}, s16[25,16,128]{2,1,0:T(8,128)(2,1)}, s16[25,16,128]{2,1,0:T(8,128)(2,1)}, s1...) custom-call(f32[8,384,128]{2,1,0:T(8,128)} %get-tuple-element.305.mi, ...), custom_call_target="tpu_custom_call" | custom-call | tf_op jit(solution)/shard_map/cond/branch_2_fun/merge_scores/pallas_call | solution.py:273
  88.5 12.6 %collective-permute-start.26 = (s16[25,16,128]{2,1,0:T(8,128)(2,1)}, s16[25,16,128]{2,1,0:T(8,128)(2,1)S(1)}, u32[]{:S(2)}, u32[]{:S(2)}) collective-permute-start(s16[25,16,128]{2,1,0:T(8,128)(2,1)} %get-tuple-element.309), channel_id=1, source_target_pairs={{0,4},{1,5},{2,6},{3,7},{4,0},{5,1},{6,2},{7,3},{8,12},{9,13},{10,... | collective-permute-start | bytes 307208 | tf_op jit(solution)/shard_map/cond/branch_2_fun/ppermute | solution.py:509
  101.3 3.6 %collective-permute-start.28 = (s16[25,16,128]{2,1,0:T(8,128)(2,1)}, s16[25,16,128]{2,1,0:T(8,128)(2,1)S(1)}, u32[]{:S(2)}, u32[]{:S(2)}) collective-permute-start(s16[25,16,128]{2,1,0:T(8,128)(2,1)} %get-tuple-element.311), channel_id=1, source_target_pairs={{0,8},{1,9},{2,10},{3,11},{4,12},{5,13},{6,14},{7,15},{8,0},{9,1},... | collective-permute-start | bytes 307208 | tf_op jit(solution)/shard_map/cond/branch_2_fun/ppermute | solution.py:509
  109.1 10.3 %collective-permute-done.29.refs_4_ = s16[25,16,128]{2,1,0:T(8,128)(2,1)S(1)} collective-permute-done((s16[25,16,128]{2,1,0:T(8,128)(2,1)}, s16[25,16,128]{2,1,0:T(8,128)(2,1)S(1)}, u32[]{:S(2)}, u32[]{:S(2)}) %collective-permute-start.29) | collective-permute-done | bytes 102432 | tf_op jit(solution)/shard_map/cond/branch_2_fun/ppermute | solution.py:509
  120.1 3.2 %softmax_rows.9 = bf16[25,16,128]{2,1,0:T(8,128)(2,1)} custom-call(s32[5,16]{1,0:T(8,128)} %get-tuple-element.302.place_ref, f32[384,128]{1,0:T(8,128)} %get-tuple-element.307.own_ref, s16[25,16,128]{2,1,0:T(8,128)(2,1)} %copy-done.82, s16[25,16,128]{2,1,0:T(8,128)(2,1)} %copy-done.83, s16[25,16,128]{2,1,0:T(8,128)(2,1)} %copy-done.84, ...), custom_call_target="tpu_custom_call" | custom-call | tf_op jit(solution)/shard_map/cond/branch_2_fun/softmax_rows/pallas_call | solution.py:345
  123.3 4.1 %collective-permute-start.32 = (bf16[1,25,16,128]{3,2,1,0:T(8,128)(2,1)}, bf16[1,25,16,128]{3,2,1,0:T(8,128)(2,1)S(1)}, u32[]{:S(2)}, u32[]{:S(2)}) collective-permute-start(bf16[1,25,16,128]{3,2,1,0:T(8,128)(2,1)} %bitcast.43), channel_id=1, source_target_pairs={{0,8},{1,9},{2,10},{3,11},{4,12},{5,13},{6,14},{7,15},{8,0},{9,1},... | collective-permute-start | bytes 307208 | tf_op jit(solution)/shard_map/cond/branch_2_fun/ppermute | solution.py:509
  130.6 3.1 %collective-permute-start.33 = (bf16[2,25,16,128]{3,2,1,0:T(8,128)(2,1)S(1)}, bf16[2,25,16,128]{3,2,1,0:T(8,128)(2,1)S(1)}, u32[]{:S(2)}, u32[]{:S(2)}) collective-permute-start(bf16[2,25,16,128]{3,2,1,0:T(8,128)(2,1)S(1)} %pad_maximum_fusion.8), channel_id=1, source_target_pairs={{0,4},{1,5},{2,6},{3,7},{4,0},{5,1},{6,2},{7,3},{8,12},{9,13},{10,... | collective-permute-start | bytes 614408 | tf_op jit(solution)/shard_map/cond/branch_2_fun/ppermute | solution.py:509
  133.7 3.1 %collective-permute-done.33.refs_2_ = bf16[2,25,16,128]{3,2,1,0:T(8,128)(2,1)S(1)} collective-permute-done((bf16[2,25,16,128]{3,2,1,0:T(8,128)(2,1)S(1)}, bf16[2,25,16,128]{3,2,1,0:T(8,128)(2,1)S(1)}, u32[]{:S(2)}, u32[]{:S(2)}) %collective-permute-start.33) | collective-permute-done | bytes 204832 | tf_op jit(solution)/shard_map/cond/branch_2_fun/ppermute | solution.py:509
  138.8 5.9 %collective-permute-done.34.refs_3_ = bf16[4,25,16,128]{3,2,1,0:T(8,128)(2,1)S(1)} collective-permute-done((bf16[4,25,16,128]{3,2,1,0:T(8,128)(2,1)S(1)}, bf16[4,25,16,128]{3,2,1,0:T(8,128)(2,1)S(1)}, u32[]{:S(2)}, u32[]{:S(2)}) %collective-permute-start.34) | collective-permute-done | bytes 409632 | tf_op jit(solution)/shard_map/cond/branch_2_fun/ppermute | solution.py:509
  145.8 5.3 %collective-permute-start.35 = (bf16[8,25,16,128]{3,2,1,0:T(8,128)(2,1)S(1)}, bf16[8,25,16,128]{3,2,1,0:T(8,128)(2,1)S(1)}, u32[]{:S(2)}, u32[]{:S(2)}) collective-permute-start(bf16[8,25,16,128]{3,2,1,0:T(8,128)(2,1)S(1)} %pad_maximum_fusion.6), channel_id=1, source_target_pairs={{0,1},{1,0},{2,3},{3,2},{4,5},{5,4},{6,7},{7,6},{8,9},{9,8},{10,11... | collective-permute-start | bytes 2457608 | tf_op jit(solution)/shard_map/cond/branch_2_fun/ppermute | solution.py:509
  154.0 20.0 %slice_grads.9 = (bf16[256,256]{1,0:T(8,128)(2,1)S(1)}, bf16[256,256]{1,0:T(8,128)(2,1)S(1)}, bf16[256,256]{1,0:T(8,128)(2,1)S(1)}, bf16[256,256]{1,0:T(8,128)(2...) custom-call(s32[16,256]{1,0:T(8,128)} %get-tuple-element.301.own_ref, ...), custom_call_target="tpu_custom_call" | custom-call | tf_op jit(solution)/shard_map/cond/branch_2_fun/slice_grads/pallas_call | solution.py:452
  174.0 3.8 %collective-permute-start.113 = (bf16[256,256]{1,0:T(8,128)(2,1)S(1)}, bf16[256,256]{1,0:T(8,128)(2,1)S(1)}, u32[]{:S(2)}, u32[]{:S(2)}) collective-permute-start(bf16[256,256]{1,0:T(8,128)(2,1)S(1)} %get-tuple-element.629), channel_id=1, source_target_pairs={{0,15},{1,14},{2,13},{3,12},{4,11},{5,10},{6,9},{7,8},{8,7},{9,6},... | collective-permute-start | bytes 393224 | tf_op jit(solution)/shard_map/ppermute | solution.py:509
  178.5 2.9 %collective-permute-start.111 = (bf16[256,256]{1,0:T(8,128)(2,1)S(1)}, bf16[256,256]{1,0:T(8,128)(2,1)S(1)}, u32[]{:S(2)}, u32[]{:S(2)}) collective-permute-start(bf16[256,256]{1,0:T(8,128)(2,1)S(1)} %get-tuple-element.631), channel_id=1, source_target_pairs={{0,13},{1,12},{2,15},{3,14},{4,9},{5,8},{6,11},{7,10},{8,5},{9,4},... | collective-permute-start | bytes 393224 | tf_op jit(solution)/shard_map/ppermute | solution.py:509
  182.4 14.4 %collective-permute-start.108 = (bf16[256,256]{1,0:T(8,128)(2,1)S(1)}, bf16[256,256]{1,0:T(8,128)(2,1)S(1)}, u32[]{:S(2)}, u32[]{:S(2)}) collective-permute-start(bf16[256,256]{1,0:T(8,128)(2,1)S(1)} %get-tuple-element.634), channel_id=1, source_target_pairs={{0,10},{1,11},{2,8},{3,9},{4,14},{5,15},{6,12},{7,13},{8,2},{9,3},... | collective-permute-start | bytes 393224 | tf_op jit(solution)/shard_map/ppermute | solution.py:509
  196.7 2.9 %collective-permute-start.107 = (bf16[256,256]{1,0:T(8,128)(2,1)S(1)}, bf16[256,256]{1,0:T(8,128)(2,1)S(1)}, u32[]{:S(2)}, u32[]{:S(2)}) collective-permute-start(bf16[256,256]{1,0:T(8,128)(2,1)S(1)} %get-tuple-element.635), channel_id=1, source_target_pairs={{0,9},{1,8},{2,11},{3,10},{4,13},{5,12},{6,15},{7,14},{8,1},{9,0},... | collective-permute-start | bytes 393224 | tf_op jit(solution)/shard_map/ppermute | solution.py:509
  199.6 7.5 %collective-permute-start.106 = (bf16[256,256]{1,0:T(8,128)(2,1)S(1)}, bf16[256,256]{1,0:T(8,128)(2,1)S(1)}, u32[]{:S(2)}, u32[]{:S(2)}) collective-permute-start(bf16[256,256]{1,0:T(8,128)(2,1)S(1)} %get-tuple-element.636), channel_id=1, source_target_pairs={{0,8},{1,9},{2,10},{3,11},{4,12},{5,13},{6,14},{7,15},{8,0},{9,1},... | collective-permute-start | bytes 393224 | tf_op jit(solution)/shard_map/ppermute | solution.py:509
  207.1 3.6 %collective-permute-start.105 = (bf16[256,256]{1,0:T(8,128)(2,1)S(1)}, bf16[256,256]{1,0:T(8,128)(2,1)S(1)}, u32[]{:S(2)}, u32[]{:S(2)}) collective-permute-start(bf16[256,256]{1,0:T(8,128)(2,1)S(1)} %get-tuple-element.637), channel_id=1, source_target_pairs={{0,7},{1,6},{2,5},{3,4},{4,3},{5,2},{6,1},{7,0},{8,15},{9,14},{10,... | collective-permute-start | bytes 393224 | tf_op jit(solution)/shard_map/ppermute | solution.py:509
  210.7 4.9 %collective-permute-done.109.refs_11_ = bf16[256,256]{1,0:T(8,128)(2,1)S(1)} collective-permute-done((bf16[256,256]{1,0:T(8,128)(2,1)S(1)}, bf16[256,256]{1,0:T(8,128)(2,1)S(1)}, u32[]{:S(2)}, u32[]{:S(2)}) %collective-permute-start.109) | collective-permute-done | bytes 131104 | tf_op jit(solution)/shard_map/ppermute | solution.py:509
  218.0 2.9 %collective-permute-done.107.refs_9_ = bf16[256,256]{1,0:T(8,128)(2,1)S(1)} collective-permute-done((bf16[256,256]{1,0:T(8,128)(2,1)S(1)}, bf16[256,256]{1,0:T(8,128)(2,1)S(1)}, u32[]{:S(2)}, u32[]{:S(2)}) %collective-permute-start.107) | collective-permute-done | bytes 131104 | tf_op jit(solution)/shard_map/ppermute | solution.py:509
  233.3 5.5 %project_out.1 = f32[256,4096]{1,0:T(8,128)} custom-call(bf16[256,4096]{1,0:T(8,128)(2,1)} %get-tuple-element.472.normed_ref, f32[256,128]{1,0:T(8,128)} %get-tuple-element.473.inv_ref, bf16[256,256]{1,0:T(8,128)(2,1)S(1)} %get-tuple-element.644.refs_0_, bf16[256,256]{1,0:T(8,128)(2,1)} %copy-done.67, bf16[256,256]{1,0:T(8,128)(2,1)} %copy-done.66, ...), custom_call_target="tpu_custom_call" | custom-call | tf_op jit(solution)/shard_map/project_out/pallas_call | solution.py:492
  (117 shorter events, 49.5 us)
Async XLA Ops:
  8.9 9.9 %collective-permute-start.87 = (bf16[272,256]{1,0:T(8,128)(2,1)}, bf16[272,256]{1,0:T(8,128)(2,1)S(1)}, u32[]{:S(2)}, u32[]{:S(2)}) collective-permute-start(bf16[272,256]{1,0:T(8,128)(2,1)} %get-tuple-element.478), channel_id=1, source_target_pairs={{0,4},{1,5},{2,6},{3,7},{4,0},{5,1},{6,2},{7,3},{8,12},{9,13},{10,... | collective-permute-start | bytes 417800 | tf_op jit(solution)/shard_map/ppermute | solution.py:509
  10.6 8.3 %collective-permute-start.88 = (bf16[272,256]{1,0:T(8,128)(2,1)}, bf16[272,256]{1,0:T(8,128)(2,1)S(1)}, u32[]{:S(2)}, u32[]{:S(2)}) collective-permute-start(bf16[272,256]{1,0:T(8,128)(2,1)} %get-tuple-element.479), channel_id=1, source_target_pairs={{0,5},{1,4},{2,7},{3,6},{4,1},{5,0},{6,3},{7,2},{8,13},{9,12},{10,... | collective-permute-start | bytes 417800 | tf_op jit(solution)/shard_map/ppermute | solution.py:509
  10.9 16.2 %collective-permute-start.89 = (bf16[272,256]{1,0:T(8,128)(2,1)}, bf16[272,256]{1,0:T(8,128)(2,1)S(1)}, u32[]{:S(2)}, u32[]{:S(2)}) collective-permute-start(bf16[272,256]{1,0:T(8,128)(2,1)} %get-tuple-element.480), channel_id=1, source_target_pairs={{0,6},{1,7},{2,4},{3,5},{4,2},{5,3},{6,0},{7,1},{8,14},{9,15},{10,... | collective-permute-start | bytes 417800 | tf_op jit(solution)/shard_map/ppermute | solution.py:509
  13.4 17.4 %collective-permute-start.90 = (bf16[272,256]{1,0:T(8,128)(2,1)}, bf16[272,256]{1,0:T(8,128)(2,1)S(1)}, u32[]{:S(2)}, u32[]{:S(2)}) collective-permute-start(bf16[272,256]{1,0:T(8,128)(2,1)} %get-tuple-element.481), channel_id=1, source_target_pairs={{0,7},{1,6},{2,5},{3,4},{4,3},{5,2},{6,1},{7,0},{8,15},{9,14},{10,... | collective-permute-start | bytes 417800 | tf_op jit(solution)/shard_map/ppermute | solution.py:509
  16.5 15.6 %collective-permute-start.91 = (bf16[272,256]{1,0:T(8,128)(2,1)}, bf16[272,256]{1,0:T(8,128)(2,1)S(1)}, u32[]{:S(2)}, u32[]{:S(2)}) collective-permute-start(bf16[272,256]{1,0:T(8,128)(2,1)} %get-tuple-element.482), channel_id=1, source_target_pairs={{0,8},{1,9},{2,10},{3,11},{4,12},{5,13},{6,14},{7,15},{8,0},{9,1},... | collective-permute-start | bytes 417800 | tf_op jit(solution)/shard_map/ppermute | solution.py:509
  18.9 25.4 %collective-permute-start.92 = (bf16[272,256]{1,0:T(8,128)(2,1)}, bf16[272,256]{1,0:T(8,128)(2,1)S(1)}, u32[]{:S(2)}, u32[]{:S(2)}) collective-permute-start(bf16[272,256]{1,0:T(8,128)(2,1)} %get-tuple-element.483), channel_id=1, source_target_pairs={{0,9},{1,8},{2,11},{3,10},{4,13},{5,12},{6,15},{7,14},{8,1},{9,0},... | collective-permute-start | bytes 417800 | tf_op jit(solution)/shard_map/ppermute | solution.py:509
  19.0 29.9 %collective-permute-start.93 = (bf16[272,256]{1,0:T(8,128)(2,1)}, bf16[272,256]{1,0:T(8,128)(2,1)S(1)}, u32[]{:S(2)}, u32[]{:S(2)}) collective-permute-start(bf16[272,256]{1,0:T(8,128)(2,1)} %get-tuple-element.484), channel_id=1, source_target_pairs={{0,10},{1,11},{2,8},{3,9},{4,14},{5,15},{6,12},{7,13},{8,2},{9,3},... | collective-permute-start | bytes 417800 | tf_op jit(solution)/shard_map/ppermute | solution.py:509
  27.1 27.4 %collective-permute-start.94 = (bf16[272,256]{1,0:T(8,128)(2,1)}, bf16[272,256]{1,0:T(8,128)(2,1)S(1)}, u32[]{:S(2)}, u32[]{:S(2)}) collective-permute-start(bf16[272,256]{1,0:T(8,128)(2,1)} %get-tuple-element.485), channel_id=1, source_target_pairs={{0,11},{1,10},{2,9},{3,8},{4,15},{5,14},{6,13},{7,12},{8,3},{9,2},... | collective-permute-start | bytes 417800 | tf_op jit(solution)/shard_map/ppermute | solution.py:509
  30.8 23.7 %collective-permute-start.95 = (bf16[272,256]{1,0:T(8,128)(2,1)}, bf16[272,256]{1,0:T(8,128)(2,1)S(1)}, u32[]{:S(2)}, u32[]{:S(2)}) collective-permute-start(bf16[272,256]{1,0:T(8,128)(2,1)} %get-tuple-element.486), channel_id=1, source_target_pairs={{0,12},{1,13},{2,14},{3,15},{4,8},{5,9},{6,10},{7,11},{8,4},{9,5},... | collective-permute-start | bytes 417800 | tf_op jit(solution)/shard_map/ppermute | solution.py:509
  32.2 22.3 %collective-permute-start.96 = (bf16[272,256]{1,0:T(8,128)(2,1)}, bf16[272,256]{1,0:T(8,128)(2,1)S(1)}, u32[]{:S(2)}, u32[]{:S(2)}) collective-permute-start(bf16[272,256]{1,0:T(8,128)(2,1)} %get-tuple-element.487), channel_id=1, source_target_pairs={{0,13},{1,12},{2,15},{3,14},{4,9},{5,8},{6,11},{7,10},{8,5},{9,4},... | collective-permute-start | bytes 417800 | tf_op jit(solution)/shard_map/ppermute | solution.py:509
  44.2 10.3 %collective-permute-start.97 = (bf16[272,256]{1,0:T(8,128)(2,1)}, bf16[272,256]{1,0:T(8,128)(2,1)S(1)}, u32[]{:S(2)}, u32[]{:S(2)}) collective-permute-start(bf16[272,256]{1,0:T(8,128)(2,1)} %get-tuple-element.488), channel_id=1, source_target_pairs={{0,14},{1,15},{2,12},{3,13},{4,10},{5,11},{6,8},{7,9},{8,6},{9,7},... | collective-permute-start | bytes 417800 | tf_op jit(solution)/shard_map/ppermute | solution.py:509
  48.9 8.4 %collective-permute-start.98 = (bf16[272,256]{1,0:T(8,128)(2,1)}, bf16[272,256]{1,0:T(8,128)(2,1)S(1)}, u32[]{:S(2)}, u32[]{:S(2)}) collective-permute-start(bf16[272,256]{1,0:T(8,128)(2,1)} %get-tuple-element.489), channel_id=1, source_target_pairs={{0,15},{1,14},{2,13},{3,12},{4,11},{5,10},{6,9},{7,8},{8,7},{9,6},... | collective-permute-start | bytes 417800 | tf_op jit(solution)/shard_map/ppermute | solution.py:509
  88.2 16.7 %collective-permute-start.25 = (s16[25,16,128]{2,1,0:T(8,128)(2,1)}, s16[25,16,128]{2,1,0:T(8,128)(2,1)S(1)}, u32[]{:S(2)}, u32[]{:S(2)}) collective-permute-start(s16[25,16,128]{2,1,0:T(8,128)(2,1)} %get-tuple-element.308), channel_id=1, source_target_pairs={{0,2},{1,3},{2,0},{3,1},{4,6},{5,7},{6,4},{7,5},{8,10},{9,11},{10,... | collective-permute-start | bytes 307208 | tf_op jit(solution)/shard_map/cond/branch_2_fun/ppermute | solution.py:509
  88.5 18.5 %collective-permute-start.26 = (s16[25,16,128]{2,1,0:T(8,128)(2,1)}, s16[25,16,128]{2,1,0:T(8,128)(2,1)S(1)}, u32[]{:S(2)}, u32[]{:S(2)}) collective-permute-start(s16[25,16,128]{2,1,0:T(8,128)(2,1)} %get-tuple-element.309), channel_id=1, source_target_pairs={{0,4},{1,5},{2,6},{3,7},{4,0},{5,1},{6,2},{7,3},{8,12},{9,13},{10,... | collective-permute-start | bytes 307208 | tf_op jit(solution)/shard_map/cond/branch_2_fun/ppermute | solution.py:509
  101.1 8.0 %collective-permute-start.27 = (s16[25,16,128]{2,1,0:T(8,128)(2,1)}, s16[25,16,128]{2,1,0:T(8,128)(2,1)S(1)}, u32[]{:S(2)}, u32[]{:S(2)}) collective-permute-start(s16[25,16,128]{2,1,0:T(8,128)(2,1)} %get-tuple-element.310), channel_id=1, source_target_pairs={{0,6},{1,7},{2,4},{3,5},{4,2},{5,3},{6,0},{7,1},{8,14},{9,15},{10,... | collective-permute-start | bytes 307208 | tf_op jit(solution)/shard_map/cond/branch_2_fun/ppermute | solution.py:509
  104.9 14.5 %collective-permute-start.29 = (s16[25,16,128]{2,1,0:T(8,128)(2,1)}, s16[25,16,128]{2,1,0:T(8,128)(2,1)S(1)}, u32[]{:S(2)}, u32[]{:S(2)}) collective-permute-start(s16[25,16,128]{2,1,0:T(8,128)(2,1)} %get-tuple-element.312), channel_id=1, source_target_pairs={{0,10},{1,11},{2,8},{3,9},{4,14},{5,15},{6,12},{7,13},{8,2},{9,3},... | collective-permute-start | bytes 307208 | tf_op jit(solution)/shard_map/cond/branch_2_fun/ppermute | solution.py:509
  104.9 14.5 %collective-permute-start.30 = (s16[25,16,128]{2,1,0:T(8,128)(2,1)}, s16[25,16,128]{2,1,0:T(8,128)(2,1)S(1)}, u32[]{:S(2)}, u32[]{:S(2)}) collective-permute-start(s16[25,16,128]{2,1,0:T(8,128)(2,1)} %get-tuple-element.313), channel_id=1, source_target_pairs={{0,12},{1,13},{2,14},{3,15},{4,8},{5,9},{6,10},{7,11},{8,4},{9,5},... | collective-permute-start | bytes 307208 | tf_op jit(solution)/shard_map/cond/branch_2_fun/ppermute | solution.py:509
  107.0 12.4 %collective-permute-start.31 = (s16[25,16,128]{2,1,0:T(8,128)(2,1)}, s16[25,16,128]{2,1,0:T(8,128)(2,1)S(1)}, u32[]{:S(2)}, u32[]{:S(2)}) collective-permute-start(s16[25,16,128]{2,1,0:T(8,128)(2,1)} %get-tuple-element.314), channel_id=1, source_target_pairs={{0,14},{1,15},{2,12},{3,13},{4,10},{5,11},{6,8},{7,9},{8,6},{9,7},... | collective-permute-start | bytes 307208 | tf_op jit(solution)/shard_map/cond/branch_2_fun/ppermute | solution.py:509
  174.0 8.3 %collective-permute-start.113 = (bf16[256,256]{1,0:T(8,128)(2,1)S(1)}, bf16[256,256]{1,0:T(8,128)(2,1)S(1)}, u32[]{:S(2)}, u32[]{:S(2)}) collective-permute-start(bf16[256,256]{1,0:T(8,128)(2,1)S(1)} %get-tuple-element.629), channel_id=1, source_target_pairs={{0,15},{1,14},{2,13},{3,12},{4,11},{5,10},{6,9},{7,8},{8,7},{9,6},... | collective-permute-start | bytes 393224 | tf_op jit(solution)/shard_map/ppermute | solution.py:509
  177.8 19.0 %collective-permute-start.112 = (bf16[256,256]{1,0:T(8,128)(2,1)S(1)}, bf16[256,256]{1,0:T(8,128)(2,1)S(1)}, u32[]{:S(2)}, u32[]{:S(2)}) collective-permute-start(bf16[256,256]{1,0:T(8,128)(2,1)S(1)} %get-tuple-element.630), channel_id=1, source_target_pairs={{0,14},{1,15},{2,12},{3,13},{4,10},{5,11},{6,8},{7,9},{8,6},{9,7},... | collective-permute-start | bytes 393224 | tf_op jit(solution)/shard_map/ppermute | solution.py:509
  178.5 21.1 %collective-permute-start.111 = (bf16[256,256]{1,0:T(8,128)(2,1)S(1)}, bf16[256,256]{1,0:T(8,128)(2,1)S(1)}, u32[]{:S(2)}, u32[]{:S(2)}) collective-permute-start(bf16[256,256]{1,0:T(8,128)(2,1)S(1)} %get-tuple-element.631), channel_id=1, source_target_pairs={{0,13},{1,12},{2,15},{3,14},{4,9},{5,8},{6,11},{7,10},{8,5},{9,4},... | collective-permute-start | bytes 393224 | tf_op jit(solution)/shard_map/ppermute | solution.py:509
  181.4 25.7 %collective-permute-start.110 = (bf16[256,256]{1,0:T(8,128)(2,1)S(1)}, bf16[256,256]{1,0:T(8,128)(2,1)S(1)}, u32[]{:S(2)}, u32[]{:S(2)}) collective-permute-start(bf16[256,256]{1,0:T(8,128)(2,1)S(1)} %get-tuple-element.632), channel_id=1, source_target_pairs={{0,12},{1,13},{2,14},{3,15},{4,8},{5,9},{6,10},{7,11},{8,4},{9,5},... | collective-permute-start | bytes 393224 | tf_op jit(solution)/shard_map/ppermute | solution.py:509
  182.1 33.5 %collective-permute-start.109 = (bf16[256,256]{1,0:T(8,128)(2,1)S(1)}, bf16[256,256]{1,0:T(8,128)(2,1)S(1)}, u32[]{:S(2)}, u32[]{:S(2)}) collective-permute-start(bf16[256,256]{1,0:T(8,128)(2,1)S(1)} %get-tuple-element.633), channel_id=1, source_target_pairs={{0,11},{1,10},{2,9},{3,8},{4,15},{5,14},{6,13},{7,12},{8,3},{9,2},... | collective-permute-start | bytes 393224 | tf_op jit(solution)/shard_map/ppermute | solution.py:509
  182.4 35.6 %collective-permute-start.108 = (bf16[256,256]{1,0:T(8,128)(2,1)S(1)}, bf16[256,256]{1,0:T(8,128)(2,1)S(1)}, u32[]{:S(2)}, u32[]{:S(2)}) collective-permute-start(bf16[256,256]{1,0:T(8,128)(2,1)S(1)} %get-tuple-element.634), channel_id=1, source_target_pairs={{0,10},{1,11},{2,8},{3,9},{4,14},{5,15},{6,12},{7,13},{8,2},{9,3},... | collective-permute-start | bytes 393224 | tf_op jit(solution)/shard_map/ppermute | solution.py:509
  196.7 24.2 %collective-permute-start.107 = (bf16[256,256]{1,0:T(8,128)(2,1)S(1)}, bf16[256,256]{1,0:T(8,128)(2,1)S(1)}, u32[]{:S(2)}, u32[]{:S(2)}) collective-permute-start(bf16[256,256]{1,0:T(8,128)(2,1)S(1)} %get-tuple-element.635), channel_id=1, source_target_pairs={{0,9},{1,8},{2,11},{3,10},{4,13},{5,12},{6,15},{7,14},{8,1},{9,0},... | collective-permute-start | bytes 393224 | tf_op jit(solution)/shard_map/ppermute | solution.py:509
  199.6 23.7 %collective-permute-start.106 = (bf16[256,256]{1,0:T(8,128)(2,1)S(1)}, bf16[256,256]{1,0:T(8,128)(2,1)S(1)}, u32[]{:S(2)}, u32[]{:S(2)}) collective-permute-start(bf16[256,256]{1,0:T(8,128)(2,1)S(1)} %get-tuple-element.636), channel_id=1, source_target_pairs={{0,8},{1,9},{2,10},{3,11},{4,12},{5,13},{6,14},{7,15},{8,0},{9,1},... | collective-permute-start | bytes 393224 | tf_op jit(solution)/shard_map/ppermute | solution.py:509
  207.1 17.5 %collective-permute-start.105 = (bf16[256,256]{1,0:T(8,128)(2,1)S(1)}, bf16[256,256]{1,0:T(8,128)(2,1)S(1)}, u32[]{:S(2)}, u32[]{:S(2)}) collective-permute-start(bf16[256,256]{1,0:T(8,128)(2,1)S(1)} %get-tuple-element.637), channel_id=1, source_target_pairs={{0,7},{1,6},{2,5},{3,4},{4,3},{5,2},{6,1},{7,0},{8,15},{9,14},{10,... | collective-permute-start | bytes 393224 | tf_op jit(solution)/shard_map/ppermute | solution.py:509
  215.6 11.3 %collective-permute-start.104 = (bf16[256,256]{1,0:T(8,128)(2,1)S(1)}, bf16[256,256]{1,0:T(8,128)(2,1)S(1)}, u32[]{:S(2)}, u32[]{:S(2)}) collective-permute-start(bf16[256,256]{1,0:T(8,128)(2,1)S(1)} %get-tuple-element.638), channel_id=1, source_target_pairs={{0,6},{1,7},{2,4},{3,5},{4,2},{5,3},{6,0},{7,1},{8,14},{9,15},{10,... | collective-permute-start | bytes 393224 | tf_op jit(solution)/shard_map/ppermute | solution.py:509
  218.0 11.6 %collective-permute-start.103 = (bf16[256,256]{1,0:T(8,128)(2,1)S(1)}, bf16[256,256]{1,0:T(8,128)(2,1)S(1)}, u32[]{:S(2)}, u32[]{:S(2)}) collective-permute-start(bf16[256,256]{1,0:T(8,128)(2,1)S(1)} %get-tuple-element.639), channel_id=1, source_target_pairs={{0,5},{1,4},{2,7},{3,6},{4,1},{5,0},{6,3},{7,2},{8,13},{9,12},{10,... | collective-permute-start | bytes 393224 | tf_op jit(solution)/shard_map/ppermute | solution.py:509
  220.9 11.3 %collective-permute-start.102 = (bf16[256,256]{1,0:T(8,128)(2,1)S(1)}, bf16[256,256]{1,0:T(8,128)(2,1)S(1)}, u32[]{:S(2)}, u32[]{:S(2)}) collective-permute-start(bf16[256,256]{1,0:T(8,128)(2,1)S(1)} %get-tuple-element.640), channel_id=1, source_target_pairs={{0,4},{1,5},{2,6},{3,7},{4,0},{5,1},{6,2},{7,3},{8,12},{9,13},{10,... | collective-permute-start | bytes 393224 | tf_op jit(solution)/shard_map/ppermute | solution.py:509
  223.3 8.9 %collective-permute-start.101 = (bf16[256,256]{1,0:T(8,128)(2,1)S(1)}, bf16[256,256]{1,0:T(8,128)(2,1)S(1)}, u32[]{:S(2)}, u32[]{:S(2)}) collective-permute-start(bf16[256,256]{1,0:T(8,128)(2,1)S(1)} %get-tuple-element.641), channel_id=1, source_target_pairs={{0,3},{1,2},{2,1},{3,0},{4,7},{5,6},{6,5},{7,4},{8,11},{9,10},{10,... | collective-permute-start | bytes 393224 | tf_op jit(solution)/shard_map/ppermute | solution.py:509
  224.5 8.0 %collective-permute-start.100 = (bf16[256,256]{1,0:T(8,128)(2,1)S(1)}, bf16[256,256]{1,0:T(8,128)(2,1)S(1)}, u32[]{:S(2)}, u32[]{:S(2)}) collective-permute-start(bf16[256,256]{1,0:T(8,128)(2,1)S(1)} %get-tuple-element.642), channel_id=1, source_target_pairs={{0,2},{1,3},{2,0},{3,1},{4,6},{5,7},{6,4},{7,5},{8,10},{9,11},{10,... | collective-permute-start | bytes 393224 | tf_op jit(solution)/shard_map/ppermute | solution.py:509
  (37 other events, 373.4 us)
